TPU v7x, 256 devices: a whole 4x4x8 slice. The times are simulated.
256 devices in a mesh: dp: 32 (over y_lo, z, core), ctx: 8 (over y_hi, x).
Axes of the slice: x: 4, y: 4 (y_hi: 2, y_lo: 2; y = y_hi * 2 + y_lo), z: 8, core: 2. Of those that a mesh axis runs over, the one named last changes fastest.
Arguments:
- tokens: bfloat16 [32768, 8192], P(('dp', 'ctx')), may hold values from -24 to 24
- queries: bfloat16 [32768, 4096], P(('dp', 'ctx')), may hold values from -160 to 160
- rotated_key_rows: bfloat16 [32768, 512], P(('dp', 'ctx')), may hold values from -6 to 6
- upstream: bfloat16 [32768, 4096], P(('dp', 'ctx')), may hold values from -6 to 6
- value_projection_weight: bfloat16 [8192, 512], P('dp'), may hold values from -0.0625 to 0.0625
- doc_lengths: int32 [256, 4], P(('dp', 'ctx')), may hold values from 1 to 32, 64 in all within a row
- stretch_order: int32 [32, 8], P('dp'), may hold values from 0 to 7, each once within a row
Outputs:
- d_query: float32 [32768, 4096], P(('dp', 'ctx'))
- d_key: float32 [32768, 512], P(('dp', 'ctx'))
- weight_grad: float32 [8192, 512], P('dp')
Inputs may be any that keep to these rules, and one draw needn't show every extreme that they name: `doc_lengths`: each row is the lengths of the 4 short documents of one device, summing to 64; its largest is exactly 32. `stretch_order`: each row is a permutation of the block numbers of one pack's long document.
All inputs are finite; a program needn't handle non-finite values.
Results may differ from a plain program's by a relative error of at most 0.0055.
Values may be sent and summed in bfloat16 or wider, within the bound.
No kernel may reach another device: no remote copies, remote signals or barrier semaphores. Data moves between devices by JAX's collectives and lax.ppermute only.
A program may use at most 128 MiB of HBM per device.

v0:
```python
import jax
import jax.numpy as jnp
from jax import lax
from jax.sharding import PartitionSpec as P

QUERY_HEADS = 32
KEY_VALUE_HEADS = 4
HEAD_SIZE = 128
LB = 64
SB = 64


def score_block(query_matrix, rotated_key_rows):
    query_heads = query_matrix.reshape(
        query_matrix.shape[0], KEY_VALUE_HEADS, QUERY_HEADS // KEY_VALUE_HEADS, HEAD_SIZE
    )
    key_heads = rotated_key_rows.reshape(rotated_key_rows.shape[0], KEY_VALUE_HEADS, HEAD_SIZE)
    return jnp.einsum(
        "nkgd,mkd->kgnm", query_heads, key_heads, preferred_element_type=jnp.float32
    ) * HEAD_SIZE ** (-0.5)


def dprob_block(upstream, projected_value_rows):
    upstream_heads = upstream.reshape(
        upstream.shape[0], KEY_VALUE_HEADS, QUERY_HEADS // KEY_VALUE_HEADS, HEAD_SIZE
    )
    value_heads = projected_value_rows.reshape(
        projected_value_rows.shape[0], KEY_VALUE_HEADS, HEAD_SIZE
    )
    return jnp.einsum(
        "nkgd,mkd->kgnm", upstream_heads, value_heads, preferred_element_type=jnp.float32
    )


def initial_stats(query_count):
    array_shape = (KEY_VALUE_HEADS, QUERY_HEADS // KEY_VALUE_HEADS, query_count)
    return (
        jnp.full(array_shape, -1e30, jnp.float32),
        jnp.zeros(array_shape, jnp.float32),
        jnp.zeros(array_shape, jnp.float32),
    )


def fold_stats(carry, query_matrix, upstream, rotated_key_rows, projected_value_rows, allowed):
    running_max, running_sum, running_dot = carry
    scores = jnp.where(allowed, score_block(query_matrix, rotated_key_rows), -1e30)
    new_max = jnp.maximum(running_max, jnp.max(scores, axis=-1))
    raised = jnp.where(allowed, jnp.exp(scores - new_max[..., None]), 0.0)
    d_prob = dprob_block(upstream, projected_value_rows)
    factor = jnp.exp(running_max - new_max)
    return (
        new_max,
        running_sum * factor + jnp.sum(raised, axis=-1),
        running_dot * factor + jnp.sum(raised * d_prob, axis=-1),
    )


def grad_block(
    query_matrix,
    upstream,
    rotated_key_rows,
    projected_value_rows,
    allowed,
    running_max,
    running_sum,
    delta,
):
    scale = HEAD_SIZE ** (-0.5)
    query_count = query_matrix.shape[0]
    key_count = rotated_key_rows.shape[0]
    scores = jnp.where(allowed, score_block(query_matrix, rotated_key_rows), -1e30)
    prob = (
        jnp.where(allowed, jnp.exp(scores - running_max[..., None]), 0.0) / running_sum[..., None]
    )
    d_prob = dprob_block(upstream, projected_value_rows)
    d_score = (prob * (d_prob - delta[..., None])).astype(jnp.bfloat16)
    query_heads = query_matrix.reshape(
        query_count, KEY_VALUE_HEADS, QUERY_HEADS // KEY_VALUE_HEADS, HEAD_SIZE
    )
    upstream_heads = upstream.reshape(
        query_count, KEY_VALUE_HEADS, QUERY_HEADS // KEY_VALUE_HEADS, HEAD_SIZE
    )
    key_heads = rotated_key_rows.reshape(key_count, KEY_VALUE_HEADS, HEAD_SIZE)
    d_query = jnp.einsum(
        "kgnm,mkd->nkgd", d_score, key_heads, preferred_element_type=jnp.float32
    ).reshape(query_count, -1)
    d_key = (
        jnp.einsum(
            "kgnm,nkgd->mkd", d_score, query_heads, preferred_element_type=jnp.float32
        ).reshape(key_count, -1)
        * scale
    )
    d_value = jnp.einsum(
        "kgnm,nkgd->mkd",
        prob.astype(jnp.bfloat16),
        upstream_heads,
        preferred_element_type=jnp.float32,
    ).reshape(key_count, -1)
    return (d_query, d_key, d_value)


def full_attend(query_matrix, upstream, rotated_key_rows, projected_value_rows, allowed):
    stats = fold_stats(
        initial_stats(query_matrix.shape[0]),
        query_matrix,
        upstream,
        rotated_key_rows,
        projected_value_rows,
        allowed,
    )
    return grad_block(
        query_matrix,
        upstream,
        rotated_key_rows,
        projected_value_rows,
        allowed,
        stats[0],
        stats[1],
        stats[2] / stats[1],
    )


def on_device(
    tokens, queries, rotated_key_rows, upstream, value_projection_weight, doc_lengths, stretch_order
):
    columns = tokens
    values = jnp.dot(
        columns,
        lax.all_gather(value_projection_weight, "dp", axis=0, tiled=True),
        preferred_element_type=jnp.float32,
    ).astype(jnp.bfloat16)
    doc_ends = jnp.cumsum(doc_lengths[0])
    positions = jnp.arange(SB, dtype=jnp.int32)
    segment = jnp.sum((positions[:, None] >= doc_ends[None, :]).astype(jnp.int32), axis=1)
    allowed_short = (segment[:, None] == segment[None, :]) & (
        positions[None, :] <= positions[:, None]
    )
    dq_short, dk_short, dv_short = full_attend(
        queries[LB:], upstream[LB:], rotated_key_rows[LB:], values[LB:], allowed_short
    )
    group_size = lax.axis_size("ctx")
    member = lax.axis_index("ctx")
    order_row = stretch_order[0]
    member_ids = jnp.arange(group_size, dtype=jnp.int32)
    my_stretch = jnp.sum(jnp.where(member_ids == member, order_row, 0))
    query_pos = my_stretch * LB + jnp.arange(LB, dtype=jnp.int32)
    long_q = queries[:LB]
    long_u = upstream[:LB]
    long_k = rotated_key_rows[:LB]
    long_v = values[:LB]

    def owner_allowed(owner_id):
        stretch_id = jnp.sum(jnp.where(member_ids == owner_id, order_row, 0))
        key_pos = stretch_id * LB + jnp.arange(LB, dtype=jnp.int32)
        return key_pos[None, :] <= query_pos[:, None]

    all_keys, all_values = (
        lax.all_gather(long_k, "ctx", axis=0, tiled=True),
        lax.all_gather(long_v, "ctx", axis=0, tiled=True),
    )

    def block_rows(source, block_id):
        return lax.dynamic_slice_in_dim(source, block_id * LB, LB, 0)

    def stats_turn(block_id, carry):
        return fold_stats(
            carry,
            long_q,
            long_u,
            block_rows(all_keys, block_id),
            block_rows(all_values, block_id),
            owner_allowed(block_id),
        )

    running_max, running_sum, running_dot = lax.fori_loop(
        0, group_size, stats_turn, initial_stats(LB)
    )
    delta = running_dot / running_sum

    def grads_turn(block_id, carry):
        dq_total, dk_buffer, dv_buffer = carry
        dq_part, dk_part, dv_part = grad_block(
            long_q,
            long_u,
            block_rows(all_keys, block_id),
            block_rows(all_values, block_id),
            owner_allowed(block_id),
            running_max,
            running_sum,
            delta,
        )
        dk_buffer = lax.dynamic_update_slice_in_dim(dk_buffer, dk_part, block_id * LB, 0)
        dv_buffer = lax.dynamic_update_slice_in_dim(dv_buffer, dv_part, block_id * LB, 0)
        return (dq_total + dq_part, dk_buffer, dv_buffer)

    zero_rows = jnp.zeros((group_size * LB, long_k.shape[1]), jnp.float32)
    dq_long, dk_all, dv_all = lax.fori_loop(
        0,
        group_size,
        grads_turn,
        (jnp.zeros((LB, long_q.shape[1]), jnp.float32), zero_rows, zero_rows),
    )
    dk_long, dv_long = (
        lax.psum_scatter(dk_all, "ctx", scatter_dimension=0, tiled=True),
        lax.psum_scatter(dv_all, "ctx", scatter_dimension=0, tiled=True),
    )
    d_query = jnp.concatenate([dq_long, dq_short], axis=0) * HEAD_SIZE ** (-0.5)
    d_key = jnp.concatenate([dk_long, dk_short], axis=0)
    d_value = jnp.concatenate([dv_long, dv_short], axis=0).astype(jnp.bfloat16)
    columns = tokens
    grad_share = lax.psum_scatter(
        lax.dot_general(
            columns, d_value, (((0,), (0,)), ((), ())), preferred_element_type=jnp.float32
        ),
        "dp",
        scatter_dimension=0,
        tiled=True,
    )
    weight_grad = lax.psum(grad_share, "ctx")
    return (d_query, d_key, weight_grad)


def solution(mesh):
    placed = (
        P(("dp", "ctx"), None),
        P(("dp", "ctx"), None),
        P(("dp", "ctx"), None),
        P(("dp", "ctx"), None),
        P("dp", None),
        P(("dp", "ctx"), None),
        P("dp", None),
    )
    return jax.shard_map(
        on_device,
        mesh=mesh,
        in_specs=placed,
        out_specs=(P(("dp", "ctx"), None), P(("dp", "ctx"), None), P("dp", None)),
        check_vma=False,
    )
```

profile of v0, /device:TPU:32, one launch (start us, length us, event | category | flops | bytes accessed | tf_op | source)
XLA Modules:
  0.0 637.5 jit_solution(15301980540417657381)
XLA Ops:
  8.0 1.3 fusion.62
  10.0 0.9 fusion.69
  10.8 37.4 %all_gather.9 = bf16[512,512]{1,0:T(8,128)(2,1)} all-gather(bf16[64,512]{1,0:T(8,128)(2,1)S(1)} %get-tuple-element.584), channel_id=1, replica_groups=mesh['dp'=32,'ctx'=8] {'ctx'}, dimensions={0}, use_global_device_ids=true | all-gather | bytes 589824 | tf_op jit(solution)/shard_map/all_gather | solution.py:158
  48.3 2.7 fusion.66
  51.0 32.9 %all-gather.2.cloned.1.call-done = bf16[8192,512]{1,0:T(8,128)(2,1)} async-done(((bf16[256,512]{1,0:T(8,128)(2,1)}), bf16[8192,512]{1,0:T(8,128)(2,1)}) %all-gather.2.cloned.1.call-update) | async-done | bytes 8388624 | tf_op jit(solution)/shard_map/all_gather | solution.py:129
  83.9 4.6 convolution_convert_fusion
  88.6 37.6 %all_gather.11 = bf16[512,512]{1,0:T(8,128)(2,1)} all-gather(bf16[64,512]{1,0:T(8,128)(2,1)S(1)} %get-tuple-element.582), channel_id=1, replica_groups=mesh['dp'=32,'ctx'=8] {'ctx'}, dimensions={0}, use_global_device_ids=true | all-gather | bytes 589824 | tf_op jit(solution)/shard_map/all_gather | solution.py:159
  126.1 34.3 %while.36 = (s32[]{:T(128)}, f32[4,8,64]{2,1,0:T(8,128)S(1)}, f32[4,8,64]{2,1,0:T(8,128)S(1)}, f32[4,8,64]{2,1,0:T(8,128)S(1)}, s32[8]{0:T(128)S(1)}, /*index=5*...) while((s32[]{:T(128)}, f32[4,8,64]{2,1,0:T(8,128)S(1)}, ...), condition=%wide.region_6.7_spmd.clone, body=%wide.region_1.6_spmd.clone.sunk | while | flops 68438176 | bytes 5539078 | solution.py:175
  127.6 0.9 constant_dynamic-slice_fusion.7
  131.9 0.9 constant_dynamic-slice_fusion.7
  136.2 0.9 constant_dynamic-slice_fusion.7
  140.5 0.9 constant_dynamic-slice_fusion.7
  144.8 0.9 constant_dynamic-slice_fusion.7
  149.1 0.9 constant_dynamic-slice_fusion.7
  153.4 0.9 constant_dynamic-slice_fusion.7
  157.7 0.9 constant_dynamic-slice_fusion.7
  160.5 1.1 broadcast_in_dim.119.clone
  161.6 1.2 broadcast_in_dim.119
  162.8 67.6 %while.37 = (s32[]{:T(128)}, f32[64,4096]{1,0:T(8,128)}, f32[512,512]{1,0:T(8,128)}, f32[512,512]{1,0:T(8,128)}, bf16[512,512]{1,0:T(8,128)(2,1)}, /*index=5*/s3...) while((s32[]{:T(128)}, f32[64,4096]{1,0:T(8,128)}, ...), condition=%wide.region_9.10_spmd.clone, body=%wide.region_7.9_spmd.clone.sunk | while | flops 169513120 | bytes 22775132 | solution.py:197
  164.1 0.9 constant_dynamic-slice_fusion.9
  165.0 0.9 constant_dynamic-slice_fusion.8
  169.3 0.8 bitcast_add_fusion.2
  170.1 0.8 bitcast_dynamic-update-slice_fusion.3
  172.6 0.9 constant_dynamic-slice_fusion.9
  173.4 0.9 constant_dynamic-slice_fusion.8
  177.8 0.8 bitcast_add_fusion.2
  178.6 0.8 bitcast_dynamic-update-slice_fusion.3
  181.0 0.9 constant_dynamic-slice_fusion.9
  181.9 0.9 constant_dynamic-slice_fusion.8
  186.2 0.8 bitcast_add_fusion.2
  187.0 0.8 bitcast_dynamic-update-slice_fusion.3
  189.5 0.9 constant_dynamic-slice_fusion.9
  190.3 0.9 constant_dynamic-slice_fusion.8
  194.7 0.8 bitcast_add_fusion.2
  195.5 0.8 bitcast_dynamic-update-slice_fusion.3
  197.9 0.9 constant_dynamic-slice_fusion.9
  198.8 0.9 constant_dynamic-slice_fusion.8
  203.1 0.8 bitcast_add_fusion.2
  203.9 0.8 bitcast_dynamic-update-slice_fusion.3
  206.4 0.9 constant_dynamic-slice_fusion.9
  207.2 0.9 constant_dynamic-slice_fusion.8
  211.6 0.8 bitcast_add_fusion.2
  212.4 0.8 bitcast_dynamic-update-slice_fusion.3
  214.8 0.9 constant_dynamic-slice_fusion.9
  215.7 0.9 constant_dynamic-slice_fusion.8
  220.0 0.8 bitcast_add_fusion.2
  220.8 0.8 bitcast_dynamic-update-slice_fusion.3
  223.3 0.9 constant_dynamic-slice_fusion.9
  224.2 0.9 constant_dynamic-slice_fusion.8
  228.5 0.8 bitcast_add_fusion.2
  229.3 0.8 bitcast_dynamic-update-slice_fusion.3
  230.7 2.0 copy.114
  234.3 2.8 fusion.47
  237.6 69.8 %reduce-scatter.6.cloned.1.call-done = f32[64,512]{1,0:T(8,128)} async-done(((f32[512,512]{1,0:T(8,128)}), f32[64,512]{1,0:T(8,128)}) %reduce-scatter.6.cloned.1.call-update) | async-done | bytes 131088 | tf_op jit(solution)/shard_map/reduce_scatter | solution.py:205
  307.4 0.9 convert.8
  308.3 8.1 %convolution_bitcast_fusion.5 = f32[8192,512]{0,1:T(8,128)} fusion(bf16[128,8192]{1,0:T(8,128)(2,1)S(1)} %copy-done, bf16[64,512]{1,0:T(8,128)(2,1)S(1)} %bitcast.209, bf16[64,512]{1,0:T(8,128)(2,1)S(1)} %convert.8), kind=kOutput, calls=%fused_computation.63 | convolution fusion | flops 1074003968 | bytes 19005440 | tf_op jit(solution)/shard_map/dot_general | solution.py:212
  317.3 1.6 multiply_convert_fusion
  320.3 1.6 copy.170
  321.9 133.3 %reduce-scatter.8.cloned.1.call-done = f32[256,512]{0,1:T(8,128)} async-done(((f32[8192,512]{0,1:T(8,128)}), f32[256,512]{0,1:T(8,128)}) %reduce-scatter.8.cloned.1.call-update) | async-done | bytes 524304 | tf_op jit(solution)/shard_map/reduce_scatter | solution.py:211
  455.2 2.8 maximum_multiply_fusion
  457.9 79.0 %reduce-scatter.4.cloned.1.call-done = f32[64,512]{1,0:T(8,128)} async-done(((f32[512,512]{1,0:T(8,128)}), f32[64,512]{1,0:T(8,128)}) %reduce-scatter.4.cloned.1.call-update) | async-done | bytes 131088 | tf_op jit(solution)/shard_map/reduce_scatter | solution.py:204
  536.9 1.6 pad_maximum_fusion
  538.6 90.4 %all-reduce.2.cloned.1.call-done = f32[256,512]{0,1:T(8,128)} async-done(((f32[256,512]{0,1:T(8,128)}), f32[256,512]{0,1:T(8,128)}) %all-reduce.2.cloned.1.call-update) | async-done | bytes 524304 | tf_op jit(solution)/shard_map/psum | solution.py:219
  629.0 2.0 copy.73
  (295 shorter events, 61.8 us)
Async XLA Ops:
  7.2 76.8 %copy-start = (bf16[128,8192]{1,0:T(8,128)(2,1)S(1)}, bf16[128,8192]{1,0:T(8,128)(2,1)}, u32[]{:S(2)}) copy-start(bf16[128,8192]{1,0:T(8,128)(2,1)} %param.11) | copy-start | bytes 6291460
  7.2 76.7 %all-gather.2.cloned.1.call-start = ((), (), s32[]{:S(2)}) async-start(), calls=%async_computation.3 | async-start | bytes 8650752 | tf_op jit(solution)/shard_map/all_gather | solution.py:129
  7.9 299.5 %reduce-scatter.6.cloned.1.call-start = ((), (), s32[]{:S(2)}) async-start(), calls=%async_computation.5 | async-start | bytes 1179648 | tf_op jit(solution)/shard_map/reduce_scatter | solution.py:205
  51.0 75.2 %copy-start.8 = (s32[1,8]{1,0:T(1,128)S(1)}, s32[1,8]{1,0:T(1,128)}, u32[]{:S(2)}) copy-start(s32[1,8]{1,0:T(1,128)} %param.17) | copy-start | bytes 100
  162.8 67.7 %copy-start.9 = (s32[1,4]{1,0:T(1,128)S(1)}, s32[1,4]{1,0:T(1,128)}, u32[]{:S(2)}) copy-start(s32[1,4]{1,0:T(1,128)} %param.16) | copy-start | bytes 52
  168.1 1.2 copy-start.1
  170.1 1.1 copy-start.2
  176.5 1.2 copy-start.1
  178.6 1.1 copy-start.2
  185.0 1.2 copy-start.1
  187.0 1.1 copy-start.2
  193.4 1.2 copy-start.1
  195.5 1.1 copy-start.2
  201.9 1.2 copy-start.1
  203.9 1.1 copy-start.2
  210.3 1.2 copy-start.1
  212.4 1.1 copy-start.2
  218.8 1.2 copy-start.1
  220.8 1.1 copy-start.2
  227.3 1.2 copy-start.1
  229.3 1.1 copy-start.2
  230.4 2.3 copy-start.7
  230.4 224.7 %reduce-scatter.8.cloned.1.call-start = ((), (), s32[]{:S(2)}) async-start(), calls=%async_computation.6 | async-start | bytes 17301504 | tf_op jit(solution)/shard_map/reduce_scatter | solution.py:211
  232.8 0.8 copy-start.4
  234.2 2.8 copy-start.6
  316.5 220.5 %reduce-scatter.4.cloned.1.call-start = ((), (), s32[]{:S(2)}) async-start(), calls=%async_computation.4 | async-start | bytes 1179648 | tf_op jit(solution)/shard_map/reduce_scatter | solution.py:204
  317.0 311.9 %all-reduce.2.cloned.1.call-start = ((), (), s32[]{:S(2)}) async-start(), calls=%async_computation.7 | async-start | bytes 1048576 | tf_op jit(solution)/shard_map/psum | solution.py:219
  317.3 1.7 copy-start.5
  319.6 135.5 %copy-start.3 = (f32[64,4096]{1,0:T(8,128)S(1)}, f32[64,4096]{1,0:T(8,128)}, u32[]{:S(2)}) copy-start(f32[64,4096]{1,0:T(8,128)} %get-tuple-element.423) | copy-start | bytes 3145732
Sparse Core Ops, SparseCore 0:
  9.9 74.0 all-gather.1
  230.6 76.8 reduce-scatter.5
  316.6 138.5 reduce-scatter.7
  459.4 77.4 reduce-scatter.3
  539.4 89.5 all-reduce.1
where the time goes:
time: 640 us; the launch traced here: 638 us
  waiting for transfers between devices  407 us (64%)
  blocking collectives  75 us (12%)
  local copies, waits for them, and re-layouts  52.9 us (8%)
  matrix products  46.5 us (7%)
  other arithmetic  29.4 us (5%)
  between operations  14.7 us (2%)
  loops' own time  11.9 us (2%)
    reduce_scatter x1, waiting for transfers between devices, on_device(): lax.psum_scatter(lax.dot_general(columns, d_value, (((0,), (0,)), ((), ()...  133 us
    psum x1, waiting for transfers between devices, on_device(): weight_grad = lax.psum(grad_share, 'ctx')  90.4 us
    reduce_scatter x1, waiting for transfers between devices, on_device(): lax.psum_scatter(dk_all, 'ctx', scatter_dimension=0, tiled=True)  79 us
    reduce_scatter x1, waiting for transfers between devices, on_device(): lax.psum_scatter(dv_all, 'ctx', scatter_dimension=0, tiled=True)  69.8 us
    all_gather x1, blocking collectives, on_device(): lax.all_gather(long_v, 'ctx', axis=0, tiled=True)  37.6 us
    all_gather x1, blocking collectives, on_device(): lax.all_gather(long_k, 'ctx', axis=0, tiled=True)  37.4 us
    all_gather x1, waiting for transfers between devices, on_device(): lax.all_gather(value_projection_weight, 'dp', axis=0, tiled=True)  32.9 us
    dynamic_slice x24, local copies, waits for them, and re-layouts, block_rows(): return lax.dynamic_slice_in_dim(source, block_id * LB, LB, 0)  20.7 us
  transfers between devices with their start and end apart: 5, of which 5 were waited for; matrix products, arithmetic and copies ran while one was open for 3% of the time, Pallas kernels for 0%

commit v1 on v0

v1 whole, which is shorter than its diff:
```python
import functools
import math

import jax
import jax.numpy as jnp
from jax import lax
from jax.experimental import pallas as pl
from jax.experimental.pallas import tpu as pltpu
from jax.sharding import Mesh
from jax.sharding import PartitionSpec as P

QUERY_HEADS = 32
KEY_VALUE_HEADS = 4
HEAD_SIZE = 128
GROUP = QUERY_HEADS // KEY_VALUE_HEADS
LB = 64
SB = 64
S_DOCS = 4
N_CTX = 8
CHUNK = 4
LANES = CHUNK * LB
SCALE = HEAD_SIZE ** -0.5
NEG = -1e30


def fill_masks(order_ref, place_ref, ends_ref, long_bias, short_bias):
    key = lax.broadcasted_iota(jnp.int32, (LB, LANES), 0)
    query = lax.broadcasted_iota(jnp.int32, (LB, LANES), 1) & (LB - 1)
    mine = place_ref[0]
    for block in range(N_CTX):
        ahead = order_ref[block] * LB + key <= mine * LB + query
        long_bias[pl.ds(block * LB, LB), :] = jnp.where(ahead, 0.0, NEG)
    key_doc = jnp.zeros((SB, LANES), jnp.int32)
    query_doc = jnp.zeros((SB, LANES), jnp.int32)
    for doc in range(S_DOCS):
        key_doc += (key >= ends_ref[doc]).astype(jnp.int32)
        query_doc += (query >= ends_ref[doc]).astype(jnp.int32)
    short_bias[...] = jnp.where((key_doc == query_doc) & (key <= query), 0.0, NEG)


def head_rows(ref, first, at):
    return jnp.concatenate(
        [ref[first:first + LB, (at + g) * HEAD_SIZE:(at + g + 1) * HEAD_SIZE] for g in range(CHUNK)],
        axis=0,
    )


def probs(keys, q_rows, bias):
    s = lax.dot_general(keys, q_rows, (((1,), (1,)), ((), ())), preferred_element_type=jnp.float32)
    s = s * (SCALE * math.log2(math.e)) + bias
    e = jnp.exp2(s - jnp.max(s, axis=0, keepdims=True))
    return e * (1.0 / jnp.sum(e, axis=0, keepdims=True))


def stacked(refs):
    return jnp.concatenate([ref[...] for ref in refs], axis=0)


def unstack(value, refs):
    for block, ref in enumerate(refs):
        ref[...] = value[block * LB:(block + 1) * LB].astype(ref.dtype)


def dvalue_kernel(order_ref, place_ref, ends_ref, slot_ref, q_ref, u_ref, ks_ref, *refs):
    k_refs, dvl_refs = refs[:N_CTX], refs[N_CTX:2 * N_CTX]
    dvs_ref, long_bias, short_bias = refs[2 * N_CTX:]

    @pl.when(pl.program_id(0) == 0)
    def _():
        fill_masks(order_ref, place_ref, ends_ref, long_bias, short_bias)

    for first, keys, bias, out in (
        (0, stacked(k_refs), long_bias, dvl_refs),
        (LB, ks_ref[LB:, :], short_bias, [dvs_ref]),
    ):
        total = None
        for at in range(0, GROUP, CHUNK):
            p = probs(keys, head_rows(q_ref, first, at), bias[...]).astype(jnp.bfloat16)
            part = jnp.dot(p, head_rows(u_ref, first, at), preferred_element_type=jnp.float32)
            total = part if total is None else total + part
        unstack(total, out)


def dscore_kernel(order_ref, place_ref, ends_ref, slot_ref, q_ref, u_ref, ks_ref, vs_ref, *refs):
    k_refs, v_refs = refs[:N_CTX], refs[N_CTX:2 * N_CTX]
    dq_ref, *dkl_refs = refs[2 * N_CTX:3 * N_CTX + 1]
    dks_ref, long_bias, short_bias = refs[3 * N_CTX + 1:]

    @pl.when(pl.program_id(0) == 0)
    def _():
        fill_masks(order_ref, place_ref, ends_ref, long_bias, short_bias)

    for first, keys, values, bias, out in (
        (0, stacked(k_refs), stacked(v_refs), long_bias, dkl_refs),
        (LB, ks_ref[LB:, :], vs_ref[LB:, :], short_bias, [dks_ref]),
    ):
        total = None
        for at in range(0, GROUP, CHUNK):
            q_rows = head_rows(q_ref, first, at)
            p = probs(keys, q_rows, bias[...])
            dp = lax.dot_general(values, head_rows(u_ref, first, at), (((1,), (1,)), ((), ())),
                                 preferred_element_type=jnp.float32)
            delta = jnp.sum(p * dp, axis=0, keepdims=True)
            ds = (p * (dp - delta)).astype(jnp.bfloat16)
            part = jnp.dot(ds, q_rows, preferred_element_type=jnp.float32)
            total = part if total is None else total + part
            dq = lax.dot_general(ds, keys, (((0,), (0,)), ((), ())),
                                 preferred_element_type=jnp.float32) * SCALE
            for g in range(CHUNK):
                dq_ref[first:first + LB, (at + g) * HEAD_SIZE:(at + g + 1) * HEAD_SIZE] = (
                    dq[g * LB:(g + 1) * LB])
        unstack(total * SCALE, out)


WIDE = GROUP * HEAD_SIZE


def block(rows, columns):
    return pl.BlockSpec((rows, columns), lambda k, *_: (0, k))


def slot_block(slot):
    return pl.BlockSpec((LB, HEAD_SIZE), lambda k, *scalars: (scalars[3][slot], k))


def scratch():
    return [pltpu.VMEM((N_CTX * LB, LANES), jnp.float32), pltpu.VMEM((SB, LANES), jnp.float32)]


def dvalues(scalars, queries, upstream, keys, all_keys, kind):
    tok = LB + SB
    long_rows = jax.ShapeDtypeStruct((LB, KEY_VALUE_HEADS * HEAD_SIZE), kind)
    out = pl.pallas_call(
        dvalue_kernel,
        grid_spec=pltpu.PrefetchScalarGridSpec(
            num_scalar_prefetch=4,
            grid=(KEY_VALUE_HEADS,),
            in_specs=[block(tok, WIDE)] * 2 + [block(tok, HEAD_SIZE)]
            + [slot_block(s) for s in range(N_CTX)],
            out_specs=[block(LB, HEAD_SIZE)] * N_CTX + [block(SB, HEAD_SIZE)],
            scratch_shapes=scratch(),
        ),
        out_shape=[long_rows] * N_CTX
        + [jax.ShapeDtypeStruct((SB, KEY_VALUE_HEADS * HEAD_SIZE), jnp.bfloat16)],
        compiler_params=pltpu.CompilerParams(vmem_limit_bytes=32 << 20),
        cost_estimate=pl.CostEstimate(flops=700_000_000, bytes_accessed=4 << 20, transcendentals=1 << 20),
    )(*scalars, queries, upstream, keys, *[all_keys] * N_CTX)
    return out[:N_CTX], out[N_CTX]


def dscores(scalars, queries, upstream, keys, values, all_keys, value_blocks, kind):
    tok = LB + SB
    long_rows = jax.ShapeDtypeStruct((LB, KEY_VALUE_HEADS * HEAD_SIZE), kind)
    out = pl.pallas_call(
        dscore_kernel,
        grid_spec=pltpu.PrefetchScalarGridSpec(
            num_scalar_prefetch=4,
            grid=(KEY_VALUE_HEADS,),
            in_specs=[block(tok, WIDE)] * 2 + [block(tok, HEAD_SIZE)] * 2
            + [slot_block(s) for s in range(N_CTX)] + [block(LB, HEAD_SIZE)] * N_CTX,
            out_specs=[block(tok, WIDE)] + [block(LB, HEAD_SIZE)] * N_CTX + [block(SB, HEAD_SIZE)],
            scratch_shapes=scratch(),
        ),
        out_shape=[jax.ShapeDtypeStruct((tok, QUERY_HEADS * HEAD_SIZE), jnp.float32)]
        + [long_rows] * N_CTX
        + [jax.ShapeDtypeStruct((SB, KEY_VALUE_HEADS * HEAD_SIZE), jnp.float32)],
        compiler_params=pltpu.CompilerParams(vmem_limit_bytes=32 << 20),
        cost_estimate=pl.CostEstimate(flops=1_400_000_000, bytes_accessed=6 << 20, transcendentals=1 << 20),
    )(*scalars, queries, upstream, keys, values, *[all_keys] * N_CTX, *value_blocks)
    return out[0], out[1:1 + N_CTX], out[1 + N_CTX]


Y_LO, CORES = 2, 2
DP = ("ylo", "z", "core")
CTX = ("yhi", "x")


PIECE = 32
DP_BLOCK = N_CTX * PIECE
TOGETHER = 4


def whole(count=1):
    return [pl.BlockSpec(memory_space=pltpu.VMEM)] * count


def regroup_kernel(me_ref, *refs):
    *block_refs, out_ref = refs
    for member in range(N_CTX):
        out_ref[member] = jnp.concatenate(
            [ref[:, member * PIECE:(member + 1) * PIECE] for ref in block_refs], axis=1)


def regroup(me, tokens):
    rows, width = tokens.shape
    depth = width // (DP_BLOCK * Y_LO * CORES)

    def source(at):
        def index(g, me_ref):
            slot = g * TOGETHER + at
            core, y_lo, z = slot // (Y_LO * depth), slot // depth % Y_LO, slot % depth
            return 0, ((y_lo * depth + z) * CORES + core) ^ me_ref[0]
        return pl.BlockSpec((rows, DP_BLOCK), index)

    return pl.pallas_call(
        regroup_kernel,
        grid_spec=pltpu.PrefetchScalarGridSpec(
            num_scalar_prefetch=1,
            grid=(width // (DP_BLOCK * TOGETHER),),
            in_specs=[source(at) for at in range(TOGETHER)],
            out_specs=pl.BlockSpec((N_CTX, rows, PIECE * TOGETHER), lambda g, *_: (0, 0, g)),
        ),
        out_shape=jax.ShapeDtypeStruct((N_CTX, rows, width // N_CTX), tokens.dtype),
        cost_estimate=pl.CostEstimate(flops=0, bytes_accessed=4 << 20, transcendentals=0),
    )(me[None], *[tokens] * TOGETHER)


def values_kernel(slot_ref, tokens_ref, mine_ref, theirs_ref, *refs):
    *out_refs, total = refs
    rows, columns = out_refs[0].shape
    weight = jnp.concatenate([mine_ref[...], theirs_ref[...]], axis=0)
    for first in range(0, total.shape[0], 2 * rows):
        total[first:first + 2 * rows] = jnp.dot(
            tokens_ref[first:first + 2 * rows], weight, preferred_element_type=jnp.float32)
    for slot, ref in enumerate(out_refs):
        start = pl.multiple_of(slot_ref[slot] * rows, rows)
        ref[...] = total[pl.ds(start, rows), :].astype(ref.dtype)


def value_parts(slots, tokens, mine, theirs):
    rows, columns = tokens.shape[0] // N_CTX, mine.shape[1]
    return pl.pallas_call(
        values_kernel,
        in_specs=[pl.BlockSpec(memory_space=pltpu.SMEM)] + whole(3),
        out_specs=whole(N_CTX),
        out_shape=[jax.ShapeDtypeStruct((rows, columns), jnp.bfloat16)] * N_CTX,
        scratch_shapes=[pltpu.VMEM((tokens.shape[0], columns), jnp.float32)],
        compiler_params=pltpu.CompilerParams(vmem_limit_bytes=32 << 20),
        cost_estimate=pl.CostEstimate(flops=2 * tokens.size * columns, bytes_accessed=4 << 20,
                                      transcendentals=0),
    )(slots, tokens, mine, theirs)


def weight_kernel(half, me_ref, tokens_ref, d_value_ref, *refs):
    *add_refs, out_ref = refs
    count, rows, columns = out_ref.shape
    some = min(DP_BLOCK // PIECE, count)
    for first in range(0, count, some):
        at = (half * count + first) * rows
        part = lax.dot_general(
            tokens_ref[:, at:at + some * rows], d_value_ref[...], (((0,), (0,)), ((), ())),
            preferred_element_type=jnp.float32)
        for slot in range(some):
            block = (first + slot) ^ me_ref[0]
            piece = part[slot * rows:(slot + 1) * rows]
            for ref in add_refs:
                piece += ref[block].astype(jnp.float32)
            out_ref[block] = piece.astype(out_ref.dtype)


def weight_share(half, me, tokens, d_value, *added):
    count, columns = tokens.shape[1] // (CORES * PIECE), d_value.shape[1]
    return pl.pallas_call(
        functools.partial(weight_kernel, half),
        in_specs=[pl.BlockSpec(memory_space=pltpu.SMEM)] + whole(2 + len(added)),
        out_specs=whole()[0],
        out_shape=jax.ShapeDtypeStruct((count, PIECE, columns), jnp.bfloat16),
        compiler_params=pltpu.CompilerParams(vmem_limit_bytes=32 << 20),
        cost_estimate=pl.CostEstimate(flops=tokens.size * columns, bytes_accessed=3 << 20,
                                      transcendentals=0),
    )(me[None], tokens, d_value, *added)


def exchange(pieces, axes):
    return lax.all_to_all(pieces, axes, 0, 0, tiled=True)


def spread(piece, axes):
    count = lax.axis_size(axes)
    return exchange(jnp.broadcast_to(piece[None], (count,) + piece.shape), axes)


def swap(array, step):
    return lax.ppermute(array, CTX, [(i, i ^ step) for i in range(N_CTX)]) if step else array


def total_kernel(pieces_ref, out_ref):
    total = pieces_ref[0].astype(jnp.float32)
    for piece in range(1, pieces_ref.shape[0]):
        total += pieces_ref[piece].astype(jnp.float32)
    out_ref[...] = total.astype(out_ref.dtype)


def total_of(pieces, kind):
    return pl.pallas_call(
        total_kernel,
        in_specs=[pl.BlockSpec(memory_space=pltpu.VMEM)],
        out_specs=pl.BlockSpec(memory_space=pltpu.VMEM),
        out_shape=jax.ShapeDtypeStruct(pieces.shape[1:], kind),
        cost_estimate=pl.CostEstimate(flops=pieces.size, bytes_accessed=2 * pieces.size, transcendentals=0),
    )(pieces)


def swap_along(array, axis, step):
    count = lax.axis_size(axis)
    return lax.ppermute(array, axis, [(i, i ^ step) for i in range(count)])


def on_device(tokens, queries, rotated_key_rows, upstream, value_projection_weight, doc_lengths,
              stretch_order):
    width = KEY_VALUE_HEADS * HEAD_SIZE
    tok_dev = LB + SB
    member = lax.axis_index(CTX)
    plane = lax.axis_index(("ylo", "z"))
    slots = member ^ jnp.arange(N_CTX, dtype=jnp.int32)
    order = jnp.take(stretch_order[0], slots)
    scalars = (order, order[:1], jnp.cumsum(doc_lengths[0]), slots)

    all_keys = spread(rotated_key_rows[:LB], CTX).reshape(N_CTX * LB, width)
    grouped = regroup(plane * CORES + lax.axis_index("core"), tokens)
    grouped, all_keys = lax.optimization_barrier((grouped, all_keys))
    tok = exchange(grouped, CTX).reshape(N_CTX * tok_dev, -1)

    dv_parts, dv_short = dvalues(scalars, queries, upstream, rotated_key_rows, all_keys, jnp.bfloat16)
    dv_long = sum(swap(dv_parts[s], s).astype(jnp.float32) for s in range(N_CTX)).astype(jnp.bfloat16)

    weight = lax.dynamic_slice_in_dim(value_projection_weight, member * PIECE, PIECE, 0)
    weight, _ = lax.optimization_barrier((weight, grouped))
    step = 1
    while step < lax.axis_size("z"):
        weight = jnp.concatenate([weight, swap_along(weight, "z", step)], axis=0)
        step *= 2
    weight = jnp.concatenate([weight, swap_along(weight, "ylo", 1)], axis=0)
    other_weight = swap_along(weight, "core", 1)

    d_value = jnp.concatenate([dv_long, dv_short], axis=0)
    d_value, tok, weight, other_weight = lax.optimization_barrier((d_value, tok, weight, other_weight))
    d_value = spread(d_value, CTX).reshape(N_CTX * tok_dev, width)
    parts = value_parts(slots, tok, weight, other_weight)
    values = sum(swap(parts[s], s).astype(jnp.float32) for s in range(N_CTX)).astype(jnp.bfloat16)

    share = swap_along(weight_share(1, plane, tok, d_value), "core", 1)
    share = weight_share(0, plane, tok, d_value, share)
    share, values = lax.optimization_barrier((share, values))
    share = exchange(share, ("ylo", "z"))
    value_blocks = [swap(values[:LB], s) for s in range(N_CTX)]
    share = total_of(share, jnp.bfloat16)
    share, value_blocks = lax.optimization_barrier((share, value_blocks))
    weight_grad = spread(share, CTX).reshape(DP_BLOCK, width).astype(jnp.float32)
    d_query, dk_parts, dk_short = dscores(scalars, queries, upstream, rotated_key_rows, values,
                                          all_keys, value_blocks, jnp.bfloat16)
    dk_long = sum(swap(dk_parts[s], s).astype(jnp.float32) for s in range(N_CTX))
    d_key = jnp.concatenate([dk_long, dk_short], axis=0)
    return d_query, d_key, weight_grad


def solution(mesh):
    packs = mesh.shape["dp"]
    mesh = Mesh(mesh.devices.reshape(Y_LO, packs // (Y_LO * CORES), CORES, 2, N_CTX // 2), DP + CTX)
    rows = P(DP + CTX, None)
    return jax.shard_map(
        on_device,
        mesh=mesh,
        in_specs=(rows, rows, rows, rows, P(DP, None), rows, P(DP, None)),
        out_specs=(rows, rows, P(DP, None)),
        check_vma=False,
    )
```

time: 640 us -> 200 us (0.31)
  waiting for transfers between devices: 407 us -> 49.4 us
  starting transfers between devices: 0.38 us -> 89.9 us
  blocking collectives: 75 us -> 19.2 us
  matrix products: 46.5 us -> 0 us
  local copies, waits for them, and re-layouts: 52.9 us -> 8.9 us
  Pallas kernels: 0 us -> 28.3 us
  other arithmetic: 29.4 us -> 2.12 us
  between operations: 14.7 us -> 0.92 us
  loops' own time: 11.9 us -> 0 us
    reduce_scatter x3 -> x0, waiting for transfers between devices: 282 us -> none  [the longest x1 133 us: on_device(): lax.psum_scatter(lax.dot_general(columns, d_value, (((0,), (0,)), ((), ()...]
    psum x1 -> x0, waiting for transfers between devices: 90.4 us -> none  [on_device(): weight_grad = lax.psum(grad_share, 'ctx')]
    all_gather x2 -> x0, blocking collectives: 75 us -> none  [the longest x1 37.6 us: on_device(): lax.all_gather(long_v, 'ctx', axis=0, tiled=True)]
    ppermute x0 -> x34, starting transfers between devices: none -> 65.2 us  [the longest x28 54.7 us: swap(): lax.ppermute(array, CTX, [(i, i ^ step) for i in range(N_CTX)])]
    dot_general x63 -> x0, matrix products: 46.5 us -> none  [the longest x17 13.3 us: dprob_block(): jnp.einsum('nkgd,mkd->kgnm', upstream_heads, value_heads, preferred_eleme...]
    ppermute x0 -> x34, waiting for transfers between devices: none -> 36.5 us  [the longest x6 18.8 us: swap_along(): return lax.ppermute(array, axis, [(i, i ^ step) for i in range(count)])]
    all_gather x1 -> x0, waiting for transfers between devices: 32.9 us -> none  [on_device(): lax.all_gather(value_projection_weight, 'dp', axis=0, tiled=True)]
    pallas_call x0 -> x7, Pallas kernels: none -> 28.3 us  [the longest x1 10.4 us: dscores(): pl.pallas_call(dscore_kernel, grid_spec=pltpu.PrefetchScalarGridSpec(num_...]
  transfers between devices with their start and end apart: 5 -> 38, of which waited for: 5 -> 15; matrix products, arithmetic and copies ran while one was open for 3% -> 1% of each run, Pallas kernels for 0% -> 8%
where the time goes in v1:
time: 200 us; the launch traced here: 199 us
  starting transfers between devices  89.9 us (45%)
  waiting for transfers between devices  49.4 us (25%)
  Pallas kernels  28.3 us (14%)
  blocking collectives  19.2 us (10%)
  local copies, waits for them, and re-layouts  8.9 us (4%)
  other arithmetic  2.12 us (1%)
    ppermute x28, starting transfers between devices, swap(): lax.ppermute(array, CTX, [(i, i ^ step) for i in range(N_CTX)])  54.7 us
    all_to_all x4, starting transfers between devices, exchange(): return lax.all_to_all(pieces, axes, 0, 0, tiled=True)  24.7 us
    all_to_all x1, blocking collectives, exchange(): return lax.all_to_all(pieces, axes, 0, 0, tiled=True)  19.2 us
    ppermute x6, waiting for transfers between devices, swap_along(): return lax.ppermute(array, axis, [(i, i ^ step) for i in range(count)])  18.8 us
    ppermute x28, waiting for transfers between devices, swap(): lax.ppermute(array, CTX, [(i, i ^ step) for i in range(N_CTX)])  17.7 us
    all_to_all x4, waiting for transfers between devices, exchange(): return lax.all_to_all(pieces, axes, 0, 0, tiled=True)  12.9 us
    ppermute x6, starting transfers between devices, swap_along(): return lax.ppermute(array, axis, [(i, i ^ step) for i in range(count)])  10.5 us
    pallas_call x1, Pallas kernels, dscores(): pl.pallas_call(dscore_kernel, grid_spec=pltpu.PrefetchScalarGridSpec(num_...  10.4 us
  transfers between devices with their start and end apart: 38, of which 15 were waited for; matrix products, arithmetic and copies ran while one was open for 1% of the time, Pallas kernels for 8%

profile of v1, /device:TPU:32, one launch (start us, length us, event | category | flops | bytes accessed | tf_op | source)
XLA Modules:
  0.0 198.7 jit_solution(3400313542800913892)
XLA Ops:
  0.6 0.9 slice.7
  1.5 0.8 broadcast_in_dim.14
  2.4 6.9 %all-to-all-start = ((bf16[8,64,512]{2,1,0:T(8,128)(2,1)}), bf16[8,64,512]{2,1,0:T(8,128)(2,1)S(1)}, u32[]{:S(2)}, u32[]{:S(2)}) async-start(bf16[8,64,512]{2,1,0:T(8,128)(2,1)} %broadcast_in_dim.14), calls=%async_computation | async-start | bytes 1048576 | tf_op jit(solution)/shard_map/all_to_all | solution.py:275
  9.3 6.6 %shard_map.94 = bf16[8,128,1024]{2,1,0:T(8,128)(2,1)} custom-call(s32[1]{0:T(128)} %bitcast.5.me_ref, bf16[128,8192]{1,0:T(8,128)(2,1)} %refs_3_.1, bf16[128,8192]{1,0:T(8,128)(2,1)} %refs_3_.1, bf16[128,8192]{1,0:T(8,128)(2,1)} %refs_3_.1, bf16[128,8192]{1,0:T(8,128)(2,1)} %refs_3_.1), custom_call_target="tpu_custom_call" | custom-call | bytes 4194304 | tf_op jit(solution)/shard_map/pallas_call | solution.py:205
  15.9 5.0 %all-to-all-done = bf16[8,64,512]{2,1,0:T(8,128)(2,1)S(1)} async-done(((bf16[8,64,512]{2,1,0:T(8,128)(2,1)}), bf16[8,64,512]{2,1,0:T(8,128)(2,1)S(1)}, u32[]{:S(2)}, u32[]{:S(2)}) %all-to-all-start) | async-done | bytes 524320 | tf_op jit(solution)/shard_map/all_to_all | solution.py:275
  20.9 3.7 %all-to-all-start.1 = ((bf16[8,128,1024]{2,1,0:T(8,128)(2,1)}), bf16[8,128,1024]{2,1,0:T(8,128)(2,1)S(1)}, u32[]{:S(2)}, u32[]{:S(2)}) async-start(bf16[8,128,1024]{2,1,0:T(8,128)(2,1)} %shard_map.94), calls=%async_computation.1 | async-start | bytes 4194304 | tf_op jit(solution)/shard_map/all_to_all | solution.py:275
  24.9 3.8 %collective-permute-done.7 = bf16[32,512]{1,0:T(8,128)(2,1)S(1)} collective-permute-done((bf16[32,512]{1,0:T(8,128)(2,1)S(1)}, bf16[32,512]{1,0:T(8,128)(2,1)S(1)}, u32[]{:S(2)}, u32[]{:S(2)}) %collective-permute-start.7) | collective-permute-done | bytes 32800 | tf_op jit(solution)/shard_map/ppermute | solution.py:306
  28.7 3.3 %collective-permute-start.8 = (bf16[64,512]{1,0:T(8,128)(2,1)S(1)}, bf16[64,512]{1,0:T(8,128)(2,1)S(1)}, u32[]{:S(2)}, u32[]{:S(2)}) collective-permute-start(bf16[64,512]{1,0:T(8,128)(2,1)S(1)} %pad_maximum_fusion.4), channel_id=1, source_target_pairs={{0,32},{16,48},{32,0},{48,16},{64,96},{80,112},{96,64},{112,80},{1... | collective-permute-start | bytes 196616 | tf_op jit(solution)/shard_map/ppermute | solution.py:306
  31.9 0.6 gather_fusion
  32.6 1.6 collective-permute-done.8
  34.2 6.1 %collective-permute-start.9 = (bf16[128,512]{1,0:T(8,128)(2,1)S(1)}, bf16[128,512]{1,0:T(8,128)(2,1)S(1)}, u32[]{:S(2)}, u32[]{:S(2)}) collective-permute-start(bf16[128,512]{1,0:T(8,128)(2,1)S(1)} %pad_maximum_fusion.3), channel_id=1, source_target_pairs={{0,64},{16,80},{32,96},{48,112},{64,0},{80,16},{96,32},{112,48},{1... | collective-permute-start | bytes 393224 | tf_op jit(solution)/shard_map/ppermute | solution.py:306
  40.5 3.5 %collective-permute-done.9 = bf16[128,512]{1,0:T(8,128)(2,1)S(1)} collective-permute-done((bf16[128,512]{1,0:T(8,128)(2,1)S(1)}, bf16[128,512]{1,0:T(8,128)(2,1)S(1)}, u32[]{:S(2)}, u32[]{:S(2)}) %collective-permute-start.9) | collective-permute-done | bytes 131104 | tf_op jit(solution)/shard_map/ppermute | solution.py:306
  44.0 0.8 collective-permute-start.10
  44.8 9.8 %collective-permute-done.10 = bf16[256,512]{1,0:T(8,128)(2,1)S(1)} collective-permute-done((bf16[256,512]{1,0:T(8,128)(2,1)S(1)}, bf16[256,512]{1,0:T(8,128)(2,1)S(1)}, u32[]{:S(2)}, u32[]{:S(2)}) %collective-permute-start.10) | collective-permute-done | bytes 262176 | tf_op jit(solution)/shard_map/ppermute | solution.py:306
  54.9 1.3 copy-done.3
  56.1 5.3 %shard_map.95 = (bf16[64,512]{1,0:T(8,128)(2,1)S(1)}, bf16[64,512]{1,0:T(8,128)(2,1)S(1)}, bf16[64,512]{1,0:T(8,128)(2,1)S(1)}, bf16[64,512]{1,0:T(8,128)(2,1)S(...) custom-call(s32[8]{0:T(128)S(1)} %get-tuple-element.93.order_ref, ...), custom_call_target="tpu_custom_call" | custom-call | flops 700000000 | bytes 4194304 | tf_op jit(solution)/shard_map/pallas_call | solution.py:133
  61.5 5.9 %collective-permute-start.6 = (bf16[64,512]{1,0:T(8,128)(2,1)S(1)}, bf16[64,512]{1,0:T(8,128)(2,1)S(1)}, u32[]{:S(2)}, u32[]{:S(2)}) collective-permute-start(bf16[64,512]{1,0:T(8,128)(2,1)S(1)} %get-tuple-element.56), channel_id=1, source_target_pairs={{0,7},{1,6},{2,5},{3,4},{4,3},{5,2},{6,1},{7,0},{8,15},{9,14},{10,... | collective-permute-start | bytes 196616 | tf_op jit(solution)/shard_map/ppermute | solution.py:284
  67.3 0.8 collective-permute-start.5
  68.1 3.0 %collective-permute-start.4 = (bf16[64,512]{1,0:T(8,128)(2,1)S(1)}, bf16[64,512]{1,0:T(8,128)(2,1)S(1)}, u32[]{:S(2)}, u32[]{:S(2)}) collective-permute-start(bf16[64,512]{1,0:T(8,128)(2,1)S(1)} %get-tuple-element.54), channel_id=1, source_target_pairs={{0,5},{1,4},{2,7},{3,6},{4,1},{5,0},{6,3},{7,2},{8,13},{9,12},{10,... | collective-permute-start | bytes 196616 | tf_op jit(solution)/shard_map/ppermute | solution.py:284
  71.1 0.6 collective-permute-start.3
  71.7 2.2 %collective-permute-start.2 = (bf16[64,512]{1,0:T(8,128)(2,1)S(1)}, bf16[64,512]{1,0:T(8,128)(2,1)S(1)}, u32[]{:S(2)}, u32[]{:S(2)}) collective-permute-start(bf16[64,512]{1,0:T(8,128)(2,1)S(1)} %get-tuple-element.52), channel_id=1, source_target_pairs={{0,3},{1,2},{2,1},{3,0},{4,7},{5,6},{6,5},{7,4},{8,11},{9,10},{10,... | collective-permute-start | bytes 196616 | tf_op jit(solution)/shard_map/ppermute | solution.py:284
  73.9 2.4 %collective-permute-done.5 = bf16[64,512]{1,0:T(8,128)(2,1)S(1)} collective-permute-done((bf16[64,512]{1,0:T(8,128)(2,1)S(1)}, bf16[64,512]{1,0:T(8,128)(2,1)S(1)}, u32[]{:S(2)}, u32[]{:S(2)}) %collective-permute-start.5) | collective-permute-done | bytes 65568 | tf_op jit(solution)/shard_map/ppermute | solution.py:284
  76.2 1.8 collective-permute-start.1
  78.1 3.9 %collective-permute-done.1 = bf16[64,512]{1,0:T(8,128)(2,1)S(1)} collective-permute-done((bf16[64,512]{1,0:T(8,128)(2,1)S(1)}, bf16[64,512]{1,0:T(8,128)(2,1)S(1)}, u32[]{:S(2)}, u32[]{:S(2)}) %collective-permute-start.1) | collective-permute-done | bytes 65568 | tf_op jit(solution)/shard_map/ppermute | solution.py:284
  82.4 0.8 copy-done.8
  83.3 19.2 %all_to_all.25 = bf16[8,128,512]{2,1,0:T(8,128)(2,1)S(1)} all-to-all(bf16[8,128,512]{2,1,0:T(8,128)(2,1)S(1)} %broadcast_in_dim.15), channel_id=1, replica_groups=mesh['ylo'=2,'z'=8,'core'=2,'yhi'=2,'x'=4] {'yhi','x'}, dimensions={0} | all-to-all | bytes 2097152 | tf_op jit(solution)/shard_map/all_to_all | solution.py:275
  102.5 0.8 shard_map.96
  103.7 1.9 shard_map.98
  105.6 1.6 collective-permute-start.19
  107.3 3.9 %collective-permute-start.18 = (bf16[128,512]{1,0:T(8,128)(2,1)S(1)}, bf16[128,512]{1,0:T(8,128)(2,1)S(1)}, u32[]{:S(2)}, u32[]{:S(2)}) collective-permute-start(bf16[128,512]{1,0:T(8,128)(2,1)S(1)} %get-tuple-element.70), channel_id=1, source_target_pairs={{0,6},{1,7},{2,4},{3,5},{4,2},{5,3},{6,0},{7,1},{8,14},{9,15},{10,... | collective-permute-start | bytes 393224 | tf_op jit(solution)/shard_map/ppermute | solution.py:284
  111.1 1.1 collective-permute-start.17
  112.2 3.0 %collective-permute-start.16 = (bf16[128,512]{1,0:T(8,128)(2,1)S(1)}, bf16[128,512]{1,0:T(8,128)(2,1)S(1)}, u32[]{:S(2)}, u32[]{:S(2)}) collective-permute-start(bf16[128,512]{1,0:T(8,128)(2,1)S(1)} %get-tuple-element.68), channel_id=1, source_target_pairs={{0,4},{1,5},{2,6},{3,7},{4,0},{5,1},{6,2},{7,3},{8,12},{9,13},{10,... | collective-permute-start | bytes 393224 | tf_op jit(solution)/shard_map/ppermute | solution.py:284
  115.2 4.1 %collective-permute-done.19 = bf16[128,512]{1,0:T(8,128)(2,1)S(1)} collective-permute-done((bf16[128,512]{1,0:T(8,128)(2,1)S(1)}, bf16[128,512]{1,0:T(8,128)(2,1)S(1)}, u32[]{:S(2)}, u32[]{:S(2)}) %collective-permute-start.19) | collective-permute-done | bytes 131104 | tf_op jit(solution)/shard_map/ppermute | solution.py:284
  119.3 1.3 collective-permute-start.15
  120.6 2.7 %collective-permute-start.13 = (bf16[128,512]{1,0:T(8,128)(2,1)S(1)}, bf16[128,512]{1,0:T(8,128)(2,1)S(1)}, u32[]{:S(2)}, u32[]{:S(2)}) collective-permute-start(bf16[128,512]{1,0:T(8,128)(2,1)S(1)} %get-tuple-element.65), channel_id=1, source_target_pairs={{0,1},{1,0},{2,3},{3,2},{4,5},{5,4},{6,7},{7,6},{8,9},{9,8},{10,11... | collective-permute-start | bytes 393224 | tf_op jit(solution)/shard_map/ppermute | solution.py:284
  123.4 2.1 %collective-permute-done.15 = bf16[128,512]{1,0:T(8,128)(2,1)S(1)} collective-permute-done((bf16[128,512]{1,0:T(8,128)(2,1)S(1)}, bf16[128,512]{1,0:T(8,128)(2,1)S(1)}, u32[]{:S(2)}, u32[]{:S(2)}) %collective-permute-start.15) | collective-permute-done | bytes 131104 | tf_op jit(solution)/shard_map/ppermute | solution.py:284
  125.4 1.6 collective-permute-done.14
  127.1 0.6 collective-permute-done.13
  127.9 1.6 shard_map.97
  129.4 8.4 %all-to-all-start.3 = ((bf16[16,32,512]{2,1,0:T(8,128)(2,1)}), bf16[16,32,512]{2,1,0:T(8,128)(2,1)S(1)}, u32[]{:S(2)}, u32[]{:S(2)}) async-start(bf16[16,32,512]{2,1,0:T(8,128)(2,1)} %shard_map.97), calls=%async_computation.3 | async-start | bytes 1048576 | tf_op jit(solution)/shard_map/all_to_all | solution.py:275
  137.9 0.7 collective-permute-start.20
  138.6 2.1 %collective-permute-start.21 = (bf16[64,512]{1,0:T(8,128)(2,1)S(1)}, bf16[64,512]{1,0:T(8,128)(2,1)S(1)}, u32[]{:S(2)}, u32[]{:S(2)}) collective-permute-start(bf16[64,512]{1,0:T(8,128)(2,1)S(1)} %slice.8.refs_8_), channel_id=1, source_target_pairs={{0,2},{1,3},{2,0},{3,1},{4,6},{5,7},{6,4},{7,5},{8,10},{9,11},{10,... | collective-permute-start | bytes 196616 | tf_op jit(solution)/shard_map/ppermute | solution.py:284
  140.7 2.0 collective-permute-start.22
  142.7 0.6 collective-permute-start.23
  143.3 1.7 collective-permute-start.24
  145.1 3.4 %collective-permute-start.25 = (bf16[64,512]{1,0:T(8,128)(2,1)S(1)}, bf16[64,512]{1,0:T(8,128)(2,1)S(1)}, u32[]{:S(2)}, u32[]{:S(2)}) collective-permute-start(bf16[64,512]{1,0:T(8,128)(2,1)S(1)} %slice.8.refs_8_), channel_id=1, source_target_pairs={{0,6},{1,7},{2,4},{3,5},{4,2},{5,3},{6,0},{7,1},{8,14},{9,15},{10,... | collective-permute-start | bytes 196616 | tf_op jit(solution)/shard_map/ppermute | solution.py:284
  148.5 4.3 %collective-permute-start.26 = (bf16[64,512]{1,0:T(8,128)(2,1)S(1)}, bf16[64,512]{1,0:T(8,128)(2,1)S(1)}, u32[]{:S(2)}, u32[]{:S(2)}) collective-permute-start(bf16[64,512]{1,0:T(8,128)(2,1)S(1)} %slice.8.refs_8_), channel_id=1, source_target_pairs={{0,7},{1,6},{2,5},{3,4},{4,3},{5,2},{6,1},{7,0},{8,15},{9,14},{10,... | collective-permute-start | bytes 196616 | tf_op jit(solution)/shard_map/ppermute | solution.py:284
  152.8 0.8 copy-done.11
  153.5 1.7 shard_map.99
  155.3 1.0 collective-permute-done.26.refs_15_
  156.3 1.2 copy-done.2
  157.6 1.2 copy-done.4
  158.8 10.4 %shard_map.100 = (f32[128,4096]{1,0:T(8,128)}, bf16[64,512]{1,0:T(8,128)(2,1)S(1)}, bf16[64,512]{1,0:T(8,128)(2,1)S(1)}, bf16[64,512]{1,0:T(8,128)(2,1)S(1)}, bf...) custom-call(s32[8]{0:T(128)S(1)} %get-tuple-element.93.order_ref, ...), custom_call_target="tpu_custom_call" | custom-call | flops 1400000000 | bytes 6291456 | tf_op jit(solution)/shard_map/pallas_call | solution.py:154
  169.2 4.3 %collective-permute-start.33 = (bf16[64,512]{1,0:T(8,128)(2,1)S(1)}, bf16[64,512]{1,0:T(8,128)(2,1)S(1)}, u32[]{:S(2)}, u32[]{:S(2)}) collective-permute-start(bf16[64,512]{1,0:T(8,128)(2,1)S(1)} %get-tuple-element.90), channel_id=1, source_target_pairs={{0,7},{1,6},{2,5},{3,4},{4,3},{5,2},{6,1},{7,0},{8,15},{9,14},{10,... | collective-permute-start | bytes 196616 | tf_op jit(solution)/shard_map/ppermute | solution.py:284
  173.5 4.5 %collective-permute-start.31 = (bf16[64,512]{1,0:T(8,128)(2,1)S(1)}, bf16[64,512]{1,0:T(8,128)(2,1)S(1)}, u32[]{:S(2)}, u32[]{:S(2)}) collective-permute-start(bf16[64,512]{1,0:T(8,128)(2,1)S(1)} %get-tuple-element.88), channel_id=1, source_target_pairs={{0,5},{1,4},{2,7},{3,6},{4,1},{5,0},{6,3},{7,2},{8,13},{9,12},{10,... | collective-permute-start | bytes 196616 | tf_op jit(solution)/shard_map/ppermute | solution.py:284
  178.0 0.6 collective-permute-start.30
  178.7 2.0 collective-permute-start.29
  180.7 1.5 collective-permute-done.32
  182.2 0.6 collective-permute-start.27
  182.8 0.7 broadcast_in_dim.16
  183.5 5.6 %all-to-all-start.4 = ((bf16[8,32,512]{2,1,0:T(8,128)(2,1)}), bf16[8,32,512]{2,1,0:T(8,128)(2,1)S(1)}, u32[]{:S(2)}, u32[]{:S(2)}) async-start(bf16[8,32,512]{2,1,0:T(8,128)(2,1)} %broadcast_in_dim.16), calls=%async_computation.4 | async-start | bytes 524288 | tf_op jit(solution)/shard_map/all_to_all | solution.py:275
  189.2 0.7 pad_maximum_fusion.1
  189.9 7.9 %all-to-all-done.4 = bf16[8,32,512]{2,1,0:T(8,128)(2,1)S(1)} async-done(((bf16[8,32,512]{2,1,0:T(8,128)(2,1)}), bf16[8,32,512]{2,1,0:T(8,128)(2,1)S(1)}, u32[]{:S(2)}, u32[]{:S(2)}) %all-to-all-start.4) | async-done | bytes 262176 | tf_op jit(solution)/shard_map/all_to_all | solution.py:275
  197.8 0.9 bitcast_convert_fusion
  (73 shorter events, 1.8 us)
Async XLA Ops:
  0.6 15.3 %copy-start = (bf16[256,512]{1,0:T(8,128)(2,1)S(1)}, bf16[256,512]{1,0:T(8,128)(2,1)}, u32[]{:S(2)}) copy-start(bf16[256,512]{1,0:T(8,128)(2,1)} %param.11) | copy-start | bytes 786436
  2.4 18.5 %all-to-all-start = ((bf16[8,64,512]{2,1,0:T(8,128)(2,1)}), bf16[8,64,512]{2,1,0:T(8,128)(2,1)S(1)}, u32[]{:S(2)}, u32[]{:S(2)}) async-start(bf16[8,64,512]{2,1,0:T(8,128)(2,1)} %broadcast_in_dim.14), calls=%async_computation | async-start | bytes 1048576 | tf_op jit(solution)/shard_map/all_to_all | solution.py:275
  20.9 11.0 %copy-start.10 = (s32[1,8]{1,0:T(1,128)S(1)}, s32[1,8]{1,0:T(1,128)}, u32[]{:S(2)}) copy-start(s32[1,8]{1,0:T(1,128)} %param.13) | copy-start | bytes 100
  20.9 19.4 %copy-start.13 = (s32[1,4]{1,0:T(1,128)S(1)}, s32[1,4]{1,0:T(1,128)}, u32[]{:S(2)}) copy-start(s32[1,4]{1,0:T(1,128)} %param.12) | copy-start | bytes 52
  20.9 62.3 %all-to-all-start.1 = ((bf16[8,128,1024]{2,1,0:T(8,128)(2,1)}), bf16[8,128,1024]{2,1,0:T(8,128)(2,1)S(1)}, u32[]{:S(2)}, u32[]{:S(2)}) async-start(bf16[8,128,1024]{2,1,0:T(8,128)(2,1)} %shard_map.94), calls=%async_computation.1 | async-start | bytes 4194304 | tf_op jit(solution)/shard_map/all_to_all | solution.py:275
  24.6 30.2 %copy-start.5 = (bf16[128,512]{1,0:T(8,128)(2,1)S(1)}, bf16[128,512]{1,0:T(8,128)(2,1)}, u32[]{:S(2)}) copy-start(bf16[128,512]{1,0:T(8,128)(2,1)} %ks_ref.3) | copy-start | bytes 393220
  24.6 4.0 %collective-permute-start.7 = (bf16[32,512]{1,0:T(8,128)(2,1)S(1)}, bf16[32,512]{1,0:T(8,128)(2,1)S(1)}, u32[]{:S(2)}, u32[]{:S(2)}) collective-permute-start(bf16[32,512]{1,0:T(8,128)(2,1)S(1)} %constant_dynamic-slice_fusion), channel_id=1, source_target_pairs={{0,16},{16,0},{32,48},{48,32},{64,80},{80,64},{96,112},{112,96},{1... | collective-permute-start | bytes 98312 | tf_op jit(solution)/shard_map/ppermute | solution.py:306
  28.7 5.5 %collective-permute-start.8 = (bf16[64,512]{1,0:T(8,128)(2,1)S(1)}, bf16[64,512]{1,0:T(8,128)(2,1)S(1)}, u32[]{:S(2)}, u32[]{:S(2)}) collective-permute-start(bf16[64,512]{1,0:T(8,128)(2,1)S(1)} %pad_maximum_fusion.4), channel_id=1, source_target_pairs={{0,32},{16,48},{32,0},{48,16},{64,96},{80,112},{96,64},{112,80},{1... | collective-permute-start | bytes 196616 | tf_op jit(solution)/shard_map/ppermute | solution.py:306
  34.2 9.8 %collective-permute-start.9 = (bf16[128,512]{1,0:T(8,128)(2,1)S(1)}, bf16[128,512]{1,0:T(8,128)(2,1)S(1)}, u32[]{:S(2)}, u32[]{:S(2)}) collective-permute-start(bf16[128,512]{1,0:T(8,128)(2,1)S(1)} %pad_maximum_fusion.3), channel_id=1, source_target_pairs={{0,64},{16,80},{32,96},{48,112},{64,0},{80,16},{96,32},{112,48},{1... | collective-permute-start | bytes 393224 | tf_op jit(solution)/shard_map/ppermute | solution.py:306
  40.5 14.3 %copy-start.1 = (bf16[128,4096]{1,0:T(8,128)(2,1)S(1)}, bf16[128,4096]{1,0:T(8,128)(2,1)}, u32[]{:S(2)}) copy-start(bf16[128,4096]{1,0:T(8,128)(2,1)} %q_ref.3) | copy-start | bytes 3145732
  44.0 10.6 %collective-permute-start.10 = (bf16[256,512]{1,0:T(8,128)(2,1)S(1)}, bf16[256,512]{1,0:T(8,128)(2,1)S(1)}, u32[]{:S(2)}, u32[]{:S(2)}) collective-permute-start(bf16[256,512]{1,0:T(8,128)(2,1)S(1)} %pad_maximum_fusion), channel_id=1, source_target_pairs={{0,128},{128,0},{1,129},{129,1},{2,130},{130,2},{3,131},{131,3},{4... | collective-permute-start | bytes 786440 | tf_op jit(solution)/shard_map/ppermute | solution.py:306
  54.7 6.8 %copy-start.6 = (bf16[512,512]{1,0:T(8,128)(2,1)}, bf16[512,512]{1,0:T(8,128)(2,1)S(1)}, u32[]{:S(2)}) copy-start(bf16[512,512]{1,0:T(8,128)(2,1)S(1)} %constant_dynamic-update-slice_fusion.mine_ref) | copy-start | bytes 1572868
  54.7 27.7 %collective-permute-start.11 = (bf16[512,512]{1,0:T(8,128)(2,1)S(1)}, bf16[512,512]{1,0:T(8,128)(2,1)S(1)}, u32[]{:S(2)}, u32[]{:S(2)}) collective-permute-start(bf16[512,512]{1,0:T(8,128)(2,1)S(1)} %constant_dynamic-update-slice_fusion.mine_ref), channel_id=1, source_target_pairs={{0,8},{8,0},{1,9},{9,1},{2,10},{10,2},{3,11},{11,3},{4,12},{12,4},... | collective-permute-start | bytes 1572872 | tf_op jit(solution)/shard_map/ppermute | solution.py:306
  54.8 1.3 copy-start.3
  61.5 10.2 %collective-permute-start.6 = (bf16[64,512]{1,0:T(8,128)(2,1)S(1)}, bf16[64,512]{1,0:T(8,128)(2,1)S(1)}, u32[]{:S(2)}, u32[]{:S(2)}) collective-permute-start(bf16[64,512]{1,0:T(8,128)(2,1)S(1)} %get-tuple-element.56), channel_id=1, source_target_pairs={{0,7},{1,6},{2,5},{3,4},{4,3},{5,2},{6,1},{7,0},{8,15},{9,14},{10,... | collective-permute-start | bytes 196616 | tf_op jit(solution)/shard_map/ppermute | solution.py:284
  67.3 8.9 %collective-permute-start.5 = (bf16[64,512]{1,0:T(8,128)(2,1)S(1)}, bf16[64,512]{1,0:T(8,128)(2,1)S(1)}, u32[]{:S(2)}, u32[]{:S(2)}) collective-permute-start(bf16[64,512]{1,0:T(8,128)(2,1)S(1)} %get-tuple-element.55), channel_id=1, source_target_pairs={{0,6},{1,7},{2,4},{3,5},{4,2},{5,3},{6,0},{7,1},{8,14},{9,15},{10,... | collective-permute-start | bytes 196616 | tf_op jit(solution)/shard_map/ppermute | solution.py:284
  68.1 9.9 %collective-permute-start.4 = (bf16[64,512]{1,0:T(8,128)(2,1)S(1)}, bf16[64,512]{1,0:T(8,128)(2,1)S(1)}, u32[]{:S(2)}, u32[]{:S(2)}) collective-permute-start(bf16[64,512]{1,0:T(8,128)(2,1)S(1)} %get-tuple-element.54), channel_id=1, source_target_pairs={{0,5},{1,4},{2,7},{3,6},{4,1},{5,0},{6,3},{7,2},{8,13},{9,12},{10,... | collective-permute-start | bytes 196616 | tf_op jit(solution)/shard_map/ppermute | solution.py:284
  71.1 7.0 %collective-permute-start.3 = (bf16[64,512]{1,0:T(8,128)(2,1)S(1)}, bf16[64,512]{1,0:T(8,128)(2,1)S(1)}, u32[]{:S(2)}, u32[]{:S(2)}) collective-permute-start(bf16[64,512]{1,0:T(8,128)(2,1)S(1)} %get-tuple-element.53), channel_id=1, source_target_pairs={{0,4},{1,5},{2,6},{3,7},{4,0},{5,1},{6,2},{7,3},{8,12},{9,13},{10,... | collective-permute-start | bytes 196616 | tf_op jit(solution)/shard_map/ppermute | solution.py:284
  71.7 6.4 %collective-permute-start.2 = (bf16[64,512]{1,0:T(8,128)(2,1)S(1)}, bf16[64,512]{1,0:T(8,128)(2,1)S(1)}, u32[]{:S(2)}, u32[]{:S(2)}) collective-permute-start(bf16[64,512]{1,0:T(8,128)(2,1)S(1)} %get-tuple-element.52), channel_id=1, source_target_pairs={{0,3},{1,2},{2,1},{3,0},{4,7},{5,6},{6,5},{7,4},{8,11},{9,10},{10,... | collective-permute-start | bytes 196616 | tf_op jit(solution)/shard_map/ppermute | solution.py:284
  76.2 5.8 %collective-permute-start.1 = (bf16[64,512]{1,0:T(8,128)(2,1)S(1)}, bf16[64,512]{1,0:T(8,128)(2,1)S(1)}, u32[]{:S(2)}, u32[]{:S(2)}) collective-permute-start(bf16[64,512]{1,0:T(8,128)(2,1)S(1)} %get-tuple-element.51), channel_id=1, source_target_pairs={{0,2},{1,3},{2,0},{3,1},{4,6},{5,7},{6,4},{7,5},{8,10},{9,11},{10,... | collective-permute-start | bytes 196616 | tf_op jit(solution)/shard_map/ppermute | solution.py:284
  78.1 4.3 %collective-permute-start = (bf16[64,512]{1,0:T(8,128)(2,1)S(1)}, bf16[64,512]{1,0:T(8,128)(2,1)S(1)}, u32[]{:S(2)}, u32[]{:S(2)}) collective-permute-start(bf16[64,512]{1,0:T(8,128)(2,1)S(1)} %get-tuple-element.50), channel_id=1, source_target_pairs={{0,1},{1,0},{2,3},{3,2},{4,5},{5,4},{6,7},{7,6},{8,9},{9,8},{10,11... | collective-permute-start | bytes 196616 | tf_op jit(solution)/shard_map/ppermute | solution.py:284
  82.4 0.8 copy-start.8
  102.5 1.0 copy-start.7
  102.5 1.2 copy-start.9
  103.3 24.6 %collective-permute-start.12 = (bf16[16,32,512]{2,1,0:T(8,128)(2,1)S(1)}, bf16[16,32,512]{2,1,0:T(8,128)(2,1)S(1)}, u32[]{:S(2)}, u32[]{:S(2)}) collective-permute-start(bf16[16,32,512]{2,1,0:T(8,128)(2,1)S(1)} %shard_map.96), channel_id=1, source_target_pairs={{0,8},{8,0},{1,9},{9,1},{2,10},{10,2},{3,11},{11,3},{4,12},{12,4},... | collective-permute-start | bytes 1572872 | tf_op jit(solution)/shard_map/ppermute | solution.py:306
  105.6 13.6 %collective-permute-start.19 = (bf16[128,512]{1,0:T(8,128)(2,1)S(1)}, bf16[128,512]{1,0:T(8,128)(2,1)S(1)}, u32[]{:S(2)}, u32[]{:S(2)}) collective-permute-start(bf16[128,512]{1,0:T(8,128)(2,1)S(1)} %get-tuple-element.71), channel_id=1, source_target_pairs={{0,7},{1,6},{2,5},{3,4},{4,3},{5,2},{6,1},{7,0},{8,15},{9,14},{10,... | collective-permute-start | bytes 393224 | tf_op jit(solution)/shard_map/ppermute | solution.py:284
  107.3 13.3 %collective-permute-start.18 = (bf16[128,512]{1,0:T(8,128)(2,1)S(1)}, bf16[128,512]{1,0:T(8,128)(2,1)S(1)}, u32[]{:S(2)}, u32[]{:S(2)}) collective-permute-start(bf16[128,512]{1,0:T(8,128)(2,1)S(1)} %get-tuple-element.70), channel_id=1, source_target_pairs={{0,6},{1,7},{2,4},{3,5},{4,2},{5,3},{6,0},{7,1},{8,14},{9,15},{10,... | collective-permute-start | bytes 393224 | tf_op jit(solution)/shard_map/ppermute | solution.py:284
  111.1 9.5 %collective-permute-start.17 = (bf16[128,512]{1,0:T(8,128)(2,1)S(1)}, bf16[128,512]{1,0:T(8,128)(2,1)S(1)}, u32[]{:S(2)}, u32[]{:S(2)}) collective-permute-start(bf16[128,512]{1,0:T(8,128)(2,1)S(1)} %get-tuple-element.69), channel_id=1, source_target_pairs={{0,5},{1,4},{2,7},{3,6},{4,1},{5,0},{6,3},{7,2},{8,13},{9,12},{10,... | collective-permute-start | bytes 393224 | tf_op jit(solution)/shard_map/ppermute | solution.py:284
  112.2 11.2 %collective-permute-start.16 = (bf16[128,512]{1,0:T(8,128)(2,1)S(1)}, bf16[128,512]{1,0:T(8,128)(2,1)S(1)}, u32[]{:S(2)}, u32[]{:S(2)}) collective-permute-start(bf16[128,512]{1,0:T(8,128)(2,1)S(1)} %get-tuple-element.68), channel_id=1, source_target_pairs={{0,4},{1,5},{2,6},{3,7},{4,0},{5,1},{6,2},{7,3},{8,12},{9,13},{10,... | collective-permute-start | bytes 393224 | tf_op jit(solution)/shard_map/ppermute | solution.py:284
  119.3 6.2 %collective-permute-start.15 = (bf16[128,512]{1,0:T(8,128)(2,1)S(1)}, bf16[128,512]{1,0:T(8,128)(2,1)S(1)}, u32[]{:S(2)}, u32[]{:S(2)}) collective-permute-start(bf16[128,512]{1,0:T(8,128)(2,1)S(1)} %get-tuple-element.67), channel_id=1, source_target_pairs={{0,3},{1,2},{2,1},{3,0},{4,7},{5,6},{6,5},{7,4},{8,11},{9,10},{10,... | collective-permute-start | bytes 393224 | tf_op jit(solution)/shard_map/ppermute | solution.py:284
  120.6 6.5 %collective-permute-start.14 = (bf16[128,512]{1,0:T(8,128)(2,1)S(1)}, bf16[128,512]{1,0:T(8,128)(2,1)S(1)}, u32[]{:S(2)}, u32[]{:S(2)}) collective-permute-start(bf16[128,512]{1,0:T(8,128)(2,1)S(1)} %get-tuple-element.66), channel_id=1, source_target_pairs={{0,2},{1,3},{2,0},{3,1},{4,6},{5,7},{6,4},{7,5},{8,10},{9,11},{10,... | collective-permute-start | bytes 393224 | tf_op jit(solution)/shard_map/ppermute | solution.py:284
  120.6 7.1 %collective-permute-start.13 = (bf16[128,512]{1,0:T(8,128)(2,1)S(1)}, bf16[128,512]{1,0:T(8,128)(2,1)S(1)}, u32[]{:S(2)}, u32[]{:S(2)}) collective-permute-start(bf16[128,512]{1,0:T(8,128)(2,1)S(1)} %get-tuple-element.65), channel_id=1, source_target_pairs={{0,1},{1,0},{2,3},{3,2},{4,5},{5,4},{6,7},{7,6},{8,9},{9,8},{10,11... | collective-permute-start | bytes 393224 | tf_op jit(solution)/shard_map/ppermute | solution.py:284
  129.4 23.3 %all-to-all-start.3 = ((bf16[16,32,512]{2,1,0:T(8,128)(2,1)}), bf16[16,32,512]{2,1,0:T(8,128)(2,1)S(1)}, u32[]{:S(2)}, u32[]{:S(2)}) async-start(bf16[16,32,512]{2,1,0:T(8,128)(2,1)} %shard_map.97), calls=%async_computation.3 | async-start | bytes 1048576 | tf_op jit(solution)/shard_map/all_to_all | solution.py:275
  137.9 7.2 %collective-permute-start.20 = (bf16[64,512]{1,0:T(8,128)(2,1)S(1)}, bf16[64,512]{1,0:T(8,128)(2,1)S(1)}, u32[]{:S(2)}, u32[]{:S(2)}) collective-permute-start(bf16[64,512]{1,0:T(8,128)(2,1)S(1)} %slice.8.refs_8_), channel_id=1, source_target_pairs={{0,1},{1,0},{2,3},{3,2},{4,5},{5,4},{6,7},{7,6},{8,9},{9,8},{10,11... | collective-permute-start | bytes 196616 | tf_op jit(solution)/shard_map/ppermute | solution.py:284
  138.6 9.9 %collective-permute-start.21 = (bf16[64,512]{1,0:T(8,128)(2,1)S(1)}, bf16[64,512]{1,0:T(8,128)(2,1)S(1)}, u32[]{:S(2)}, u32[]{:S(2)}) collective-permute-start(bf16[64,512]{1,0:T(8,128)(2,1)S(1)} %slice.8.refs_8_), channel_id=1, source_target_pairs={{0,2},{1,3},{2,0},{3,1},{4,6},{5,7},{6,4},{7,5},{8,10},{9,11},{10,... | collective-permute-start | bytes 196616 | tf_op jit(solution)/shard_map/ppermute | solution.py:284
  140.7 14.6 %collective-permute-start.22 = (bf16[64,512]{1,0:T(8,128)(2,1)S(1)}, bf16[64,512]{1,0:T(8,128)(2,1)S(1)}, u32[]{:S(2)}, u32[]{:S(2)}) collective-permute-start(bf16[64,512]{1,0:T(8,128)(2,1)S(1)} %slice.8.refs_8_), channel_id=1, source_target_pairs={{0,3},{1,2},{2,1},{3,0},{4,7},{5,6},{6,5},{7,4},{8,11},{9,10},{10,... | collective-permute-start | bytes 196616 | tf_op jit(solution)/shard_map/ppermute | solution.py:284
  142.7 12.6 %collective-permute-start.23 = (bf16[64,512]{1,0:T(8,128)(2,1)S(1)}, bf16[64,512]{1,0:T(8,128)(2,1)S(1)}, u32[]{:S(2)}, u32[]{:S(2)}) collective-permute-start(bf16[64,512]{1,0:T(8,128)(2,1)S(1)} %slice.8.refs_8_), channel_id=1, source_target_pairs={{0,4},{1,5},{2,6},{3,7},{4,0},{5,1},{6,2},{7,3},{8,12},{9,13},{10,... | collective-permute-start | bytes 196616 | tf_op jit(solution)/shard_map/ppermute | solution.py:284
  143.3 12.0 %collective-permute-start.24 = (bf16[64,512]{1,0:T(8,128)(2,1)S(1)}, bf16[64,512]{1,0:T(8,128)(2,1)S(1)}, u32[]{:S(2)}, u32[]{:S(2)}) collective-permute-start(bf16[64,512]{1,0:T(8,128)(2,1)S(1)} %slice.8.refs_8_), channel_id=1, source_target_pairs={{0,5},{1,4},{2,7},{3,6},{4,1},{5,0},{6,3},{7,2},{8,13},{9,12},{10,... | collective-permute-start | bytes 196616 | tf_op jit(solution)/shard_map/ppermute | solution.py:284
  145.1 10.2 %collective-permute-start.25 = (bf16[64,512]{1,0:T(8,128)(2,1)S(1)}, bf16[64,512]{1,0:T(8,128)(2,1)S(1)}, u32[]{:S(2)}, u32[]{:S(2)}) collective-permute-start(bf16[64,512]{1,0:T(8,128)(2,1)S(1)} %slice.8.refs_8_), channel_id=1, source_target_pairs={{0,6},{1,7},{2,4},{3,5},{4,2},{5,3},{6,0},{7,1},{8,14},{9,15},{10,... | collective-permute-start | bytes 196616 | tf_op jit(solution)/shard_map/ppermute | solution.py:284
  148.5 7.9 %collective-permute-start.26 = (bf16[64,512]{1,0:T(8,128)(2,1)S(1)}, bf16[64,512]{1,0:T(8,128)(2,1)S(1)}, u32[]{:S(2)}, u32[]{:S(2)}) collective-permute-start(bf16[64,512]{1,0:T(8,128)(2,1)S(1)} %slice.8.refs_8_), channel_id=1, source_target_pairs={{0,7},{1,6},{2,5},{3,4},{4,3},{5,2},{6,1},{7,0},{8,15},{9,14},{10,... | collective-permute-start | bytes 196616 | tf_op jit(solution)/shard_map/ppermute | solution.py:284
  152.8 0.8 copy-start.11
  156.3 1.2 copy-start.2
  157.6 1.2 copy-start.4
  158.8 24.0 %copy-start.12 = (bf16[32,512]{1,0:T(8,128)(2,1)S(1)}, bf16[32,512]{1,0:T(8,128)(2,1)}, u32[]{:S(2)}) copy-start(bf16[32,512]{1,0:T(8,128)(2,1)} %shard_map.99) | copy-start | bytes 98308
  169.2 11.4 %collective-permute-start.33 = (bf16[64,512]{1,0:T(8,128)(2,1)S(1)}, bf16[64,512]{1,0:T(8,128)(2,1)S(1)}, u32[]{:S(2)}, u32[]{:S(2)}) collective-permute-start(bf16[64,512]{1,0:T(8,128)(2,1)S(1)} %get-tuple-element.90), channel_id=1, source_target_pairs={{0,7},{1,6},{2,5},{3,4},{4,3},{5,2},{6,1},{7,0},{8,15},{9,14},{10,... | collective-permute-start | bytes 196616 | tf_op jit(solution)/shard_map/ppermute | solution.py:284
  173.5 8.7 %collective-permute-start.32 = (bf16[64,512]{1,0:T(8,128)(2,1)S(1)}, bf16[64,512]{1,0:T(8,128)(2,1)S(1)}, u32[]{:S(2)}, u32[]{:S(2)}) collective-permute-start(bf16[64,512]{1,0:T(8,128)(2,1)S(1)} %get-tuple-element.89), channel_id=1, source_target_pairs={{0,6},{1,7},{2,4},{3,5},{4,2},{5,3},{6,0},{7,1},{8,14},{9,15},{10,... | collective-permute-start | bytes 196616 | tf_op jit(solution)/shard_map/ppermute | solution.py:284
  173.5 15.6 %collective-permute-start.31 = (bf16[64,512]{1,0:T(8,128)(2,1)S(1)}, bf16[64,512]{1,0:T(8,128)(2,1)S(1)}, u32[]{:S(2)}, u32[]{:S(2)}) collective-permute-start(bf16[64,512]{1,0:T(8,128)(2,1)S(1)} %get-tuple-element.88), channel_id=1, source_target_pairs={{0,5},{1,4},{2,7},{3,6},{4,1},{5,0},{6,3},{7,2},{8,13},{9,12},{10,... | collective-permute-start | bytes 196616 | tf_op jit(solution)/shard_map/ppermute | solution.py:284
  178.0 11.0 %collective-permute-start.30 = (bf16[64,512]{1,0:T(8,128)(2,1)S(1)}, bf16[64,512]{1,0:T(8,128)(2,1)S(1)}, u32[]{:S(2)}, u32[]{:S(2)}) collective-permute-start(bf16[64,512]{1,0:T(8,128)(2,1)S(1)} %get-tuple-element.87), channel_id=1, source_target_pairs={{0,4},{1,5},{2,6},{3,7},{4,0},{5,1},{6,2},{7,3},{8,12},{9,13},{10,... | collective-permute-start | bytes 196616 | tf_op jit(solution)/shard_map/ppermute | solution.py:284
  178.7 10.4 %collective-permute-start.29 = (bf16[64,512]{1,0:T(8,128)(2,1)S(1)}, bf16[64,512]{1,0:T(8,128)(2,1)S(1)}, u32[]{:S(2)}, u32[]{:S(2)}) collective-permute-start(bf16[64,512]{1,0:T(8,128)(2,1)S(1)} %get-tuple-element.86), channel_id=1, source_target_pairs={{0,3},{1,2},{2,1},{3,0},{4,7},{5,6},{6,5},{7,4},{8,11},{9,10},{10,... | collective-permute-start | bytes 196616 | tf_op jit(solution)/shard_map/ppermute | solution.py:284
  180.6 8.5 %collective-permute-start.28 = (bf16[64,512]{1,0:T(8,128)(2,1)S(1)}, bf16[64,512]{1,0:T(8,128)(2,1)S(1)}, u32[]{:S(2)}, u32[]{:S(2)}) collective-permute-start(bf16[64,512]{1,0:T(8,128)(2,1)S(1)} %get-tuple-element.85), channel_id=1, source_target_pairs={{0,2},{1,3},{2,0},{3,1},{4,6},{5,7},{6,4},{7,5},{8,10},{9,11},{10,... | collective-permute-start | bytes 196616 | tf_op jit(solution)/shard_map/ppermute | solution.py:284
  182.2 6.9 %collective-permute-start.27 = (bf16[64,512]{1,0:T(8,128)(2,1)S(1)}, bf16[64,512]{1,0:T(8,128)(2,1)S(1)}, u32[]{:S(2)}, u32[]{:S(2)}) collective-permute-start(bf16[64,512]{1,0:T(8,128)(2,1)S(1)} %get-tuple-element.84), channel_id=1, source_target_pairs={{0,1},{1,0},{2,3},{3,2},{4,5},{5,4},{6,7},{7,6},{8,9},{9,8},{10,11... | collective-permute-start | bytes 196616 | tf_op jit(solution)/shard_map/ppermute | solution.py:284
  183.5 14.3 %all-to-all-start.4 = ((bf16[8,32,512]{2,1,0:T(8,128)(2,1)}), bf16[8,32,512]{2,1,0:T(8,128)(2,1)S(1)}, u32[]{:S(2)}, u32[]{:S(2)}) async-start(bf16[8,32,512]{2,1,0:T(8,128)(2,1)} %broadcast_in_dim.16), calls=%async_computation.4 | async-start | bytes 524288 | tf_op jit(solution)/shard_map/all_to_all | solution.py:275

commit v2 on v1

v2 whole, which is shorter than its diff:
```python
import functools
import math

import jax
import jax.numpy as jnp
from jax import lax
from jax.experimental import pallas as pl
from jax.experimental.pallas import tpu as pltpu
from jax.sharding import Mesh
from jax.sharding import PartitionSpec as P

QUERY_HEADS = 32
KEY_VALUE_HEADS = 4
HEAD_SIZE = 128
GROUP = QUERY_HEADS // KEY_VALUE_HEADS
LB = 64
SB = 64
S_DOCS = 4
N_CTX = 8
CHUNK = 4
LANES = CHUNK * LB
SCALE = HEAD_SIZE ** -0.5
NEG = -1e30


def fill_masks(order_ref, place_ref, ends_ref, long_bias, short_bias):
    key = lax.broadcasted_iota(jnp.int32, (LB, LANES), 0)
    query = lax.broadcasted_iota(jnp.int32, (LB, LANES), 1) & (LB - 1)
    mine = place_ref[0]
    for block in range(N_CTX):
        ahead = order_ref[block] * LB + key <= mine * LB + query
        long_bias[pl.ds(block * LB, LB), :] = jnp.where(ahead, 0.0, NEG)
    key_doc = jnp.zeros((SB, LANES), jnp.int32)
    query_doc = jnp.zeros((SB, LANES), jnp.int32)
    for doc in range(S_DOCS):
        key_doc += (key >= ends_ref[doc]).astype(jnp.int32)
        query_doc += (query >= ends_ref[doc]).astype(jnp.int32)
    short_bias[...] = jnp.where((key_doc == query_doc) & (key <= query), 0.0, NEG)


def head_rows(ref, first, at):
    return jnp.concatenate(
        [ref[first:first + LB, (at + g) * HEAD_SIZE:(at + g + 1) * HEAD_SIZE] for g in range(CHUNK)],
        axis=0,
    )


def probs(keys, q_rows, bias):
    s = lax.dot_general(keys, q_rows, (((1,), (1,)), ((), ())), preferred_element_type=jnp.float32)
    s = s * (SCALE * math.log2(math.e)) + bias
    e = jnp.exp2(s - jnp.max(s, axis=0, keepdims=True))
    return e * (1.0 / jnp.sum(e, axis=0, keepdims=True))


def dvalue_kernel(order_ref, place_ref, ends_ref, q_ref, u_ref, ks_ref, k_ref,
                  dvl_ref, dvs_ref, long_bias, short_bias):
    @pl.when(pl.program_id(0) == 0)
    def _():
        fill_masks(order_ref, place_ref, ends_ref, long_bias, short_bias)

    for first, keys, bias, out in (
        (0, k_ref[...].reshape(N_CTX * LB, HEAD_SIZE), long_bias, dvl_ref),
        (LB, ks_ref[LB:, :], short_bias, dvs_ref),
    ):
        total = None
        for at in range(0, GROUP, CHUNK):
            p = probs(keys, head_rows(q_ref, first, at), bias[...]).astype(jnp.bfloat16)
            part = jnp.dot(p, head_rows(u_ref, first, at), preferred_element_type=jnp.float32)
            total = part if total is None else total + part
        out[...] = total.astype(out.dtype).reshape(out.shape)


def dscore_kernel(order_ref, place_ref, ends_ref, q_ref, u_ref, ks_ref, vs_ref, k_ref, v_ref,
                  dq_ref, dkl_ref, dks_ref, long_bias, short_bias):
    @pl.when(pl.program_id(0) == 0)
    def _():
        fill_masks(order_ref, place_ref, ends_ref, long_bias, short_bias)

    long_shape = (N_CTX * LB, HEAD_SIZE)
    for first, keys, values, bias, out in (
        (0, k_ref[...].reshape(long_shape), v_ref[...].reshape(long_shape), long_bias, dkl_ref),
        (LB, ks_ref[LB:, :], vs_ref[LB:, :], short_bias, dks_ref),
    ):
        total = None
        for at in range(0, GROUP, CHUNK):
            q_rows = head_rows(q_ref, first, at)
            p = probs(keys, q_rows, bias[...])
            dp = lax.dot_general(values, head_rows(u_ref, first, at), (((1,), (1,)), ((), ())),
                                 preferred_element_type=jnp.float32)
            delta = jnp.sum(p * dp, axis=0, keepdims=True)
            ds = (p * (dp - delta)).astype(jnp.bfloat16)
            part = jnp.dot(ds, q_rows, preferred_element_type=jnp.float32)
            total = part if total is None else total + part
            dq = lax.dot_general(ds, keys, (((0,), (0,)), ((), ())),
                                 preferred_element_type=jnp.float32) * SCALE
            for g in range(CHUNK):
                dq_ref[first:first + LB, (at + g) * HEAD_SIZE:(at + g + 1) * HEAD_SIZE] = (
                    dq[g * LB:(g + 1) * LB])
        out[...] = (total * SCALE).astype(out.dtype).reshape(out.shape)


WIDE = GROUP * HEAD_SIZE
WIDTH = KEY_VALUE_HEADS * HEAD_SIZE
TOK = LB + SB


def block(rows, columns):
    return pl.BlockSpec((rows, columns), lambda k, *_: (0, k))


def long_block(at):
    return pl.BlockSpec((N_CTX, LB, HEAD_SIZE), lambda k, *_: (0, at, k))


def scratch():
    return [pltpu.VMEM((N_CTX * LB, LANES), jnp.float32), pltpu.VMEM((SB, LANES), jnp.float32)]


LONG_ROWS = jax.ShapeDtypeStruct((N_CTX, LB, WIDTH), jnp.bfloat16)


def dvalues(scalars, queries, upstream, keys, all_keys):
    return pl.pallas_call(
        dvalue_kernel,
        grid_spec=pltpu.PrefetchScalarGridSpec(
            num_scalar_prefetch=3,
            grid=(KEY_VALUE_HEADS,),
            in_specs=[block(TOK, WIDE), block(TOK, WIDE), block(TOK, HEAD_SIZE), long_block(0)],
            out_specs=[long_block(0), block(SB, HEAD_SIZE)],
            scratch_shapes=scratch(),
        ),
        out_shape=[LONG_ROWS, jax.ShapeDtypeStruct((SB, WIDTH), jnp.bfloat16)],
        compiler_params=pltpu.CompilerParams(vmem_limit_bytes=32 << 20),
        cost_estimate=pl.CostEstimate(flops=700_000_000, bytes_accessed=4 << 20, transcendentals=1 << 20),
    )(*scalars, queries, upstream, keys, all_keys)


def dscores(scalars, queries, upstream, keys, values, all_keys, spread_rows):
    return pl.pallas_call(
        dscore_kernel,
        grid_spec=pltpu.PrefetchScalarGridSpec(
            num_scalar_prefetch=3,
            grid=(KEY_VALUE_HEADS,),
            in_specs=[block(TOK, WIDE), block(TOK, WIDE), block(TOK, HEAD_SIZE), block(TOK, HEAD_SIZE),
                      long_block(0), long_block(TOK // LB)],
            out_specs=[block(TOK, WIDE), long_block(0), block(SB, HEAD_SIZE)],
            scratch_shapes=scratch(),
        ),
        out_shape=[jax.ShapeDtypeStruct((TOK, QUERY_HEADS * HEAD_SIZE), jnp.float32), LONG_ROWS,
                   jax.ShapeDtypeStruct((SB, WIDTH), jnp.float32)],
        compiler_params=pltpu.CompilerParams(vmem_limit_bytes=32 << 20),
        cost_estimate=pl.CostEstimate(flops=1_400_000_000, bytes_accessed=6 << 20, transcendentals=1 << 20),
    )(*scalars, queries, upstream, keys, values, all_keys, spread_rows)


Y_LO, CORES = 2, 2
DP = ("ylo", "z", "core")
CTX = ("yhi", "x")


PIECE = 32
DP_BLOCK = N_CTX * PIECE
TOGETHER = 4


def whole(count=1):
    return [pl.BlockSpec(memory_space=pltpu.VMEM)] * count


def regroup_kernel(me_ref, *refs):
    *block_refs, out_ref = refs
    for member in range(N_CTX):
        out_ref[member] = jnp.concatenate(
            [ref[:, member * PIECE:(member + 1) * PIECE] for ref in block_refs], axis=1)


def regroup(me, tokens):
    rows, width = tokens.shape
    depth = width // (DP_BLOCK * Y_LO * CORES)

    def source(at):
        def index(g, me_ref):
            slot = g * TOGETHER + at
            core, y_lo, z = slot // (Y_LO * depth), slot // depth % Y_LO, slot % depth
            return 0, ((y_lo * depth + z) * CORES + core) ^ me_ref[0]
        return pl.BlockSpec((rows, DP_BLOCK), index)

    return pl.pallas_call(
        regroup_kernel,
        grid_spec=pltpu.PrefetchScalarGridSpec(
            num_scalar_prefetch=1,
            grid=(width // (DP_BLOCK * TOGETHER),),
            in_specs=[source(at) for at in range(TOGETHER)],
            out_specs=pl.BlockSpec((N_CTX, rows, PIECE * TOGETHER), lambda g, *_: (0, 0, g)),
        ),
        out_shape=jax.ShapeDtypeStruct((N_CTX, rows, width // N_CTX), tokens.dtype),
        cost_estimate=pl.CostEstimate(flops=0, bytes_accessed=4 << 20, transcendentals=0),
    )(me[None], *[tokens] * TOGETHER)


def values_kernel(tokens_ref, mine_ref, theirs_ref, dv_ref, out_ref):
    weight = jnp.concatenate([mine_ref[...], theirs_ref[...]], axis=0)
    for member in range(0, N_CTX, 2):
        part = jnp.dot(tokens_ref[member * TOK:(member + 2) * TOK], weight,
                       preferred_element_type=jnp.float32).astype(out_ref.dtype)
        out_ref[member, LB:] = part[:TOK]
        out_ref[member + 1, LB:] = part[TOK:]
    out_ref[:, :LB] = dv_ref[...]


def value_parts(tokens, mine, theirs, dv_all):
    return pl.pallas_call(
        values_kernel,
        in_specs=whole(4),
        out_specs=whole()[0],
        out_shape=jax.ShapeDtypeStruct((N_CTX, LB + TOK, WIDTH), jnp.bfloat16),
        compiler_params=pltpu.CompilerParams(vmem_limit_bytes=32 << 20),
        cost_estimate=pl.CostEstimate(flops=2 * tokens.size * WIDTH, bytes_accessed=6 << 20,
                                      transcendentals=0),
    )(tokens, mine, theirs, dv_all)


def added_up(ref, first, last):
    total = ref[0, first:last].astype(jnp.float32)
    for piece in range(1, ref.shape[0]):
        total += ref[piece, first:last].astype(jnp.float32)
    return total


def middle_kernel(parts_ref, dv_short_ref, out_ref, values_ref):
    values_ref[...] = added_up(parts_ref, LB, LB + TOK).astype(values_ref.dtype)
    dv_long = added_up(parts_ref, 0, LB).astype(out_ref.dtype)
    for member in range(N_CTX):
        out_ref[member, :LB] = dv_long
        out_ref[member, LB:TOK] = dv_short_ref[...]
        out_ref[member, TOK:] = values_ref[:LB]


def middle(parts, dv_short):
    return pl.pallas_call(
        middle_kernel,
        in_specs=whole(2),
        out_specs=whole(2),
        out_shape=[jax.ShapeDtypeStruct(parts.shape, parts.dtype),
                   jax.ShapeDtypeStruct((TOK, WIDTH), jnp.bfloat16)],
        cost_estimate=pl.CostEstimate(flops=parts.size, bytes_accessed=4 * parts.size, transcendentals=0),
    )(parts, dv_short)


def closing_kernel(pieces_ref, dk_ref, out_ref):
    share = added_up(pieces_ref, 0, PIECE).astype(out_ref.dtype)
    for member in range(N_CTX):
        out_ref[member, :PIECE] = share
    out_ref[:, PIECE:] = dk_ref[...]


def closing(pieces, dk_all):
    return pl.pallas_call(
        closing_kernel,
        in_specs=whole(2),
        out_specs=whole()[0],
        out_shape=jax.ShapeDtypeStruct((N_CTX, PIECE + LB, WIDTH), jnp.bfloat16),
        cost_estimate=pl.CostEstimate(flops=pieces.size, bytes_accessed=4 * pieces.size, transcendentals=0),
    )(pieces, dk_all)


def last_kernel(parts_ref, dk_short_ref, dk_ref, grad_ref):
    dk_ref[:LB] = added_up(parts_ref, PIECE, PIECE + LB)
    dk_ref[LB:] = dk_short_ref[...]
    grad_ref[...] = parts_ref[:, :PIECE].astype(grad_ref.dtype).reshape(grad_ref.shape)


def last(parts, dk_short):
    return pl.pallas_call(
        last_kernel,
        in_specs=whole(2),
        out_specs=whole(2),
        out_shape=[jax.ShapeDtypeStruct((TOK, WIDTH), jnp.float32),
                   jax.ShapeDtypeStruct((DP_BLOCK, WIDTH), jnp.float32)],
        cost_estimate=pl.CostEstimate(flops=parts.size, bytes_accessed=4 * parts.size, transcendentals=0),
    )(parts, dk_short)


def weight_kernel(half, me_ref, tokens_ref, d_value_ref, *refs):
    *add_refs, out_ref = refs
    count, rows, columns = out_ref.shape
    some = min(DP_BLOCK // PIECE, count)
    d_value = d_value_ref[:, :TOK].reshape(N_CTX * TOK, columns)
    for first in range(0, count, some):
        at = (half * count + first) * rows
        part = lax.dot_general(
            tokens_ref[:, at:at + some * rows], d_value, (((0,), (0,)), ((), ())),
            preferred_element_type=jnp.float32)
        for slot in range(some):
            block = (first + slot) ^ me_ref[0]
            piece = part[slot * rows:(slot + 1) * rows]
            for ref in add_refs:
                piece += ref[block].astype(jnp.float32)
            out_ref[block] = piece.astype(out_ref.dtype)


def weight_share(half, me, tokens, d_value, *added):
    count, columns = tokens.shape[1] // (CORES * PIECE), WIDTH
    return pl.pallas_call(
        functools.partial(weight_kernel, half),
        in_specs=[pl.BlockSpec(memory_space=pltpu.SMEM)] + whole(2 + len(added)),
        out_specs=whole()[0],
        out_shape=jax.ShapeDtypeStruct((count, PIECE, columns), jnp.bfloat16),
        compiler_params=pltpu.CompilerParams(vmem_limit_bytes=32 << 20),
        cost_estimate=pl.CostEstimate(flops=tokens.size * columns, bytes_accessed=3 << 20,
                                      transcendentals=0),
    )(me[None], tokens, d_value, *added)


def exchange(pieces, axes):
    return lax.all_to_all(pieces, axes, 0, 0, tiled=True)


def spread(piece, axes):
    count = lax.axis_size(axes)
    return exchange(jnp.broadcast_to(piece[None], (count,) + piece.shape), axes)


def swap_along(array, axis, step):
    count = lax.axis_size(axis)
    return lax.ppermute(array, axis, [(i, i ^ step) for i in range(count)])


def after(value, other):
    return lax.optimization_barrier((value, other))[0]


def on_device(tokens, queries, rotated_key_rows, upstream, value_projection_weight, doc_lengths,
              stretch_order):
    member = lax.axis_index(CTX)
    plane = lax.axis_index(("ylo", "z"))
    order = stretch_order[0]
    scalars = (order, lax.dynamic_slice(order, (member,), (1,)), jnp.cumsum(doc_lengths[0]))

    all_keys = spread(rotated_key_rows[:LB], CTX)
    grouped = regroup(plane * CORES + lax.axis_index("core"), tokens)
    grouped, all_keys = lax.optimization_barrier((grouped, all_keys))
    tok = exchange(grouped, CTX).reshape(N_CTX * TOK, -1)
    dv_all, dv_short = dvalues(scalars, queries, upstream, rotated_key_rows, all_keys)

    weight = lax.dynamic_slice_in_dim(value_projection_weight, member * PIECE, PIECE, 0)
    weight = after(weight, grouped)
    step = 1
    while step < lax.axis_size("z"):
        if step == 4:
            weight = after(weight, dv_all)
        weight = jnp.concatenate([weight, swap_along(weight, "z", step)], axis=0)
        step *= 2
    weight = jnp.concatenate([weight, swap_along(weight, "ylo", 1)], axis=0)
    other_weight = swap_along(weight, "core", 1)

    parts = exchange(value_parts(tok, weight, other_weight, dv_all), CTX)
    spread_rows, values = middle(parts, dv_short)
    spread_rows = exchange(spread_rows, CTX)

    share = swap_along(weight_share(1, plane, tok, spread_rows), "core", 1)
    share = weight_share(0, plane, tok, spread_rows, share)
    values = after(values, share)
    share = exchange(share, ("ylo", "z"))
    d_query, dk_all, dk_short = dscores(scalars, queries, upstream, rotated_key_rows, values,
                                        all_keys, spread_rows)
    d_key, weight_grad = last(exchange(closing(share, dk_all), CTX), dk_short)
    return d_query, d_key, weight_grad


def solution(mesh):
    packs = mesh.shape["dp"]
    mesh = Mesh(mesh.devices.reshape(Y_LO, packs // (Y_LO * CORES), CORES, 2, N_CTX // 2), DP + CTX)
    rows = P(DP + CTX, None)
    return jax.shard_map(
        on_device,
        mesh=mesh,
        in_specs=(rows, rows, rows, rows, P(DP, None), rows, P(DP, None)),
        out_specs=(rows, rows, P(DP, None)),
        check_vma=False,
    )
```

time: 200 us -> 172 us (0.86)
  starting transfers between devices: 89.9 us -> 25.6 us
  blocking collectives: 19.2 us -> 74.4 us
  waiting for transfers between devices: 49.4 us -> 23.8 us
  Pallas kernels: 28.3 us -> 33 us
  local copies, waits for them, and re-layouts: 8.9 us -> 13.1 us
    all_to_all x1 -> x3, blocking collectives: 19.2 us -> 74.4 us  [exchange(): return lax.all_to_all(pieces, axes, 0, 0, tiled=True)]
    ppermute x28 -> x0, starting transfers between devices: 54.7 us -> none  [swap(): lax.ppermute(array, CTX, [(i, i ^ step) for i in range(N_CTX)])]
    ppermute x28 -> x0, waiting for transfers between devices: 17.7 us -> none  [swap(): lax.ppermute(array, CTX, [(i, i ^ step) for i in range(N_CTX)])]
    all_to_all x4 -> x3, starting transfers between devices: 24.7 us -> 16.6 us  [exchange(): return lax.all_to_all(pieces, axes, 0, 0, tiled=True)]
    all_to_all x4 -> x3, waiting for transfers between devices: 12.9 us -> 5.06 us  [exchange(): return lax.all_to_all(pieces, axes, 0, 0, tiled=True)]
    unnamed x32 -> x38, local copies, waits for them, and re-layouts: 5.7 us -> 10.7 us
    pallas_call x2 -> x4, Pallas kernels: 3.66 us -> 8.45 us  [the longest x1 2.9 us: middle(): pl.pallas_call(middle_kernel, in_specs=whole(2), out_specs=whole(2), out_...]
  transfers between devices with their start and end apart: 38 -> 9, of which waited for: 15 -> 7; matrix products, arithmetic and copies ran while one was open for 1% -> 1% of each run, Pallas kernels for 8% -> 13%
where the time goes in v2:
time: 172 us; the launch traced here: 171 us
  blocking collectives  74.4 us (43%)
  Pallas kernels  33 us (19%)
  starting transfers between devices  25.6 us (15%)
  waiting for transfers between devices  23.8 us (14%)
  local copies, waits for them, and re-layouts  13.1 us (8%)
    all_to_all x3, blocking collectives, exchange(): return lax.all_to_all(pieces, axes, 0, 0, tiled=True)  74.4 us
    ppermute x6, waiting for transfers between devices, swap_along(): return lax.ppermute(array, axis, [(i, i ^ step) for i in range(count)])  18.8 us
    all_to_all x3, starting transfers between devices, exchange(): return lax.all_to_all(pieces, axes, 0, 0, tiled=True)  16.6 us
    unnamed x38, local copies, waits for them, and re-layouts  10.7 us
    pallas_call x1, Pallas kernels, dscores(): pl.pallas_call(dscore_kernel, grid_spec=pltpu.PrefetchScalarGridSpec(num_...  10.3 us
    ppermute x6, starting transfers between devices, swap_along(): return lax.ppermute(array, axis, [(i, i ^ step) for i in range(count)])  9 us
    pallas_call x1, Pallas kernels, regroup(): pl.pallas_call(regroup_kernel, grid_spec=pltpu.PrefetchScalarGridSpec(num...  6.6 us
    pallas_call x1, Pallas kernels, dvalues(): pl.pallas_call(dvalue_kernel, grid_spec=pltpu.PrefetchScalarGridSpec(num_...  5.31 us
  transfers between devices with their start and end apart: 9, of which 7 were waited for; matrix products, arithmetic and copies ran while one was open for 1% of the time, Pallas kernels for 13%

profile of v2, /device:TPU:32, one launch (start us, length us, event | category | flops | bytes accessed | tf_op | source)
XLA Modules:
  0.0 170.8 jit_solution(5668647802979558234)
XLA Ops:
  0.6 0.0 copy-start
  0.6 0.9 slice.3
  1.5 0.8 broadcast_in_dim.14
  2.4 6.9 %all-to-all-start = ((bf16[8,64,512]{2,1,0:T(8,128)(2,1)}), bf16[8,64,512]{2,1,0:T(8,128)(2,1)S(1)}, u32[]{:S(2)}, u32[]{:S(2)}) async-start(bf16[8,64,512]{2,1,0:T(8,128)(2,1)} %broadcast_in_dim.14), calls=%async_computation | async-start | bytes 1048576 | tf_op jit(solution)/shard_map/all_to_all | solution.py:316
  9.3 6.6 %shard_map.94 = bf16[8,128,1024]{2,1,0:T(8,128)(2,1)} custom-call(s32[1]{0:T(128)} %bitcast.4.me_ref, bf16[128,8192]{1,0:T(8,128)(2,1)} %refs_3_.1, bf16[128,8192]{1,0:T(8,128)(2,1)} %refs_3_.1, bf16[128,8192]{1,0:T(8,128)(2,1)} %refs_3_.1, bf16[128,8192]{1,0:T(8,128)(2,1)} %refs_3_.1), custom_call_target="tpu_custom_call" | custom-call | bytes 4194304 | tf_op jit(solution)/shard_map/pallas_call | solution.py:188
  15.9 0.0 copy-start.17
  15.9 0.0 copy-start.15
  15.9 0.0 copy-start.12
  15.9 5.0 %all-to-all-done.k_ref = bf16[8,64,512]{2,1,0:T(8,128)(2,1)S(1)} async-done(((bf16[8,64,512]{2,1,0:T(8,128)(2,1)}), bf16[8,64,512]{2,1,0:T(8,128)(2,1)S(1)}, u32[]{:S(2)}, u32[]{:S(2)}) %all-to-all-start) | async-done | bytes 524320 | tf_op jit(solution)/shard_map/all_to_all | solution.py:316
  20.9 3.6 %all-to-all-start.1 = ((bf16[8,128,1024]{2,1,0:T(8,128)(2,1)}), bf16[8,128,1024]{2,1,0:T(8,128)(2,1)S(1)}, u32[]{:S(2)}, u32[]{:S(2)}) async-start(bf16[8,128,1024]{2,1,0:T(8,128)(2,1)} %shard_map.94), calls=%async_computation.1 | async-start | bytes 4194304 | tf_op jit(solution)/shard_map/all_to_all | solution.py:316
  24.5 0.0 copy-done
  24.5 0.2 collective-permute-start
  24.7 0.0 copy-done.17
  24.7 0.2 reduce-window.9
  24.9 0.0 copy-done.15
  24.9 0.6 constant_dynamic-slice_fusion.1
  25.6 3.0 %collective-permute-done = bf16[32,512]{1,0:T(8,128)(2,1)S(1)} collective-permute-done((bf16[32,512]{1,0:T(8,128)(2,1)S(1)}, bf16[32,512]{1,0:T(8,128)(2,1)S(1)}, u32[]{:S(2)}, u32[]{:S(2)}) %collective-permute-start) | collective-permute-done | bytes 32800 | tf_op jit(solution)/shard_map/ppermute | solution.py:326
  28.5 3.3 %collective-permute-start.1 = (bf16[64,512]{1,0:T(8,128)(2,1)S(1)}, bf16[64,512]{1,0:T(8,128)(2,1)S(1)}, u32[]{:S(2)}, u32[]{:S(2)}) collective-permute-start(bf16[64,512]{1,0:T(8,128)(2,1)S(1)} %pad_maximum_fusion.2), channel_id=1, source_target_pairs={{0,32},{16,48},{32,0},{48,16},{64,96},{80,112},{96,64},{112,80},{1... | collective-permute-start | bytes 196616 | tf_op jit(solution)/shard_map/ppermute | solution.py:326
  31.8 0.0 copy-done.12
  31.8 0.0 copy-start.3
  31.8 1.2 copy-done.3
  33.0 0.0 copy-start.5
  33.0 1.2 copy-done.5
  34.3 5.3 %shard_map.95 = (bf16[8,64,512]{2,1,0:T(8,128)(2,1)S(1)}, bf16[64,512]{1,0:T(8,128)(2,1)S(1)}) custom-call(s32[8]{0:T(128)S(1)} %bitcast.10, s32[1]{0:T(128)} %bitcast.1.place_ref, s32[4]{0:T(128)S(1)} %bitcast.12, bf16[128,4096]{1,0:T(8,128)(2,1)S(1)} %copy-done.3, bf16[128,4096]{1,0:T(8,128)(2,1)S(1)} %copy-done.5, bf16[128,512]{1,0:T(8,128)(2,1)S(1)} %copy-done.12, ...), custom_call_target="tpu_custom_call" | custom-call | flops 700000000 | bytes 4194304 | tf_op jit(solution)/shard_map/pallas_call | solution.py:123
  39.6 0.0 copy-start.7
  39.6 0.0 copy-start.14
  39.6 0.0 collective-permute-done.1
  39.6 4.6 %collective-permute-start.2 = (bf16[128,512]{1,0:T(8,128)(2,1)S(1)}, bf16[128,512]{1,0:T(8,128)(2,1)S(1)}, u32[]{:S(2)}, u32[]{:S(2)}) collective-permute-start(bf16[128,512]{1,0:T(8,128)(2,1)S(1)} %pad_maximum_fusion.1), channel_id=1, source_target_pairs={{0,64},{16,80},{32,96},{48,112},{64,0},{80,16},{96,32},{112,48},{1... | collective-permute-start | bytes 393224 | tf_op jit(solution)/shard_map/ppermute | solution.py:326
  44.2 5.7 %collective-permute-done.2 = bf16[128,512]{1,0:T(8,128)(2,1)S(1)} collective-permute-done((bf16[128,512]{1,0:T(8,128)(2,1)S(1)}, bf16[128,512]{1,0:T(8,128)(2,1)S(1)}, u32[]{:S(2)}, u32[]{:S(2)}) %collective-permute-start.2) | collective-permute-done | bytes 131104 | tf_op jit(solution)/shard_map/ppermute | solution.py:326
  49.9 0.8 collective-permute-start.3
  50.7 6.3 %collective-permute-done.3 = bf16[256,512]{1,0:T(8,128)(2,1)S(1)} collective-permute-done((bf16[256,512]{1,0:T(8,128)(2,1)S(1)}, bf16[256,512]{1,0:T(8,128)(2,1)S(1)}, u32[]{:S(2)}, u32[]{:S(2)}) %collective-permute-start.3) | collective-permute-done | bytes 262176 | tf_op jit(solution)/shard_map/ppermute | solution.py:326
  57.1 0.1 collective-permute-start.4
  57.2 0.0 copy-done.7
  57.2 0.0 copy-done.14
  57.2 1.9 %collective-permute-done.4.theirs_ref = bf16[512,512]{1,0:T(8,128)(2,1)S(1)} collective-permute-done((bf16[512,512]{1,0:T(8,128)(2,1)S(1)}, bf16[512,512]{1,0:T(8,128)(2,1)S(1)}, u32[]{:S(2)}, u32[]{:S(2)}) %collective-permute-start.4) | collective-permute-done | bytes 524320 | tf_op jit(solution)/shard_map/ppermute | solution.py:326
  59.0 0.0 copy-start.10
  59.1 0.8 copy-done.10
  59.8 0.0 all-to-all-done.1
  59.8 0.0 copy-start.8
  59.8 1.0 copy-done.8
  60.9 1.0 copy-done.11
  61.9 1.3 shard_map.96
  63.2 30.2 %all_to_all.30.parts_ref = bf16[8,192,512]{2,1,0:T(8,128)(2,1)} all-to-all(bf16[8,192,512]{2,1,0:T(8,128)(2,1)S(1)} %shard_map.96), channel_id=1, replica_groups=mesh['ylo'=2,'z'=8,'core'=2,'yhi'=2,'x'=4] {'yhi','x'}, dimensions={0} | all-to-all | bytes 3145728 | tf_op jit(solution)/shard_map/all_to_all | solution.py:316
  93.4 2.9 %shard_map.97 = (bf16[8,192,512]{2,1,0:T(8,128)(2,1)}, bf16[128,512]{1,0:T(8,128)(2,1)}) custom-call(bf16[8,192,512]{2,1,0:T(8,128)(2,1)} %all_to_all.30.parts_ref, bf16[64,512]{1,0:T(8,128)(2,1)} %copy-done.14), custom_call_target="tpu_custom_call" | custom-call | flops 786432 | bytes 3145728 | tf_op jit(solution)/shard_map/pallas_call | solution.py:240
  96.3 25.7 %all_to_all.31.d_value_ref.v_ref = bf16[8,192,512]{2,1,0:T(8,128)(2,1)S(1)} all-to-all(bf16[8,192,512]{2,1,0:T(8,128)(2,1)} %get-tuple-element.24), channel_id=1, replica_groups=mesh['ylo'=2,'z'=8,'core'=2,'yhi'=2,'x'=4] {'yhi','x'}, dimensions={0} | all-to-all | bytes 3145728 | tf_op jit(solution)/shard_map/all_to_all | solution.py:316
  122.0 0.7 shard_map.98
  122.7 0.0 copy-start.16
  122.7 0.1 collective-permute-start.5
  122.8 1.9 %collective-permute-done.5.refs_0_ = bf16[16,32,512]{2,1,0:T(8,128)(2,1)S(1)} collective-permute-done((bf16[16,32,512]{2,1,0:T(8,128)(2,1)S(1)}, bf16[16,32,512]{2,1,0:T(8,128)(2,1)S(1)}, u32[]{:S(2)}, u32[]{:S(2)}) %collective-permute-start.5) | collective-permute-done | bytes 524320 | tf_op jit(solution)/shard_map/ppermute | solution.py:326
  124.7 0.0 copy-done.1
  124.7 1.5 shard_map.99
  126.3 6.0 %all-to-all-start.4 = ((bf16[16,32,512]{2,1,0:T(8,128)(2,1)}), bf16[16,32,512]{2,1,0:T(8,128)(2,1)}, u32[]{:S(2)}, u32[]{:S(2)}) async-start(bf16[16,32,512]{2,1,0:T(8,128)(2,1)} %shard_map.99), calls=%async_computation.4 | async-start | bytes 1048576 | tf_op jit(solution)/shard_map/all_to_all | solution.py:316
  132.3 0.0 copy-done.16
  132.3 0.0 copy-start.2
  132.3 1.4 copy-done.2
  133.7 1.2 copy-done.4
  134.9 1.2 copy-done.6
  136.2 10.3 %shard_map.100 = (f32[128,4096]{1,0:T(8,128)}, bf16[8,64,512]{2,1,0:T(8,128)(2,1)S(1)}, f32[64,512]{1,0:T(8,128)S(1)}) custom-call(s32[8]{0:T(128)S(1)} %bitcast.11, s32[1]{0:T(128)} %bitcast.1.place_ref, s32[4]{0:T(128)S(1)} %bitcast.13, bf16[128,4096]{1,0:T(8,128)(2,1)S(1)} %copy-done.4, bf16[128,4096]{1,0:T(8,128)(2,1)S(1)} %copy-done.6, ...), custom_call_target="tpu_custom_call" | custom-call | flops 1400000000 | bytes 6291456 | tf_op jit(solution)/shard_map/pallas_call | solution.py:139
  146.5 0.8 copy-done.9
  147.3 0.6 copy-done.13
  147.9 0.1 all-to-all-done.4.pieces_ref
  148.0 2.2 %shard_map.101 = bf16[8,96,512]{2,1,0:T(8,128)(2,1)} custom-call(bf16[16,32,512]{2,1,0:T(8,128)(2,1)} %all-to-all-done.4.pieces_ref, bf16[8,64,512]{2,1,0:T(8,128)(2,1)} %copy-done.9), custom_call_target="tpu_custom_call" | custom-call | flops 262144 | bytes 1048576 | tf_op jit(solution)/shard_map/pallas_call | solution.py:258
  150.2 18.5 %all_to_all.32.parts_ref = bf16[8,96,512]{2,1,0:T(8,128)(2,1)} all-to-all(bf16[8,96,512]{2,1,0:T(8,128)(2,1)} %shard_map.101), channel_id=1, replica_groups=mesh['ylo'=2,'z'=8,'core'=2,'yhi'=2,'x'=4] {'yhi','x'}, dimensions={0} | all-to-all | bytes 1572864 | tf_op jit(solution)/shard_map/all_to_all | solution.py:316
  168.7 2.1 %shard_map.102 = (f32[128,512]{1,0:T(8,128)}, f32[256,512]{1,0:T(8,128)}) custom-call(bf16[8,96,512]{2,1,0:T(8,128)(2,1)} %all_to_all.32.parts_ref, f32[64,512]{1,0:T(8,128)} %copy-done.13), custom_call_target="tpu_custom_call" | custom-call | flops 393216 | bytes 1572864 | tf_op jit(solution)/shard_map/pallas_call | solution.py:274
  (13 shorter events, 0.1 us)
Async XLA Ops:
  0.6 23.9 %copy-start = (bf16[256,512]{1,0:T(8,128)(2,1)S(1)}, bf16[256,512]{1,0:T(8,128)(2,1)}, u32[]{:S(2)}) copy-start(bf16[256,512]{1,0:T(8,128)(2,1)} %param.11) | copy-start | bytes 786436
  2.4 18.5 %all-to-all-start = ((bf16[8,64,512]{2,1,0:T(8,128)(2,1)}), bf16[8,64,512]{2,1,0:T(8,128)(2,1)S(1)}, u32[]{:S(2)}, u32[]{:S(2)}) async-start(bf16[8,64,512]{2,1,0:T(8,128)(2,1)} %broadcast_in_dim.14), calls=%async_computation | async-start | bytes 1048576 | tf_op jit(solution)/shard_map/all_to_all | solution.py:316
  15.9 8.8 %copy-start.17 = (s32[1,4]{1,0:T(1,128)S(1)}, s32[1,4]{1,0:T(1,128)}, u32[]{:S(2)}) copy-start(s32[1,4]{1,0:T(1,128)} %param.12) | copy-start | bytes 52
  15.9 9.0 %copy-start.15 = (s32[1,8]{1,0:T(1,128)S(1)}, s32[1,8]{1,0:T(1,128)}, u32[]{:S(2)}) copy-start(s32[1,8]{1,0:T(1,128)} %param.13) | copy-start | bytes 100
  15.9 15.9 %copy-start.12 = (bf16[128,512]{1,0:T(8,128)(2,1)S(1)}, bf16[128,512]{1,0:T(8,128)(2,1)}, u32[]{:S(2)}) copy-start(bf16[128,512]{1,0:T(8,128)(2,1)} %ks_ref.3) | copy-start | bytes 393220
  20.9 39.0 %all-to-all-start.1 = ((bf16[8,128,1024]{2,1,0:T(8,128)(2,1)}), bf16[8,128,1024]{2,1,0:T(8,128)(2,1)S(1)}, u32[]{:S(2)}, u32[]{:S(2)}) async-start(bf16[8,128,1024]{2,1,0:T(8,128)(2,1)} %shard_map.94), calls=%async_computation.1 | async-start | bytes 4194304 | tf_op jit(solution)/shard_map/all_to_all | solution.py:316
  24.5 4.0 %collective-permute-start = (bf16[32,512]{1,0:T(8,128)(2,1)S(1)}, bf16[32,512]{1,0:T(8,128)(2,1)S(1)}, u32[]{:S(2)}, u32[]{:S(2)}) collective-permute-start(bf16[32,512]{1,0:T(8,128)(2,1)S(1)} %constant_dynamic-slice_fusion), channel_id=1, source_target_pairs={{0,16},{16,0},{32,48},{48,32},{64,80},{80,64},{96,112},{112,96},{1... | collective-permute-start | bytes 98312 | tf_op jit(solution)/shard_map/ppermute | solution.py:326
  28.5 11.1 %collective-permute-start.1 = (bf16[64,512]{1,0:T(8,128)(2,1)S(1)}, bf16[64,512]{1,0:T(8,128)(2,1)S(1)}, u32[]{:S(2)}, u32[]{:S(2)}) collective-permute-start(bf16[64,512]{1,0:T(8,128)(2,1)S(1)} %pad_maximum_fusion.2), channel_id=1, source_target_pairs={{0,32},{16,48},{32,0},{48,16},{64,96},{80,112},{96,64},{112,80},{1... | collective-permute-start | bytes 196616 | tf_op jit(solution)/shard_map/ppermute | solution.py:326
  31.8 1.2 copy-start.3
  33.0 1.2 copy-start.5
  39.6 17.6 %copy-start.7 = (bf16[8,64,512]{2,1,0:T(8,128)(2,1)}, bf16[8,64,512]{2,1,0:T(8,128)(2,1)S(1)}, u32[]{:S(2)}) copy-start(bf16[8,64,512]{2,1,0:T(8,128)(2,1)S(1)} %get-tuple-element.20.dv_ref) | copy-start | bytes 1572868
  39.6 17.6 %copy-start.14 = (bf16[64,512]{1,0:T(8,128)(2,1)}, bf16[64,512]{1,0:T(8,128)(2,1)S(1)}, u32[]{:S(2)}) copy-start(bf16[64,512]{1,0:T(8,128)(2,1)S(1)} %get-tuple-element.22.dv_short_ref) | copy-start | bytes 196612
  39.6 10.3 %collective-permute-start.2 = (bf16[128,512]{1,0:T(8,128)(2,1)S(1)}, bf16[128,512]{1,0:T(8,128)(2,1)S(1)}, u32[]{:S(2)}, u32[]{:S(2)}) collective-permute-start(bf16[128,512]{1,0:T(8,128)(2,1)S(1)} %pad_maximum_fusion.1), channel_id=1, source_target_pairs={{0,64},{16,80},{32,96},{48,112},{64,0},{80,16},{96,32},{112,48},{1... | collective-permute-start | bytes 393224 | tf_op jit(solution)/shard_map/ppermute | solution.py:326
  49.9 7.1 %collective-permute-start.3 = (bf16[256,512]{1,0:T(8,128)(2,1)S(1)}, bf16[256,512]{1,0:T(8,128)(2,1)S(1)}, u32[]{:S(2)}, u32[]{:S(2)}) collective-permute-start(bf16[256,512]{1,0:T(8,128)(2,1)S(1)} %pad_maximum_fusion), channel_id=1, source_target_pairs={{0,128},{128,0},{1,129},{129,1},{2,130},{130,2},{3,131},{131,3},{4... | collective-permute-start | bytes 786440 | tf_op jit(solution)/shard_map/ppermute | solution.py:326
  57.1 2.0 %collective-permute-start.4 = (bf16[512,512]{1,0:T(8,128)(2,1)S(1)}, bf16[512,512]{1,0:T(8,128)(2,1)S(1)}, u32[]{:S(2)}, u32[]{:S(2)}) collective-permute-start(bf16[512,512]{1,0:T(8,128)(2,1)S(1)} %constant_dynamic-update-slice_fusion.mine_ref), channel_id=1, source_target_pairs={{0,8},{8,0},{1,9},{9,1},{2,10},{10,2},{3,11},{11,3},{4,12},{12,4},... | collective-permute-start | bytes 1572872 | tf_op jit(solution)/shard_map/ppermute | solution.py:326
  59.0 0.8 copy-start.10
  59.8 1.0 copy-start.8
  60.9 1.0 copy-start.11
  122.0 2.8 %copy-start.1 = (bf16[8,192,512]{2,1,0:T(8,128)(2,1)}, bf16[8,192,512]{2,1,0:T(8,128)(2,1)S(1)}, u32[]{:S(2)}) copy-start(bf16[8,192,512]{2,1,0:T(8,128)(2,1)S(1)} %all_to_all.31.d_value_ref.v_ref) | copy-start | bytes 4718596
  122.7 9.6 %copy-start.16 = (bf16[128,512]{1,0:T(8,128)(2,1)S(1)}, bf16[128,512]{1,0:T(8,128)(2,1)}, u32[]{:S(2)}) copy-start(bf16[128,512]{1,0:T(8,128)(2,1)} %get-tuple-element.25.vs_ref) | copy-start | bytes 393220
  122.7 2.0 %collective-permute-start.5 = (bf16[16,32,512]{2,1,0:T(8,128)(2,1)S(1)}, bf16[16,32,512]{2,1,0:T(8,128)(2,1)S(1)}, u32[]{:S(2)}, u32[]{:S(2)}) collective-permute-start(bf16[16,32,512]{2,1,0:T(8,128)(2,1)S(1)} %shard_map.98), channel_id=1, source_target_pairs={{0,8},{8,0},{1,9},{9,1},{2,10},{10,2},{3,11},{11,3},{4,12},{12,4},... | collective-permute-start | bytes 1572872 | tf_op jit(solution)/shard_map/ppermute | solution.py:326
  126.3 21.7 %all-to-all-start.4 = ((bf16[16,32,512]{2,1,0:T(8,128)(2,1)}), bf16[16,32,512]{2,1,0:T(8,128)(2,1)}, u32[]{:S(2)}, u32[]{:S(2)}) async-start(bf16[16,32,512]{2,1,0:T(8,128)(2,1)} %shard_map.99), calls=%async_computation.4 | async-start | bytes 1048576 | tf_op jit(solution)/shard_map/all_to_all | solution.py:316
  132.3 1.4 copy-start.2
  133.7 1.2 copy-start.4
  134.9 1.2 copy-start.6
  146.5 0.8 copy-start.9
  147.3 0.6 copy-start.13

commit v3 on v2

--- a/solution.py
+++ b/solution.py
@@ -30,6 +30,12 @@
     for block in range(N_CTX):
         ahead = order_ref[block] * LB + key <= mine * LB + query
         long_bias[pl.ds(block * LB, LB), :] = jnp.where(ahead, 0.0, NEG)
+    fill_short_mask(ends_ref, short_bias)
+
+
+def fill_short_mask(ends_ref, short_bias):
+    key = lax.broadcasted_iota(jnp.int32, (SB, LANES), 0)
+    query = lax.broadcasted_iota(jnp.int32, (SB, LANES), 1) & (LB - 1)
     key_doc = jnp.zeros((SB, LANES), jnp.int32)
     query_doc = jnp.zeros((SB, LANES), jnp.int32)
     for doc in range(S_DOCS):
@@ -52,26 +58,66 @@
     return e * (1.0 / jnp.sum(e, axis=0, keepdims=True))
 
 
-def dvalue_kernel(order_ref, place_ref, ends_ref, q_ref, u_ref, ks_ref, k_ref,
-                  dvl_ref, dvs_ref, long_bias, short_bias):
+def fetch(sources, buffers, sems):
+    def copy(at, head):
+        source, rows, lanes = sources[at]
+        return pltpu.make_async_copy(
+            source.at[rows + (pl.ds(pl.multiple_of(head * lanes, lanes), lanes),)],
+            buffers[at].at[head], sems.at[at, head])
+
+    step = pl.program_id(0)
+
+    @pl.when(step == 0)
+    def _():
+        for head in range(KEY_VALUE_HEADS):
+            for at in range(len(sources)):
+                copy(at, head).start()
+
+    for at in range(len(sources)):
+        copy(at, step).wait()
+    return [buffer.at[step] for buffer in buffers]
+
+
+ALL = slice(None)
+
+
+def short_dvalue_kernel(ends_ref, q_ref, u_ref, ks_ref, out_ref, short_bias):
+    @pl.when(pl.program_id(0) == 0)
+    def _():
+        fill_short_mask(ends_ref, short_bias)
+
+    total = None
+    for at in range(0, GROUP, CHUNK):
+        p = probs(ks_ref[...], head_rows(q_ref, 0, at), short_bias[...]).astype(jnp.bfloat16)
+        part = jnp.dot(p, head_rows(u_ref, 0, at), preferred_element_type=jnp.float32)
+        total = part if total is None else total + part
+    out_ref[...] = total.astype(out_ref.dtype)
+
+
+def dvalue_kernel(order_ref, place_ref, ends_ref, q_hbm, u_hbm, k_ref, dvl_ref,
+                  long_bias, short_bias, q_buffer, u_buffer, sems):
+    rows = (pl.ds(0, LB),)
+    q_ref, u_ref = fetch([(q_hbm, rows, WIDE), (u_hbm, rows, WIDE)], [q_buffer, u_buffer], sems)
+
     @pl.when(pl.program_id(0) == 0)
     def _():
         fill_masks(order_ref, place_ref, ends_ref, long_bias, short_bias)
 
-    for first, keys, bias, out in (
-        (0, k_ref[...].reshape(N_CTX * LB, HEAD_SIZE), long_bias, dvl_ref),
-        (LB, ks_ref[LB:, :], short_bias, dvs_ref),
-    ):
-        total = None
-        for at in range(0, GROUP, CHUNK):
-            p = probs(keys, head_rows(q_ref, first, at), bias[...]).astype(jnp.bfloat16)
-            part = jnp.dot(p, head_rows(u_ref, first, at), preferred_element_type=jnp.float32)
-            total = part if total is None else total + part
-        out[...] = total.astype(out.dtype).reshape(out.shape)
-
-
-def dscore_kernel(order_ref, place_ref, ends_ref, q_ref, u_ref, ks_ref, vs_ref, k_ref, v_ref,
-                  dq_ref, dkl_ref, dks_ref, long_bias, short_bias):
+    keys = k_ref[...].reshape(N_CTX * LB, HEAD_SIZE)
+    total = None
+    for at in range(0, GROUP, CHUNK):
+        p = probs(keys, head_rows(q_ref, 0, at), long_bias[...]).astype(jnp.bfloat16)
+        part = jnp.dot(p, head_rows(u_ref, 0, at), preferred_element_type=jnp.float32)
+        total = part if total is None else total + part
+    dvl_ref[...] = total.astype(dvl_ref.dtype).reshape(dvl_ref.shape)
+
+
+def dscore_kernel(order_ref, place_ref, ends_ref, q_hbm, u_hbm, ks_ref, vs_ref, k_ref, v_hbm,
+                  dq_ref, dkl_ref, dks_ref, long_bias, short_bias, q_buffer, u_buffer, v_buffer, sems):
+    q_ref, u_ref, v_ref = fetch(
+        [(q_hbm, (ALL,), WIDE), (u_hbm, (ALL,), WIDE), (v_hbm, (ALL, pl.ds(LB, LB)), HEAD_SIZE)],
+        [q_buffer, u_buffer, v_buffer], sems)
+
     @pl.when(pl.program_id(0) == 0)
     def _():
         fill_masks(order_ref, place_ref, ends_ref, long_bias, short_bias)
@@ -102,6 +148,7 @@
 WIDE = GROUP * HEAD_SIZE
 WIDTH = KEY_VALUE_HEADS * HEAD_SIZE
 TOK = LB + SB
+SHORT_ROWS = KEY_VALUE_HEADS * SB
 
 
 def block(rows, columns):
@@ -112,27 +159,51 @@
     return pl.BlockSpec((N_CTX, LB, HEAD_SIZE), lambda k, *_: (0, at, k))
 
 
-def scratch():
-    return [pltpu.VMEM((N_CTX * LB, LANES), jnp.float32), pltpu.VMEM((SB, LANES), jnp.float32)]
+def scratch(*fetched):
+    return [pltpu.VMEM((N_CTX * LB, LANES), jnp.float32), pltpu.VMEM((SB, LANES), jnp.float32)] + [
+        pltpu.VMEM((KEY_VALUE_HEADS,) + shape, jnp.bfloat16) for shape in fetched
+    ] + [pltpu.SemaphoreType.DMA((len(fetched), KEY_VALUE_HEADS))]
+
+
+ELSEWHERE = pl.BlockSpec(memory_space=pltpu.HBM)
 
 
 LONG_ROWS = jax.ShapeDtypeStruct((N_CTX, LB, WIDTH), jnp.bfloat16)
 
 
-def dvalues(scalars, queries, upstream, keys, all_keys):
+def short_dvalues(ends, queries, upstream, keys):
+    def rows(columns):
+        return pl.BlockSpec((SB, columns), lambda k, *_: (1, k))
+
+    return pl.pallas_call(
+        short_dvalue_kernel,
+        grid_spec=pltpu.PrefetchScalarGridSpec(
+            num_scalar_prefetch=1,
+            grid=(KEY_VALUE_HEADS,),
+            in_specs=[rows(WIDE), rows(WIDE), rows(HEAD_SIZE)],
+            out_specs=pl.BlockSpec((SB, HEAD_SIZE), lambda k, *_: (k, 0)),
+            scratch_shapes=[pltpu.VMEM((SB, LANES), jnp.float32)],
+        ),
+        out_shape=jax.ShapeDtypeStruct((SHORT_ROWS, HEAD_SIZE), jnp.bfloat16),
+        compiler_params=pltpu.CompilerParams(vmem_limit_bytes=16 << 20),
+        cost_estimate=pl.CostEstimate(flops=70_000_000, bytes_accessed=1 << 20, transcendentals=1 << 17),
+    )(ends, queries, upstream, keys)
+
+
+def dvalues(scalars, queries, upstream, all_keys):
     return pl.pallas_call(
         dvalue_kernel,
         grid_spec=pltpu.PrefetchScalarGridSpec(
             num_scalar_prefetch=3,
             grid=(KEY_VALUE_HEADS,),
-            in_specs=[block(TOK, WIDE), block(TOK, WIDE), block(TOK, HEAD_SIZE), long_block(0)],
-            out_specs=[long_block(0), block(SB, HEAD_SIZE)],
-            scratch_shapes=scratch(),
+            in_specs=[ELSEWHERE, ELSEWHERE, long_block(0)],
+            out_specs=long_block(0),
+            scratch_shapes=scratch((LB, WIDE), (LB, WIDE)),
         ),
-        out_shape=[LONG_ROWS, jax.ShapeDtypeStruct((SB, WIDTH), jnp.bfloat16)],
-        compiler_params=pltpu.CompilerParams(vmem_limit_bytes=32 << 20),
-        cost_estimate=pl.CostEstimate(flops=700_000_000, bytes_accessed=4 << 20, transcendentals=1 << 20),
-    )(*scalars, queries, upstream, keys, all_keys)
+        out_shape=LONG_ROWS,
+        compiler_params=pltpu.CompilerParams(vmem_limit_bytes=16 << 20),
+        cost_estimate=pl.CostEstimate(flops=600_000_000, bytes_accessed=4 << 20, transcendentals=1 << 20),
+    )(*scalars, queries, upstream, all_keys)
 
 
 def dscores(scalars, queries, upstream, keys, values, all_keys, spread_rows):
@@ -141,14 +212,14 @@
         grid_spec=pltpu.PrefetchScalarGridSpec(
             num_scalar_prefetch=3,
             grid=(KEY_VALUE_HEADS,),
-            in_specs=[block(TOK, WIDE), block(TOK, WIDE), block(TOK, HEAD_SIZE), block(TOK, HEAD_SIZE),
-                      long_block(0), long_block(TOK // LB)],
+            in_specs=[ELSEWHERE, ELSEWHERE, block(TOK, HEAD_SIZE), block(TOK, HEAD_SIZE),
+                      long_block(0), ELSEWHERE],
             out_specs=[block(TOK, WIDE), long_block(0), block(SB, HEAD_SIZE)],
-            scratch_shapes=scratch(),
+            scratch_shapes=scratch((TOK, WIDE), (TOK, WIDE), (N_CTX, LB, HEAD_SIZE)),
         ),
         out_shape=[jax.ShapeDtypeStruct((TOK, QUERY_HEADS * HEAD_SIZE), jnp.float32), LONG_ROWS,
                    jax.ShapeDtypeStruct((SB, WIDTH), jnp.float32)],
-        compiler_params=pltpu.CompilerParams(vmem_limit_bytes=32 << 20),
+        compiler_params=pltpu.CompilerParams(vmem_limit_bytes=60 << 20),
         cost_estimate=pl.CostEstimate(flops=1_400_000_000, bytes_accessed=6 << 20, transcendentals=1 << 20),
     )(*scalars, queries, upstream, keys, values, all_keys, spread_rows)
 
@@ -168,20 +239,41 @@
 
 
 def regroup_kernel(me_ref, *refs):
-    *block_refs, out_ref = refs
+    *block_refs, short_ref, out_ref = refs
+    rows = block_refs[0].shape[0]
     for member in range(N_CTX):
-        out_ref[member] = jnp.concatenate(
+        out_ref[member, rows:] = short_ref[...]
+        out_ref[member, :rows] = jnp.concatenate(
             [ref[:, member * PIECE:(member + 1) * PIECE] for ref in block_refs], axis=1)
 
 
-def regroup(me, tokens):
+def turned(slot, depth):
+    z, bits = 0, depth.bit_length() - 1
+    for bit in range(bits):
+        z = z + ((slot >> bit) & 1) * (1 << (bits - 1 - bit))
+    return z
+
+
+def short_rows(ref, member, head):
+    step = SHORT_ROWS // (ref.shape[2] // HEAD_SIZE)
+    if step >= SB:
+        g, at = divmod(head * SB, step)
+        return ref[member, TOK + at:TOK + at + SB, g * HEAD_SIZE:(g + 1) * HEAD_SIZE]
+    return jnp.concatenate(
+        [ref[member, TOK:TOK + step, g * HEAD_SIZE:(g + 1) * HEAD_SIZE]
+         for g in range(head * SB // step, (head + 1) * SB // step)], axis=0)
+
+
+def regroup(me, tokens, dv_short):
     rows, width = tokens.shape
     depth = width // (DP_BLOCK * Y_LO * CORES)
+    steps = width // (DP_BLOCK * TOGETHER)
+    extra = SHORT_ROWS // steps
 
     def source(at):
         def index(g, me_ref):
             slot = g * TOGETHER + at
-            core, y_lo, z = slot // (Y_LO * depth), slot // depth % Y_LO, slot % depth
+            core, y_lo, z = slot // (Y_LO * depth), slot // depth % Y_LO, turned(slot % depth, depth)
             return 0, ((y_lo * depth + z) * CORES + core) ^ me_ref[0]
         return pl.BlockSpec((rows, DP_BLOCK), index)
 
@@ -189,20 +281,21 @@
         regroup_kernel,
         grid_spec=pltpu.PrefetchScalarGridSpec(
             num_scalar_prefetch=1,
-            grid=(width // (DP_BLOCK * TOGETHER),),
-            in_specs=[source(at) for at in range(TOGETHER)],
-            out_specs=pl.BlockSpec((N_CTX, rows, PIECE * TOGETHER), lambda g, *_: (0, 0, g)),
+            grid=(steps,),
+            in_specs=[source(at) for at in range(TOGETHER)]
+            + [pl.BlockSpec((extra, HEAD_SIZE), lambda g, *_: (g, 0))],
+            out_specs=pl.BlockSpec((N_CTX, rows + extra, PIECE * TOGETHER), lambda g, *_: (0, 0, g)),
         ),
-        out_shape=jax.ShapeDtypeStruct((N_CTX, rows, width // N_CTX), tokens.dtype),
+        out_shape=jax.ShapeDtypeStruct((N_CTX, rows + extra, width // N_CTX), tokens.dtype),
         cost_estimate=pl.CostEstimate(flops=0, bytes_accessed=4 << 20, transcendentals=0),
-    )(me[None], *[tokens] * TOGETHER)
+    )(me[None], *[tokens] * TOGETHER, dv_short)
 
 
 def values_kernel(tokens_ref, mine_ref, theirs_ref, dv_ref, out_ref):
     weight = jnp.concatenate([mine_ref[...], theirs_ref[...]], axis=0)
     for member in range(0, N_CTX, 2):
-        part = jnp.dot(tokens_ref[member * TOK:(member + 2) * TOK], weight,
-                       preferred_element_type=jnp.float32).astype(out_ref.dtype)
+        both = jnp.concatenate([tokens_ref[member, :TOK], tokens_ref[member + 1, :TOK]], axis=0)
+        part = jnp.dot(both, weight, preferred_element_type=jnp.float32).astype(out_ref.dtype)
         out_ref[member, LB:] = part[:TOK]
         out_ref[member + 1, LB:] = part[TOK:]
     out_ref[:, :LB] = dv_ref[...]
@@ -214,7 +307,7 @@
         in_specs=whole(4),
         out_specs=whole()[0],
         out_shape=jax.ShapeDtypeStruct((N_CTX, LB + TOK, WIDTH), jnp.bfloat16),
-        compiler_params=pltpu.CompilerParams(vmem_limit_bytes=32 << 20),
+        compiler_params=pltpu.CompilerParams(vmem_limit_bytes=16 << 20),
         cost_estimate=pl.CostEstimate(flops=2 * tokens.size * WIDTH, bytes_accessed=6 << 20,
                                       transcendentals=0),
     )(tokens, mine, theirs, dv_all)
@@ -227,24 +320,23 @@
     return total
 
 
-def middle_kernel(parts_ref, dv_short_ref, out_ref, values_ref):
+def middle_kernel(parts_ref, out_ref, values_ref):
     values_ref[...] = added_up(parts_ref, LB, LB + TOK).astype(values_ref.dtype)
     dv_long = added_up(parts_ref, 0, LB).astype(out_ref.dtype)
     for member in range(N_CTX):
         out_ref[member, :LB] = dv_long
-        out_ref[member, LB:TOK] = dv_short_ref[...]
-        out_ref[member, TOK:] = values_ref[:LB]
-
-
-def middle(parts, dv_short):
+        out_ref[member, LB:] = values_ref[:LB]
+
+
+def middle(parts):
     return pl.pallas_call(
         middle_kernel,
-        in_specs=whole(2),
+        in_specs=whole(1),
         out_specs=whole(2),
-        out_shape=[jax.ShapeDtypeStruct(parts.shape, parts.dtype),
+        out_shape=[jax.ShapeDtypeStruct((N_CTX, 2 * LB, WIDTH), parts.dtype),
                    jax.ShapeDtypeStruct((TOK, WIDTH), jnp.bfloat16)],
         cost_estimate=pl.CostEstimate(flops=parts.size, bytes_accessed=4 * parts.size, transcendentals=0),
-    )(parts, dv_short)
+    )(parts)
 
 
 def closing_kernel(pieces_ref, dk_ref, out_ref):
@@ -285,14 +377,20 @@
     *add_refs, out_ref = refs
     count, rows, columns = out_ref.shape
     some = min(DP_BLOCK // PIECE, count)
-    d_value = d_value_ref[:, :TOK].reshape(N_CTX * TOK, columns)
+    d_value = jnp.concatenate(
+        [rows for member in range(N_CTX) for rows in (
+            d_value_ref[member, :LB],
+            jnp.concatenate([short_rows(tokens_ref, member, head) for head in range(KEY_VALUE_HEADS)], axis=1),
+        )], axis=0)
     for first in range(0, count, some):
         at = (half * count + first) * rows
         part = lax.dot_general(
-            tokens_ref[:, at:at + some * rows], d_value, (((0,), (0,)), ((), ())),
+            tokens_ref[:, :TOK, at:at + some * rows].reshape(N_CTX * TOK, some * rows), d_value, (((0,), (0,)), ((), ())),
             preferred_element_type=jnp.float32)
         for slot in range(some):
-            block = (first + slot) ^ me_ref[0]
+            depth = count // Y_LO
+            y_lo, z = divmod(first + slot, depth)
+            block = (y_lo * depth + turned(z, depth)) ^ me_ref[0]
             piece = part[slot * rows:(slot + 1) * rows]
             for ref in add_refs:
                 piece += ref[block].astype(jnp.float32)
@@ -300,13 +398,13 @@
 
 
 def weight_share(half, me, tokens, d_value, *added):
-    count, columns = tokens.shape[1] // (CORES * PIECE), WIDTH
+    count, columns = tokens.shape[2] // (CORES * PIECE), WIDTH
     return pl.pallas_call(
         functools.partial(weight_kernel, half),
         in_specs=[pl.BlockSpec(memory_space=pltpu.SMEM)] + whole(2 + len(added)),
         out_specs=whole()[0],
         out_shape=jax.ShapeDtypeStruct((count, PIECE, columns), jnp.bfloat16),
-        compiler_params=pltpu.CompilerParams(vmem_limit_bytes=32 << 20),
+        compiler_params=pltpu.CompilerParams(vmem_limit_bytes=16 << 20),
         cost_estimate=pl.CostEstimate(flops=tokens.size * columns, bytes_accessed=3 << 20,
                                       transcendentals=0),
     )(me[None], tokens, d_value, *added)
@@ -338,24 +436,24 @@
     scalars = (order, lax.dynamic_slice(order, (member,), (1,)), jnp.cumsum(doc_lengths[0]))
 
     all_keys = spread(rotated_key_rows[:LB], CTX)
-    grouped = regroup(plane * CORES + lax.axis_index("core"), tokens)
+    dv_short = short_dvalues(scalars[2], queries, upstream, rotated_key_rows)
+    grouped = regroup(plane * CORES + lax.axis_index("core"), tokens, dv_short)
     grouped, all_keys = lax.optimization_barrier((grouped, all_keys))
-    tok = exchange(grouped, CTX).reshape(N_CTX * TOK, -1)
-    dv_all, dv_short = dvalues(scalars, queries, upstream, rotated_key_rows, all_keys)
+    tok = exchange(grouped, CTX)
 
     weight = lax.dynamic_slice_in_dim(value_projection_weight, member * PIECE, PIECE, 0)
     weight = after(weight, grouped)
-    step = 1
-    while step < lax.axis_size("z"):
-        if step == 4:
-            weight = after(weight, dv_all)
-        weight = jnp.concatenate([weight, swap_along(weight, "z", step)], axis=0)
-        step *= 2
+    depth = lax.axis_size("z")
+    far = [turned(slot, depth) for slot in range(depth // 2)]
+    weight = jnp.concatenate([weight] + [swap_along(weight, "z", step) for step in far[1:]], axis=0)
+    if depth > 1:
+        weight = jnp.concatenate([weight, swap_along(weight, "z", 1)], axis=0)
+    dv_all = dvalues(scalars, queries, upstream, after(all_keys, weight))
     weight = jnp.concatenate([weight, swap_along(weight, "ylo", 1)], axis=0)
-    other_weight = swap_along(weight, "core", 1)
+    other_weight = swap_along(after(weight, dv_all), "core", 1)
 
     parts = exchange(value_parts(tok, weight, other_weight, dv_all), CTX)
-    spread_rows, values = middle(parts, dv_short)
+    spread_rows, values = middle(parts)
     spread_rows = exchange(spread_rows, CTX)
 
     share = swap_along(weight_share(1, plane, tok, spread_rows), "core", 1)

time: 172 us -> 177 us (1.029)
  starting transfers between devices: 25.6 us -> 32.7 us
  blocking collectives: 74.4 us -> 68.2 us
  Pallas kernels: 33 us -> 38.2 us
  waiting for transfers between devices: 23.8 us -> 20.4 us
    all_to_all x3, blocking collectives: 74.4 us -> 68.2 us  [exchange(): return lax.all_to_all(pieces, axes, 0, 0, tiled=True)]
    all_to_all x3, starting transfers between devices: 16.6 us -> 22.7 us  [exchange(): return lax.all_to_all(pieces, axes, 0, 0, tiled=True)]
    pallas_call x1 -> x2, Pallas kernels: 2.9 us -> 4.87 us  [the longest x1 2.69 us: middle(): pl.pallas_call(middle_kernel, in_specs=whole(1), out_specs=whole(2), out_...]
    pallas_call x1, Pallas kernels: 10.3 us -> 12.2 us  [dscores(): pl.pallas_call(dscore_kernel, grid_spec=pltpu.PrefetchScalarGridSpec(num_...]
    ppermute x6 -> x7, waiting for transfers between devices: 18.8 us -> 16.9 us  [swap_along(): return lax.ppermute(array, axis, [(i, i ^ step) for i in range(count)])]
    unnamed x38 -> x32, local copies, waits for them, and re-layouts: 10.7 us -> 9.63 us
    ppermute x6 -> x7, starting transfers between devices: 9 us -> 9.93 us  [swap_along(): return lax.ppermute(array, axis, [(i, i ^ step) for i in range(count)])]
  transfers between devices with their start and end apart: 9 -> 10, of which waited for: 7 -> 7; matrix products, arithmetic and copies ran while one was open for 1% -> 4% of each run, Pallas kernels for 13% -> 15%
where the time goes in v3:
time: 177 us; the launch traced here: 175 us
  blocking collectives  68.2 us (39%)
  Pallas kernels  38.2 us (22%)
  starting transfers between devices  32.7 us (18%)
  waiting for transfers between devices  20.4 us (12%)
  local copies, waits for them, and re-layouts  14.4 us (8%)
    all_to_all x3, blocking collectives, exchange(): return lax.all_to_all(pieces, axes, 0, 0, tiled=True)  68.2 us
    all_to_all x3, starting transfers between devices, exchange(): return lax.all_to_all(pieces, axes, 0, 0, tiled=True)  22.7 us
    ppermute x7, waiting for transfers between devices, swap_along(): return lax.ppermute(array, axis, [(i, i ^ step) for i in range(count)])  16.9 us
    pallas_call x1, Pallas kernels, dscores(): pl.pallas_call(dscore_kernel, grid_spec=pltpu.PrefetchScalarGridSpec(num_...  12.2 us
    ppermute x7, starting transfers between devices, swap_along(): return lax.ppermute(array, axis, [(i, i ^ step) for i in range(count)])  9.93 us
    unnamed x32, local copies, waits for them, and re-layouts  9.63 us
    pallas_call x1, Pallas kernels, regroup(): pl.pallas_call(regroup_kernel, grid_spec=pltpu.PrefetchScalarGridSpec(num...  6.78 us
    pallas_call x1, Pallas kernels, dvalues(): pl.pallas_call(dvalue_kernel, grid_spec=pltpu.PrefetchScalarGridSpec(num_...  5.42 us
  transfers between devices with their start and end apart: 10, of which 7 were waited for; matrix products, arithmetic and copies ran while one was open for 4% of the time, Pallas kernels for 15%

profile of v3, /device:TPU:32, one launch (start us, length us, event | category | flops | bytes accessed | tf_op | source)
XLA Modules:
  0.0 175.4 jit_solution(1512074916659777994)
XLA Ops:
  0.6 0.0 copy-start
  0.6 0.0 copy-start.2
  0.7 0.9 slice.3
  1.6 0.8 broadcast_in_dim.14
  2.4 6.9 %all-to-all-start = ((bf16[8,64,512]{2,1,0:T(8,128)(2,1)}), bf16[8,64,512]{2,1,0:T(8,128)(2,1)S(1)}, u32[]{:S(2)}, u32[]{:S(2)}) async-start(bf16[8,64,512]{2,1,0:T(8,128)(2,1)} %broadcast_in_dim.14), calls=%async_computation | async-start | bytes 1048576 | tf_op jit(solution)/shard_map/all_to_all | solution.py:414
  9.4 0.8 reduce-window.9
  10.2 0.0 copy-start.11
  10.2 0.0 copy-done.2
  10.2 0.0 copy-start.4
  10.2 1.2 copy-done.4
  11.4 0.9 copy-done.9
  12.3 2.2 %shard_map.94.refs_4_ = bf16[256,128]{1,0:T(8,128)(2,1)S(1)} custom-call(s32[4]{0:T(128)S(1)} %bitcast.6, bf16[128,4096]{1,0:T(8,128)(2,1)S(1)} %copy-done.2, bf16[128,4096]{1,0:T(8,128)(2,1)S(1)} %copy-done.4, bf16[128,512]{1,0:T(8,128)(2,1)S(1)} %copy-done.9), custom_call_target="tpu_custom_call" | custom-call | flops 70000000 | bytes 1048576 | tf_op jit(solution)/shard_map/pallas_call | solution.py:178
  14.5 0.0 copy-start.10
  14.5 0.6 copy-done.10
  15.1 6.8 %shard_map.95 = bf16[8,160,1024]{2,1,0:T(8,128)(2,1)} custom-call(s32[1]{0:T(128)} %bitcast.4.me_ref, bf16[128,8192]{1,0:T(8,128)(2,1)} %refs_3_.1, bf16[128,8192]{1,0:T(8,128)(2,1)} %refs_3_.1, bf16[128,8192]{1,0:T(8,128)(2,1)} %refs_3_.1, bf16[128,8192]{1,0:T(8,128)(2,1)} %refs_3_.1, bf16[256,128]{1,0:T(8,128)(2,1)} %copy-done.10), custom_call_target="tpu_custom_call" | custom-call | bytes 4194304 | tf_op jit(solution)/shard_map/pallas_call | solution.py:280
  21.9 0.0 all-to-all-done.k_ref
  21.9 0.0 copy-start.6
  21.9 7.2 %all-to-all-start.1 = ((bf16[8,160,1024]{2,1,0:T(8,128)(2,1)}), bf16[8,160,1024]{2,1,0:T(8,128)(2,1)S(1)}, u32[]{:S(2)}, u32[]{:S(2)}) async-start(bf16[8,160,1024]{2,1,0:T(8,128)(2,1)} %shard_map.95), calls=%async_computation.1 | async-start | bytes 5242880 | tf_op jit(solution)/shard_map/all_to_all | solution.py:414
  29.2 0.0 copy-done
  29.2 5.5 %collective-permute-start.2 = (bf16[32,512]{1,0:T(8,128)(2,1)S(1)}, bf16[32,512]{1,0:T(8,128)(2,1)S(1)}, u32[]{:S(2)}, u32[]{:S(2)}) collective-permute-start(bf16[32,512]{1,0:T(8,128)(2,1)S(1)} %constant_dynamic-slice_fusion), channel_id=1, source_target_pairs={{0,96},{16,112},{32,64},{48,80},{64,32},{80,48},{96,0},{112,16},{1... | collective-permute-start | bytes 98312 | tf_op jit(solution)/shard_map/ppermute | solution.py:424
  34.7 1.5 collective-permute-start.1
  36.1 1.0 collective-permute-start
  37.1 0.6 constant_dynamic-update-slice_fusion.4
  37.8 0.0 collective-permute-done.2
  37.8 1.7 collective-permute-done.1
  39.5 4.5 %collective-permute-done = bf16[32,512]{1,0:T(8,128)(2,1)S(1)} collective-permute-done((bf16[32,512]{1,0:T(8,128)(2,1)S(1)}, bf16[32,512]{1,0:T(8,128)(2,1)S(1)}, u32[]{:S(2)}, u32[]{:S(2)}) %collective-permute-start) | collective-permute-done | bytes 32800 | tf_op jit(solution)/shard_map/ppermute | solution.py:424
  44.0 1.2 collective-permute-start.3
  45.2 0.6 constant_dynamic-update-slice_fusion.3
  45.8 0.6 constant_dynamic-update-slice_fusion.2
  46.4 0.6 constant_dynamic-update-slice_fusion.1
  47.1 2.0 %collective-permute-done.3 = bf16[128,512]{1,0:T(8,128)(2,1)S(1)} collective-permute-done((bf16[128,512]{1,0:T(8,128)(2,1)S(1)}, bf16[128,512]{1,0:T(8,128)(2,1)S(1)}, u32[]{:S(2)}, u32[]{:S(2)}) %collective-permute-start.3) | collective-permute-done | bytes 131104 | tf_op jit(solution)/shard_map/ppermute | solution.py:424
  49.0 0.7 constant_dynamic-update-slice_fusion
  49.7 0.7 collective-permute-start.4
  50.4 0.0 copy-done.12
  50.4 0.6 constant_dynamic-slice_fusion.1
  51.0 0.0 copy-done.11
  51.0 0.0 copy-done.6
  51.0 1.2 copy-done.3
  52.3 1.2 copy-done.5
  53.5 5.4 %shard_map.96.dv_ref = bf16[8,64,512]{2,1,0:T(8,128)(2,1)S(1)} custom-call(s32[8]{0:T(128)S(1)} %bitcast.10, s32[1]{0:T(128)} %bitcast.1.place_ref, s32[4]{0:T(128)S(1)} %bitcast.7, bf16[128,4096]{1,0:T(8,128)(2,1)S(1)} %copy-done.3, bf16[128,4096]{1,0:T(8,128)(2,1)S(1)} %copy-done.5, bf16[8,64,512]{2,1,0:T(8,128)(2,1)S(1)} %all-to-all-done.k_ref), custom_call_target="tpu_custom_call" | custom-call | flops 600000000 | bytes 4194304 | tf_op jit(solution)/shard_map/pallas_call | solution.py:194
  58.9 0.0 copy-start.7
  58.9 4.8 %collective-permute-done.4 = bf16[256,512]{1,0:T(8,128)(2,1)} collective-permute-done((bf16[256,512]{1,0:T(8,128)(2,1)}, bf16[256,512]{1,0:T(8,128)(2,1)}, u32[]{:S(2)}, u32[]{:S(2)}) %collective-permute-start.4) | collective-permute-done | bytes 262176 | tf_op jit(solution)/shard_map/ppermute | solution.py:424
  63.7 1.7 constant_dynamic-update-slice_fusion.5.mine_ref
  65.4 0.0 collective-permute-start.5
  65.4 0.0 copy-done.7
  65.4 2.1 %collective-permute-done.5.theirs_ref = bf16[512,512]{1,0:T(8,128)(2,1)S(1)} collective-permute-done((bf16[512,512]{1,0:T(8,128)(2,1)}, bf16[512,512]{1,0:T(8,128)(2,1)S(1)}, u32[]{:S(2)}, u32[]{:S(2)}) %collective-permute-start.5) | collective-permute-done | bytes 524320 | tf_op jit(solution)/shard_map/ppermute | solution.py:424
  67.5 0.0 all-to-all-done.1.tokens_ref
  67.5 1.0 copy-done.8
  68.5 2.3 %shard_map.97 = bf16[8,192,512]{2,1,0:T(8,128)(2,1)S(1)} custom-call(bf16[8,160,1024]{2,1,0:T(8,128)(2,1)S(1)} %all-to-all-done.1.tokens_ref, bf16[512,512]{1,0:T(8,128)(2,1)} %constant_dynamic-update-slice_fusion.5.mine_ref, bf16[512,512]{1,0:T(8,128)(2,1)S(1)} %collective-permute-done.5.theirs_ref, bf16[8,64,512]{2,1,0:T(8,128)(2,1)S(1)} %copy-done.8), custom_call_target="tpu_custom_call" | custom-call | flops 1342177280 | bytes 6291456 | tf_op jit(solution)/shard_map/pallas_call | solution.py:305
  70.9 30.6 %all_to_all.30.parts_ref = bf16[8,192,512]{2,1,0:T(8,128)(2,1)} all-to-all(bf16[8,192,512]{2,1,0:T(8,128)(2,1)S(1)} %shard_map.97), channel_id=1, replica_groups=mesh['ylo'=2,'z'=8,'core'=2,'yhi'=2,'x'=4] {'yhi','x'}, dimensions={0} | all-to-all | bytes 3145728 | tf_op jit(solution)/shard_map/all_to_all | solution.py:414
  101.4 2.7 %shard_map.98 = (bf16[8,128,512]{2,1,0:T(8,128)(2,1)}, bf16[128,512]{1,0:T(8,128)(2,1)}) custom-call(bf16[8,192,512]{2,1,0:T(8,128)(2,1)} %all_to_all.30.parts_ref), custom_call_target="tpu_custom_call" | custom-call | flops 786432 | bytes 3145728 | tf_op jit(solution)/shard_map/pallas_call | solution.py:332
  104.1 20.1 %all_to_all.31.d_value_ref.v_hbm = bf16[8,128,512]{2,1,0:T(8,128)(2,1)S(1)} all-to-all(bf16[8,128,512]{2,1,0:T(8,128)(2,1)} %get-tuple-element.22), channel_id=1, replica_groups=mesh['ylo'=2,'z'=8,'core'=2,'yhi'=2,'x'=4] {'yhi','x'}, dimensions={0} | all-to-all | bytes 2097152 | tf_op jit(solution)/shard_map/all_to_all | solution.py:414
  124.2 0.7 shard_map.99
  125.0 0.1 collective-permute-start.6
  125.1 1.9 %collective-permute-done.6.refs_0_ = bf16[16,32,512]{2,1,0:T(8,128)(2,1)S(1)} collective-permute-done((bf16[16,32,512]{2,1,0:T(8,128)(2,1)S(1)}, bf16[16,32,512]{2,1,0:T(8,128)(2,1)S(1)}, u32[]{:S(2)}, u32[]{:S(2)}) %collective-permute-start.6) | collective-permute-done | bytes 524320 | tf_op jit(solution)/shard_map/ppermute | solution.py:424
  127.0 0.0 copy-done.1
  127.0 1.6 shard_map.100
  128.5 8.6 %all-to-all-start.4 = ((bf16[16,32,512]{2,1,0:T(8,128)(2,1)}), bf16[16,32,512]{2,1,0:T(8,128)(2,1)S(1)}, u32[]{:S(2)}, u32[]{:S(2)}) async-start(bf16[16,32,512]{2,1,0:T(8,128)(2,1)} %shard_map.100), calls=%async_computation.4 | async-start | bytes 1048576 | tf_op jit(solution)/shard_map/all_to_all | solution.py:414
  137.1 12.2 %shard_map.101 = (f32[128,4096]{1,0:T(8,128)}, bf16[8,64,512]{2,1,0:T(8,128)(2,1)}, f32[64,512]{1,0:T(8,128)}) custom-call(s32[8]{0:T(128)} %bitcast.9, s32[1]{0:T(128)} %bitcast.1.place_ref, s32[4]{0:T(128)} %bitcast.8, bf16[128,4096]{1,0:T(8,128)(2,1)} %q_hbm.3, bf16[128,4096]{1,0:T(8,128)(2,1)} %u_hbm.3, bf16[128,512]{1,0:T(8,128)(2,1)} %ks_ref.3, ...), custom_call_target="tpu_custom_call" | custom-call | flops 1400000000 | bytes 6291456 | tf_op jit(solution)/shard_map/pallas_call | solution.py:210
  149.3 3.4 %all-to-all-done.4.pieces_ref = bf16[16,32,512]{2,1,0:T(8,128)(2,1)S(1)} async-done(((bf16[16,32,512]{2,1,0:T(8,128)(2,1)}), bf16[16,32,512]{2,1,0:T(8,128)(2,1)S(1)}, u32[]{:S(2)}, u32[]{:S(2)}) %all-to-all-start.4) | async-done | bytes 524320 | tf_op jit(solution)/shard_map/all_to_all | solution.py:414
  152.7 0.8 copy-done.13
  153.6 2.2 %shard_map.102 = bf16[8,96,512]{2,1,0:T(8,128)(2,1)} custom-call(bf16[16,32,512]{2,1,0:T(8,128)(2,1)} %copy-done.13, bf16[8,64,512]{2,1,0:T(8,128)(2,1)} %get-tuple-element.25.dk_ref), custom_call_target="tpu_custom_call" | custom-call | flops 262144 | bytes 1048576 | tf_op jit(solution)/shard_map/pallas_call | solution.py:350
  155.7 17.5 %all_to_all.32.parts_ref = bf16[8,96,512]{2,1,0:T(8,128)(2,1)} all-to-all(bf16[8,96,512]{2,1,0:T(8,128)(2,1)} %shard_map.102), channel_id=1, replica_groups=mesh['ylo'=2,'z'=8,'core'=2,'yhi'=2,'x'=4] {'yhi','x'}, dimensions={0} | all-to-all | bytes 1572864 | tf_op jit(solution)/shard_map/all_to_all | solution.py:414
  173.3 2.1 %shard_map.103 = (f32[128,512]{1,0:T(8,128)}, f32[256,512]{1,0:T(8,128)}) custom-call(bf16[8,96,512]{2,1,0:T(8,128)(2,1)} %all_to_all.32.parts_ref, f32[64,512]{1,0:T(8,128)} %get-tuple-element.26.dk_short_ref), custom_call_target="tpu_custom_call" | custom-call | flops 393216 | bytes 1572864 | tf_op jit(solution)/shard_map/pallas_call | solution.py:366
  (9 shorter events, 0.0 us)
Async XLA Ops:
  0.6 28.5 %copy-start = (bf16[256,512]{1,0:T(8,128)(2,1)S(1)}, bf16[256,512]{1,0:T(8,128)(2,1)}, u32[]{:S(2)}) copy-start(bf16[256,512]{1,0:T(8,128)(2,1)} %param.11) | copy-start | bytes 786436
  0.6 9.6 %copy-start.2 = (bf16[128,4096]{1,0:T(8,128)(2,1)S(1)}, bf16[128,4096]{1,0:T(8,128)(2,1)}, u32[]{:S(2)}) copy-start(bf16[128,4096]{1,0:T(8,128)(2,1)} %q_hbm.3) | copy-start | bytes 3145732
  2.4 19.5 %all-to-all-start = ((bf16[8,64,512]{2,1,0:T(8,128)(2,1)}), bf16[8,64,512]{2,1,0:T(8,128)(2,1)S(1)}, u32[]{:S(2)}, u32[]{:S(2)}) async-start(bf16[8,64,512]{2,1,0:T(8,128)(2,1)} %broadcast_in_dim.14), calls=%async_computation | async-start | bytes 1048576 | tf_op jit(solution)/shard_map/all_to_all | solution.py:414
  10.2 40.8 %copy-start.11 = (s32[4,1]{0,1:T(1,128)}, s32[4,1]{0,1:T(1,128)S(1)}, u32[]{:S(2)}) copy-start(s32[4,1]{0,1:T(1,128)S(1)} %reduce-window.9) | copy-start | bytes 52
  10.2 1.2 copy-start.4
  11.4 0.9 copy-start.9
  14.5 0.6 copy-start.10
  21.9 28.5 %copy-start.12 = (s32[1,8]{1,0:T(1,128)S(1)}, s32[1,8]{1,0:T(1,128)}, u32[]{:S(2)}) copy-start(s32[1,8]{1,0:T(1,128)} %param.13) | copy-start | bytes 100
  21.9 29.1 %copy-start.6 = (bf16[8,64,512]{2,1,0:T(8,128)(2,1)}, bf16[8,64,512]{2,1,0:T(8,128)(2,1)S(1)}, u32[]{:S(2)}) copy-start(bf16[8,64,512]{2,1,0:T(8,128)(2,1)S(1)} %all-to-all-done.k_ref) | copy-start | bytes 1572868
  21.9 45.6 %all-to-all-start.1 = ((bf16[8,160,1024]{2,1,0:T(8,128)(2,1)}), bf16[8,160,1024]{2,1,0:T(8,128)(2,1)S(1)}, u32[]{:S(2)}, u32[]{:S(2)}) async-start(bf16[8,160,1024]{2,1,0:T(8,128)(2,1)} %shard_map.95), calls=%async_computation.1 | async-start | bytes 5242880 | tf_op jit(solution)/shard_map/all_to_all | solution.py:414
  29.2 8.6 %collective-permute-start.2 = (bf16[32,512]{1,0:T(8,128)(2,1)S(1)}, bf16[32,512]{1,0:T(8,128)(2,1)S(1)}, u32[]{:S(2)}, u32[]{:S(2)}) collective-permute-start(bf16[32,512]{1,0:T(8,128)(2,1)S(1)} %constant_dynamic-slice_fusion), channel_id=1, source_target_pairs={{0,96},{16,112},{32,64},{48,80},{64,32},{80,48},{96,0},{112,16},{1... | collective-permute-start | bytes 98312 | tf_op jit(solution)/shard_map/ppermute | solution.py:424
  34.7 4.8 %collective-permute-start.1 = (bf16[32,512]{1,0:T(8,128)(2,1)S(1)}, bf16[32,512]{1,0:T(8,128)(2,1)S(1)}, u32[]{:S(2)}, u32[]{:S(2)}) collective-permute-start(bf16[32,512]{1,0:T(8,128)(2,1)S(1)} %constant_dynamic-slice_fusion), channel_id=1, source_target_pairs={{0,32},{16,48},{32,0},{48,16},{64,96},{80,112},{96,64},{112,80},{1... | collective-permute-start | bytes 98312 | tf_op jit(solution)/shard_map/ppermute | solution.py:424
  36.1 7.8 %collective-permute-start = (bf16[32,512]{1,0:T(8,128)(2,1)S(1)}, bf16[32,512]{1,0:T(8,128)(2,1)S(1)}, u32[]{:S(2)}, u32[]{:S(2)}) collective-permute-start(bf16[32,512]{1,0:T(8,128)(2,1)S(1)} %constant_dynamic-slice_fusion), channel_id=1, source_target_pairs={{0,64},{16,80},{32,96},{48,112},{64,0},{80,16},{96,32},{112,48},{1... | collective-permute-start | bytes 98312 | tf_op jit(solution)/shard_map/ppermute | solution.py:424
  44.0 5.1 %collective-permute-start.3 = (bf16[128,512]{1,0:T(8,128)(2,1)S(1)}, bf16[128,512]{1,0:T(8,128)(2,1)S(1)}, u32[]{:S(2)}, u32[]{:S(2)}) collective-permute-start(bf16[128,512]{1,0:T(8,128)(2,1)S(1)} %pad_maximum_fusion), channel_id=1, source_target_pairs={{0,16},{16,0},{32,48},{48,32},{64,80},{80,64},{96,112},{112,96},{1... | collective-permute-start | bytes 393224 | tf_op jit(solution)/shard_map/ppermute | solution.py:424
  49.7 14.0 %collective-permute-start.4 = (bf16[256,512]{1,0:T(8,128)(2,1)}, bf16[256,512]{1,0:T(8,128)(2,1)}, u32[]{:S(2)}, u32[]{:S(2)}) collective-permute-start(bf16[256,512]{1,0:T(8,128)(2,1)} %get-tuple-element.29), channel_id=1, source_target_pairs={{0,128},{128,0},{1,129},{129,1},{2,130},{130,2},{3,131},{131,3},{4... | collective-permute-start | bytes 786440 | tf_op jit(solution)/shard_map/ppermute | solution.py:424
  51.0 1.2 copy-start.3
  52.3 1.2 copy-start.5
  58.9 6.5 %copy-start.7 = (bf16[8,64,512]{2,1,0:T(8,128)(2,1)}, bf16[8,64,512]{2,1,0:T(8,128)(2,1)S(1)}, u32[]{:S(2)}) copy-start(bf16[8,64,512]{2,1,0:T(8,128)(2,1)S(1)} %shard_map.96.dv_ref) | copy-start | bytes 1572868
  65.4 2.1 %collective-permute-start.5 = (bf16[512,512]{1,0:T(8,128)(2,1)}, bf16[512,512]{1,0:T(8,128)(2,1)S(1)}, u32[]{:S(2)}, u32[]{:S(2)}) collective-permute-start(bf16[512,512]{1,0:T(8,128)(2,1)} %constant_dynamic-update-slice_fusion.5.mine_ref), channel_id=1, source_target_pairs={{0,8},{8,0},{1,9},{9,1},{2,10},{10,2},{3,11},{11,3},{4,12},{12,4},... | collective-permute-start | bytes 1572872 | tf_op jit(solution)/shard_map/ppermute | solution.py:424
  67.5 1.0 copy-start.8
  124.2 2.8 %copy-start.1 = (bf16[8,128,512]{2,1,0:T(8,128)(2,1)}, bf16[8,128,512]{2,1,0:T(8,128)(2,1)S(1)}, u32[]{:S(2)}) copy-start(bf16[8,128,512]{2,1,0:T(8,128)(2,1)S(1)} %all_to_all.31.d_value_ref.v_hbm) | copy-start | bytes 3145732
  125.0 2.0 %collective-permute-start.6 = (bf16[16,32,512]{2,1,0:T(8,128)(2,1)S(1)}, bf16[16,32,512]{2,1,0:T(8,128)(2,1)S(1)}, u32[]{:S(2)}, u32[]{:S(2)}) collective-permute-start(bf16[16,32,512]{2,1,0:T(8,128)(2,1)S(1)} %shard_map.99), channel_id=1, source_target_pairs={{0,8},{8,0},{1,9},{9,1},{2,10},{10,2},{3,11},{11,3},{4,12},{12,4},... | collective-permute-start | bytes 1572872 | tf_op jit(solution)/shard_map/ppermute | solution.py:424
  128.5 24.2 %all-to-all-start.4 = ((bf16[16,32,512]{2,1,0:T(8,128)(2,1)}), bf16[16,32,512]{2,1,0:T(8,128)(2,1)S(1)}, u32[]{:S(2)}, u32[]{:S(2)}) async-start(bf16[16,32,512]{2,1,0:T(8,128)(2,1)} %shard_map.100), calls=%async_computation.4 | async-start | bytes 1048576 | tf_op jit(solution)/shard_map/all_to_all | solution.py:414
  152.7 0.8 copy-start.13

commit v4 on v2

--- a/solution.py
+++ b/solution.py
@@ -52,8 +52,33 @@
     return e * (1.0 / jnp.sum(e, axis=0, keepdims=True))
 
 
-def dvalue_kernel(order_ref, place_ref, ends_ref, q_ref, u_ref, ks_ref, k_ref,
-                  dvl_ref, dvs_ref, long_bias, short_bias):
+def fetch(sources, buffers, sems):
+    def copy(at, head):
+        source, rows, lanes = sources[at]
+        return pltpu.make_async_copy(
+            source.at[rows + (pl.ds(pl.multiple_of(head * lanes, lanes), lanes),)],
+            buffers[at].at[head], sems.at[at, head])
+
+    step = pl.program_id(0)
+
+    @pl.when(step == 0)
+    def _():
+        for head in range(KEY_VALUE_HEADS):
+            for at in range(len(sources)):
+                copy(at, head).start()
+
+    for at in range(len(sources)):
+        copy(at, step).wait()
+    return [buffer.at[step] for buffer in buffers]
+
+
+ALL = slice(None)
+
+
+def dvalue_kernel(order_ref, place_ref, ends_ref, q_hbm, u_hbm, ks_ref, k_ref,
+                  dvl_ref, dvs_ref, long_bias, short_bias, q_buffer, u_buffer, sems):
+    q_ref, u_ref = fetch([(q_hbm, (ALL,), WIDE), (u_hbm, (ALL,), WIDE)], [q_buffer, u_buffer], sems)
+
     @pl.when(pl.program_id(0) == 0)
     def _():
         fill_masks(order_ref, place_ref, ends_ref, long_bias, short_bias)
@@ -70,8 +95,12 @@
         out[...] = total.astype(out.dtype).reshape(out.shape)
 
 
-def dscore_kernel(order_ref, place_ref, ends_ref, q_ref, u_ref, ks_ref, vs_ref, k_ref, v_ref,
-                  dq_ref, dkl_ref, dks_ref, long_bias, short_bias):
+def dscore_kernel(order_ref, place_ref, ends_ref, q_hbm, u_hbm, ks_ref, vs_ref, k_ref, v_hbm,
+                  dq_ref, dkl_ref, dks_ref, long_bias, short_bias, q_buffer, u_buffer, v_buffer, sems):
+    q_ref, u_ref, v_ref = fetch(
+        [(q_hbm, (ALL,), WIDE), (u_hbm, (ALL,), WIDE), (v_hbm, (ALL, pl.ds(TOK, LB)), HEAD_SIZE)],
+        [q_buffer, u_buffer, v_buffer], sems)
+
     @pl.when(pl.program_id(0) == 0)
     def _():
         fill_masks(order_ref, place_ref, ends_ref, long_bias, short_bias)
@@ -102,6 +131,7 @@
 WIDE = GROUP * HEAD_SIZE
 WIDTH = KEY_VALUE_HEADS * HEAD_SIZE
 TOK = LB + SB
+PIECE = 32
 
 
 def block(rows, columns):
@@ -112,8 +142,14 @@
     return pl.BlockSpec((N_CTX, LB, HEAD_SIZE), lambda k, *_: (0, at, k))
 
 
-def scratch():
-    return [pltpu.VMEM((N_CTX * LB, LANES), jnp.float32), pltpu.VMEM((SB, LANES), jnp.float32)]
+def scratch(*more):
+    fetched = [(TOK, WIDE), (TOK, WIDE)] + list(more)
+    return [pltpu.VMEM((N_CTX * LB, LANES), jnp.float32), pltpu.VMEM((SB, LANES), jnp.float32)] + [
+        pltpu.VMEM((KEY_VALUE_HEADS,) + shape, jnp.bfloat16) for shape in fetched
+    ] + [pltpu.SemaphoreType.DMA((len(fetched), KEY_VALUE_HEADS))]
+
+
+ELSEWHERE = pl.BlockSpec(memory_space=pltpu.HBM)
 
 
 LONG_ROWS = jax.ShapeDtypeStruct((N_CTX, LB, WIDTH), jnp.bfloat16)
@@ -125,12 +161,12 @@
         grid_spec=pltpu.PrefetchScalarGridSpec(
             num_scalar_prefetch=3,
             grid=(KEY_VALUE_HEADS,),
-            in_specs=[block(TOK, WIDE), block(TOK, WIDE), block(TOK, HEAD_SIZE), long_block(0)],
+            in_specs=[ELSEWHERE, ELSEWHERE, block(TOK, HEAD_SIZE), long_block(0)],
             out_specs=[long_block(0), block(SB, HEAD_SIZE)],
             scratch_shapes=scratch(),
         ),
         out_shape=[LONG_ROWS, jax.ShapeDtypeStruct((SB, WIDTH), jnp.bfloat16)],
-        compiler_params=pltpu.CompilerParams(vmem_limit_bytes=32 << 20),
+        compiler_params=pltpu.CompilerParams(vmem_limit_bytes=16 << 20),
         cost_estimate=pl.CostEstimate(flops=700_000_000, bytes_accessed=4 << 20, transcendentals=1 << 20),
     )(*scalars, queries, upstream, keys, all_keys)
 
@@ -141,14 +177,14 @@
         grid_spec=pltpu.PrefetchScalarGridSpec(
             num_scalar_prefetch=3,
             grid=(KEY_VALUE_HEADS,),
-            in_specs=[block(TOK, WIDE), block(TOK, WIDE), block(TOK, HEAD_SIZE), block(TOK, HEAD_SIZE),
-                      long_block(0), long_block(TOK // LB)],
+            in_specs=[ELSEWHERE, ELSEWHERE, block(TOK, HEAD_SIZE), block(TOK, HEAD_SIZE),
+                      long_block(0), ELSEWHERE],
             out_specs=[block(TOK, WIDE), long_block(0), block(SB, HEAD_SIZE)],
-            scratch_shapes=scratch(),
+            scratch_shapes=scratch((N_CTX, LB, HEAD_SIZE)),
         ),
-        out_shape=[jax.ShapeDtypeStruct((TOK, QUERY_HEADS * HEAD_SIZE), jnp.float32), LONG_ROWS,
+        out_shape=[jax.ShapeDtypeStruct((TOK, QUERY_HEADS * HEAD_SIZE), jnp.float32), jax.ShapeDtypeStruct((N_CTX, LB + PIECE, WIDTH), jnp.bfloat16),
                    jax.ShapeDtypeStruct((SB, WIDTH), jnp.float32)],
-        compiler_params=pltpu.CompilerParams(vmem_limit_bytes=32 << 20),
+        compiler_params=pltpu.CompilerParams(vmem_limit_bytes=60 << 20),
         cost_estimate=pl.CostEstimate(flops=1_400_000_000, bytes_accessed=6 << 20, transcendentals=1 << 20),
     )(*scalars, queries, upstream, keys, values, all_keys, spread_rows)
 
@@ -158,7 +194,6 @@
 CTX = ("yhi", "x")
 
 
-PIECE = 32
 DP_BLOCK = N_CTX * PIECE
 TOGETHER = 4
 
@@ -174,6 +209,13 @@
             [ref[:, member * PIECE:(member + 1) * PIECE] for ref in block_refs], axis=1)
 
 
+def turned(slot, depth):
+    z, bits = 0, depth.bit_length() - 1
+    for bit in range(bits):
+        z = z + ((slot >> bit) & 1) * (1 << (bits - 1 - bit))
+    return z
+
+
 def regroup(me, tokens):
     rows, width = tokens.shape
     depth = width // (DP_BLOCK * Y_LO * CORES)
@@ -181,7 +223,7 @@
     def source(at):
         def index(g, me_ref):
             slot = g * TOGETHER + at
-            core, y_lo, z = slot // (Y_LO * depth), slot // depth % Y_LO, slot % depth
+            core, y_lo, z = slot // (Y_LO * depth), slot % Y_LO, turned(slot // Y_LO % depth, depth)
             return 0, ((y_lo * depth + z) * CORES + core) ^ me_ref[0]
         return pl.BlockSpec((rows, DP_BLOCK), index)
 
@@ -208,13 +250,29 @@
     out_ref[:, :LB] = dv_ref[...]
 
 
+def key_copies_kernel(keys_ref, out_ref):
+    for member in range(N_CTX):
+        out_ref[member] = keys_ref[...]
+
+
+def key_copies(keys):
+    return pl.pallas_call(
+        key_copies_kernel,
+        grid=(1,),
+        in_specs=[pl.BlockSpec((LB, WIDTH), lambda g: (0, 0))],
+        out_specs=pl.BlockSpec((N_CTX, LB, WIDTH), lambda g: (0, 0, 0)),
+        out_shape=LONG_ROWS,
+        cost_estimate=pl.CostEstimate(flops=0, bytes_accessed=1 << 19, transcendentals=0),
+    )(keys)
+
+
 def value_parts(tokens, mine, theirs, dv_all):
     return pl.pallas_call(
         values_kernel,
         in_specs=whole(4),
         out_specs=whole()[0],
         out_shape=jax.ShapeDtypeStruct((N_CTX, LB + TOK, WIDTH), jnp.bfloat16),
-        compiler_params=pltpu.CompilerParams(vmem_limit_bytes=32 << 20),
+        compiler_params=pltpu.CompilerParams(vmem_limit_bytes=16 << 20),
         cost_estimate=pl.CostEstimate(flops=2 * tokens.size * WIDTH, bytes_accessed=6 << 20,
                                       transcendentals=0),
     )(tokens, mine, theirs, dv_all)
@@ -247,27 +305,29 @@
     )(parts, dv_short)
 
 
-def closing_kernel(pieces_ref, dk_ref, out_ref):
+def closing_kernel(pieces_ref, _, out_ref):
     share = added_up(pieces_ref, 0, PIECE).astype(out_ref.dtype)
     for member in range(N_CTX):
-        out_ref[member, :PIECE] = share
-    out_ref[:, PIECE:] = dk_ref[...]
-
-
-def closing(pieces, dk_all):
+        out_ref[member] = share
+
+
+def closing(pieces, payload):
     return pl.pallas_call(
         closing_kernel,
-        in_specs=whole(2),
-        out_specs=whole()[0],
-        out_shape=jax.ShapeDtypeStruct((N_CTX, PIECE + LB, WIDTH), jnp.bfloat16),
-        cost_estimate=pl.CostEstimate(flops=pieces.size, bytes_accessed=4 * pieces.size, transcendentals=0),
-    )(pieces, dk_all)
+        grid=(1,),
+        in_specs=[pl.BlockSpec(pieces.shape, lambda g: (0, 0, 0)), ELSEWHERE],
+        out_specs=pl.BlockSpec((N_CTX, PIECE, WIDTH), lambda g: (0, LB // PIECE, 0)),
+        out_shape=jax.ShapeDtypeStruct(payload.shape, payload.dtype),
+        input_output_aliases={1: 0},
+        compiler_params=pltpu.CompilerParams(vmem_limit_bytes=60 << 20),
+        cost_estimate=pl.CostEstimate(flops=pieces.size, bytes_accessed=2 * pieces.size, transcendentals=0),
+    )(pieces, payload)
 
 
 def last_kernel(parts_ref, dk_short_ref, dk_ref, grad_ref):
-    dk_ref[:LB] = added_up(parts_ref, PIECE, PIECE + LB)
+    dk_ref[:LB] = added_up(parts_ref, 0, LB)
     dk_ref[LB:] = dk_short_ref[...]
-    grad_ref[...] = parts_ref[:, :PIECE].astype(grad_ref.dtype).reshape(grad_ref.shape)
+    grad_ref[...] = parts_ref[:, LB:].astype(grad_ref.dtype).reshape(grad_ref.shape)
 
 
 def last(parts, dk_short):
@@ -292,7 +352,9 @@
             tokens_ref[:, at:at + some * rows], d_value, (((0,), (0,)), ((), ())),
             preferred_element_type=jnp.float32)
         for slot in range(some):
-            block = (first + slot) ^ me_ref[0]
+            depth = count // Y_LO
+            z, y_lo = divmod(first + slot, Y_LO)
+            block = (y_lo * depth + turned(z, depth)) ^ me_ref[0]
             piece = part[slot * rows:(slot + 1) * rows]
             for ref in add_refs:
                 piece += ref[block].astype(jnp.float32)
@@ -306,7 +368,7 @@
         in_specs=[pl.BlockSpec(memory_space=pltpu.SMEM)] + whole(2 + len(added)),
         out_specs=whole()[0],
         out_shape=jax.ShapeDtypeStruct((count, PIECE, columns), jnp.bfloat16),
-        compiler_params=pltpu.CompilerParams(vmem_limit_bytes=32 << 20),
+        compiler_params=pltpu.CompilerParams(vmem_limit_bytes=16 << 20),
         cost_estimate=pl.CostEstimate(flops=tokens.size * columns, bytes_accessed=3 << 20,
                                       transcendentals=0),
     )(me[None], tokens, d_value, *added)
@@ -314,11 +376,6 @@
 
 def exchange(pieces, axes):
     return lax.all_to_all(pieces, axes, 0, 0, tiled=True)
-
-
-def spread(piece, axes):
-    count = lax.axis_size(axes)
-    return exchange(jnp.broadcast_to(piece[None], (count,) + piece.shape), axes)
 
 
 def swap_along(array, axis, step):
@@ -337,22 +394,21 @@
     order = stretch_order[0]
     scalars = (order, lax.dynamic_slice(order, (member,), (1,)), jnp.cumsum(doc_lengths[0]))
 
-    all_keys = spread(rotated_key_rows[:LB], CTX)
+    all_keys = exchange(key_copies(rotated_key_rows), CTX)
     grouped = regroup(plane * CORES + lax.axis_index("core"), tokens)
     grouped, all_keys = lax.optimization_barrier((grouped, all_keys))
     tok = exchange(grouped, CTX).reshape(N_CTX * TOK, -1)
-    dv_all, dv_short = dvalues(scalars, queries, upstream, rotated_key_rows, all_keys)
 
     weight = lax.dynamic_slice_in_dim(value_projection_weight, member * PIECE, PIECE, 0)
     weight = after(weight, grouped)
-    step = 1
-    while step < lax.axis_size("z"):
-        if step == 4:
-            weight = after(weight, dv_all)
-        weight = jnp.concatenate([weight, swap_along(weight, "z", step)], axis=0)
-        step *= 2
+    depth = lax.axis_size("z")
+    far = [turned(slot, depth) for slot in range(depth // 2)]
     weight = jnp.concatenate([weight, swap_along(weight, "ylo", 1)], axis=0)
-    other_weight = swap_along(weight, "core", 1)
+    weight = jnp.concatenate([weight] + [swap_along(weight, "z", step) for step in far[1:]], axis=0)
+    dv_all, dv_short = dvalues(scalars, queries, upstream, rotated_key_rows, after(all_keys, weight))
+    if depth > 1:
+        weight = jnp.concatenate([weight, swap_along(weight, "z", 1)], axis=0)
+    other_weight = swap_along(after(weight, dv_all), "core", 1)
 
     parts = exchange(value_parts(tok, weight, other_weight, dv_all), CTX)
     spread_rows, values = middle(parts, dv_short)

time: 172 us -> 190 us (1.10)
  waiting for transfers between devices: 23.8 us -> 33.9 us
  blocking collectives: 74.4 us -> 80.6 us
  local copies, waits for them, and re-layouts: 13.1 us -> 9.8 us
  Pallas kernels: 33 us -> 36.3 us
    ppermute x6 -> x7, waiting for transfers between devices: 18.8 us -> 25.6 us  [swap_along(): return lax.ppermute(array, axis, [(i, i ^ step) for i in range(count)])]
    all_to_all x3, blocking collectives: 74.4 us -> 80.6 us  [exchange(): return lax.all_to_all(pieces, axes, 0, 0, tiled=True)]
    all_to_all x3, waiting for transfers between devices: 5.06 us -> 8.28 us  [exchange(): return lax.all_to_all(pieces, axes, 0, 0, tiled=True)]
    unnamed x38 -> x30, local copies, waits for them, and re-layouts: 10.7 us -> 7.47 us
    pallas_call x1, Pallas kernels: 10.3 us -> 12.3 us  [dscores(): pl.pallas_call(dscore_kernel, grid_spec=pltpu.PrefetchScalarGridSpec(num_...]
    ppermute x6 -> x7, starting transfers between devices: 9 us -> 9.12 us  [swap_along(): return lax.ppermute(array, axis, [(i, i ^ step) for i in range(count)])]
  transfers between devices with their start and end apart: 9 -> 10, of which waited for: 7 -> 8; matrix products, arithmetic and copies ran while one was open for 1% -> 3% of each run, Pallas kernels for 13% -> 13%
where the time goes in v4:
time: 190 us; the launch traced here: 188 us
  blocking collectives  80.6 us (42%)
  Pallas kernels  36.3 us (19%)
  waiting for transfers between devices  33.9 us (18%)
  starting transfers between devices  26.8 us (14%)
  local copies, waits for them, and re-layouts  9.8 us (5%)
    all_to_all x3, blocking collectives, exchange(): return lax.all_to_all(pieces, axes, 0, 0, tiled=True)  80.6 us
    ppermute x7, waiting for transfers between devices, swap_along(): return lax.ppermute(array, axis, [(i, i ^ step) for i in range(count)])  25.6 us
    all_to_all x3, starting transfers between devices, exchange(): return lax.all_to_all(pieces, axes, 0, 0, tiled=True)  17.7 us
    pallas_call x1, Pallas kernels, dscores(): pl.pallas_call(dscore_kernel, grid_spec=pltpu.PrefetchScalarGridSpec(num_...  12.3 us
    ppermute x7, starting transfers between devices, swap_along(): return lax.ppermute(array, axis, [(i, i ^ step) for i in range(count)])  9.12 us
    all_to_all x3, waiting for transfers between devices, exchange(): return lax.all_to_all(pieces, axes, 0, 0, tiled=True)  8.28 us
    unnamed x30, local copies, waits for them, and re-layouts  7.47 us
    pallas_call x1, Pallas kernels, regroup(): pl.pallas_call(regroup_kernel, grid_spec=pltpu.PrefetchScalarGridSpec(num...  6.62 us
  transfers between devices with their start and end apart: 10, of which 8 were waited for; matrix products, arithmetic and copies ran while one was open for 3% of the time, Pallas kernels for 13%

profile of v4, /device:TPU:32, one launch (start us, length us, event | category | flops | bytes accessed | tf_op | source)
XLA Modules:
  0.0 188.4 jit_solution(10675295862644205477)
XLA Ops:
  0.6 0.0 copy-start
  0.6 1.7 shard_map.95
  2.4 6.9 %all-to-all-start = ((bf16[8,64,512]{2,1,0:T(8,128)(2,1)}), bf16[8,64,512]{2,1,0:T(8,128)(2,1)S(1)}, u32[]{:S(2)}, u32[]{:S(2)}) async-start(bf16[8,64,512]{2,1,0:T(8,128)(2,1)} %shard_map.95), calls=%async_computation | async-start | bytes 1048576 | tf_op jit(solution)/shard_map/all_to_all | solution.py:378
  9.3 6.6 %shard_map.94 = bf16[8,128,1024]{2,1,0:T(8,128)(2,1)} custom-call(s32[1]{0:T(128)} %bitcast.4.me_ref, bf16[128,8192]{1,0:T(8,128)(2,1)} %refs_3_.1, bf16[128,8192]{1,0:T(8,128)(2,1)} %refs_3_.1, bf16[128,8192]{1,0:T(8,128)(2,1)} %refs_3_.1, bf16[128,8192]{1,0:T(8,128)(2,1)} %refs_3_.1), custom_call_target="tpu_custom_call" | custom-call | bytes 4194304 | tf_op jit(solution)/shard_map/pallas_call | solution.py:230
  15.9 0.0 copy-start.12
  15.9 0.0 copy-start.9
  15.9 0.0 copy-start.7
  15.9 5.0 %all-to-all-done.k_ref = bf16[8,64,512]{2,1,0:T(8,128)(2,1)S(1)} async-done(((bf16[8,64,512]{2,1,0:T(8,128)(2,1)}), bf16[8,64,512]{2,1,0:T(8,128)(2,1)S(1)}, u32[]{:S(2)}, u32[]{:S(2)}) %all-to-all-start) | async-done | bytes 524320 | tf_op jit(solution)/shard_map/all_to_all | solution.py:378
  20.9 0.0 copy-start.2
  20.9 3.6 %all-to-all-start.1 = ((bf16[8,128,1024]{2,1,0:T(8,128)(2,1)}), bf16[8,128,1024]{2,1,0:T(8,128)(2,1)S(1)}, u32[]{:S(2)}, u32[]{:S(2)}) async-start(bf16[8,128,1024]{2,1,0:T(8,128)(2,1)} %shard_map.94), calls=%async_computation.1 | async-start | bytes 4194304 | tf_op jit(solution)/shard_map/all_to_all | solution.py:378
  24.5 0.0 copy-done
  24.5 0.8 collective-permute-start
  25.3 0.6 constant_dynamic-update-slice_fusion.6
  25.9 17.5 %collective-permute-done = bf16[32,512]{1,0:T(8,128)(2,1)S(1)} collective-permute-done((bf16[32,512]{1,0:T(8,128)(2,1)S(1)}, bf16[32,512]{1,0:T(8,128)(2,1)S(1)}, u32[]{:S(2)}, u32[]{:S(2)}) %collective-permute-start) | collective-permute-done | bytes 32800 | tf_op jit(solution)/shard_map/ppermute | solution.py:383
  43.4 0.6 constant_dynamic-update-slice_fusion.5
  44.1 6.3 %collective-permute-start.1 = (bf16[64,512]{1,0:T(8,128)(2,1)S(1)}, bf16[64,512]{1,0:T(8,128)(2,1)S(1)}, u32[]{:S(2)}, u32[]{:S(2)}) collective-permute-start(bf16[64,512]{1,0:T(8,128)(2,1)S(1)} %get-tuple-element.41), channel_id=1, source_target_pairs={{0,64},{16,80},{32,96},{48,112},{64,0},{80,16},{96,32},{112,48},{1... | collective-permute-start | bytes 196616 | tf_op jit(solution)/shard_map/ppermute | solution.py:383
  50.4 0.6 collective-permute-start.3
  50.9 0.9 collective-permute-start.2
  51.8 1.5 collective-permute-done.1
  53.3 0.6 constant_dynamic-update-slice_fusion.4
  53.9 2.1 %collective-permute-done.2 = bf16[64,512]{1,0:T(8,128)(2,1)S(1)} collective-permute-done((bf16[64,512]{1,0:T(8,128)(2,1)S(1)}, bf16[64,512]{1,0:T(8,128)(2,1)S(1)}, u32[]{:S(2)}, u32[]{:S(2)}) %collective-permute-start.2) | collective-permute-done | bytes 65568 | tf_op jit(solution)/shard_map/ppermute | solution.py:383
  56.1 0.6 constant_dynamic-update-slice_fusion.3
  56.7 0.7 collective-permute-done.3
  57.4 0.6 constant_dynamic-update-slice_fusion.2
  58.1 0.4 collective-permute-start.4
  58.5 0.0 copy-done.12
  58.5 0.2 reduce-window.9
  58.7 0.0 copy-start.10
  58.7 0.0 copy-done.9
  58.7 0.6 constant_dynamic-slice_fusion.1
  59.2 0.0 copy-done.2
  59.2 0.0 copy-done.7
  59.2 0.0 copy-start.3
  59.2 1.2 copy-done.3
  60.4 0.0 copy-start.4
  60.4 1.2 copy-done.4
  61.7 5.3 %shard_map.96 = (bf16[8,64,512]{2,1,0:T(8,128)(2,1)S(1)}, bf16[64,512]{1,0:T(8,128)(2,1)S(1)}) custom-call(s32[8]{0:T(128)S(1)} %bitcast.11, s32[1]{0:T(128)} %bitcast.1.place_ref, s32[4]{0:T(128)S(1)} %bitcast.12, bf16[128,4096]{1,0:T(8,128)(2,1)S(1)} %copy-done.3, bf16[128,4096]{1,0:T(8,128)(2,1)S(1)} %copy-done.4, bf16[128,512]{1,0:T(8,128)(2,1)S(1)} %copy-done.7, ...), custom_call_target="tpu_custom_call" | custom-call | flops 700000000 | bytes 4194304 | tf_op jit(solution)/shard_map/pallas_call | solution.py:159
  67.0 0.0 copy-start.8
  67.0 0.6 copy-done.8
  67.6 0.0 copy-start.5
  67.6 0.0 collective-permute-done.4
  67.6 1.1 constant_dynamic-update-slice_fusion.7.mine_ref
  68.8 0.1 collective-permute-start.5
  68.9 0.0 copy-done.5
  68.9 1.9 %collective-permute-done.5.theirs_ref = bf16[512,512]{1,0:T(8,128)(2,1)S(1)} collective-permute-done((bf16[512,512]{1,0:T(8,128)(2,1)S(1)}, bf16[512,512]{1,0:T(8,128)(2,1)S(1)}, u32[]{:S(2)}, u32[]{:S(2)}) %collective-permute-start.5) | collective-permute-done | bytes 524320 | tf_op jit(solution)/shard_map/ppermute | solution.py:383
  70.8 0.0 all-to-all-done.1
  70.8 1.0 copy-done.6
  71.8 1.3 shard_map.97
  73.1 0.0 copy-done.10
  73.1 37.3 %all_to_all.30.parts_ref = bf16[8,192,512]{2,1,0:T(8,128)(2,1)} all-to-all(bf16[8,192,512]{2,1,0:T(8,128)(2,1)S(1)} %shard_map.97), channel_id=1, replica_groups=mesh['ylo'=2,'z'=8,'core'=2,'yhi'=2,'x'=4] {'yhi','x'}, dimensions={0} | all-to-all | bytes 3145728 | tf_op jit(solution)/shard_map/all_to_all | solution.py:378
  110.4 2.9 %shard_map.98 = (bf16[8,192,512]{2,1,0:T(8,128)(2,1)}, bf16[128,512]{1,0:T(8,128)(2,1)}) custom-call(bf16[8,192,512]{2,1,0:T(8,128)(2,1)} %all_to_all.30.parts_ref, bf16[64,512]{1,0:T(8,128)(2,1)} %copy-done.8), custom_call_target="tpu_custom_call" | custom-call | flops 786432 | bytes 3145728 | tf_op jit(solution)/shard_map/pallas_call | solution.py:298
  113.3 25.7 %all_to_all.31.d_value_ref.v_hbm = bf16[8,192,512]{2,1,0:T(8,128)(2,1)S(1)} all-to-all(bf16[8,192,512]{2,1,0:T(8,128)(2,1)} %get-tuple-element.26), channel_id=1, replica_groups=mesh['ylo'=2,'z'=8,'core'=2,'yhi'=2,'x'=4] {'yhi','x'}, dimensions={0} | all-to-all | bytes 3145728 | tf_op jit(solution)/shard_map/all_to_all | solution.py:378
  139.0 0.7 shard_map.99
  139.8 0.1 collective-permute-start.6
  139.9 1.9 %collective-permute-done.6.refs_0_ = bf16[16,32,512]{2,1,0:T(8,128)(2,1)S(1)} collective-permute-done((bf16[16,32,512]{2,1,0:T(8,128)(2,1)S(1)}, bf16[16,32,512]{2,1,0:T(8,128)(2,1)S(1)}, u32[]{:S(2)}, u32[]{:S(2)}) %collective-permute-start.6) | collective-permute-done | bytes 524320 | tf_op jit(solution)/shard_map/ppermute | solution.py:383
  141.8 0.0 copy-done.1
  141.8 1.5 shard_map.100
  143.3 7.2 %all-to-all-start.4 = ((bf16[16,32,512]{2,1,0:T(8,128)(2,1)}), bf16[16,32,512]{2,1,0:T(8,128)(2,1)S(1)}, u32[]{:S(2)}, u32[]{:S(2)}) async-start(bf16[16,32,512]{2,1,0:T(8,128)(2,1)} %shard_map.100), calls=%async_computation.4 | async-start | bytes 1048576 | tf_op jit(solution)/shard_map/all_to_all | solution.py:378
  150.5 12.3 %shard_map.101 = (f32[128,4096]{1,0:T(8,128)}, bf16[8,96,512]{2,1,0:T(8,128)(2,1)}, f32[64,512]{1,0:T(8,128)}) custom-call(s32[8]{0:T(128)} %bitcast.10, s32[1]{0:T(128)} %bitcast.1.place_ref, s32[4]{0:T(128)} %bitcast.13, bf16[128,4096]{1,0:T(8,128)(2,1)} %q_hbm.3, bf16[128,4096]{1,0:T(8,128)(2,1)} %u_hbm.3, bf16[128,512]{1,0:T(8,128)(2,1)} %ks_ref.3, ...), custom_call_target="tpu_custom_call" | custom-call | flops 1400000000 | bytes 6291456 | tf_op jit(solution)/shard_map/pallas_call | solution.py:175
  162.8 3.3 %all-to-all-done.4.pieces_ref = bf16[16,32,512]{2,1,0:T(8,128)(2,1)S(1)} async-done(((bf16[16,32,512]{2,1,0:T(8,128)(2,1)}), bf16[16,32,512]{2,1,0:T(8,128)(2,1)S(1)}, u32[]{:S(2)}, u32[]{:S(2)}) %all-to-all-start.4) | async-done | bytes 524320 | tf_op jit(solution)/shard_map/all_to_all | solution.py:378
  166.1 0.8 copy-done.11
  166.9 1.8 shard_map.102
  168.7 17.6 %all_to_all.32.parts_ref = bf16[8,96,512]{2,1,0:T(8,128)(2,1)} all-to-all(bf16[8,96,512]{2,1,0:T(8,128)(2,1)} %shard_map.102), channel_id=1, replica_groups=mesh['ylo'=2,'z'=8,'core'=2,'yhi'=2,'x'=4] {'yhi','x'}, dimensions={0} | all-to-all | bytes 1572864 | tf_op jit(solution)/shard_map/all_to_all | solution.py:378
  186.3 2.1 %shard_map.103 = (f32[128,512]{1,0:T(8,128)}, f32[256,512]{1,0:T(8,128)}) custom-call(bf16[8,96,512]{2,1,0:T(8,128)(2,1)} %all_to_all.32.parts_ref, f32[64,512]{1,0:T(8,128)} %get-tuple-element.30.dk_short_ref), custom_call_target="tpu_custom_call" | custom-call | flops 393216 | bytes 1572864 | tf_op jit(solution)/shard_map/pallas_call | solution.py:334
  (4 shorter events, 0.0 us)
Async XLA Ops:
  0.6 23.9 %copy-start = (bf16[256,512]{1,0:T(8,128)(2,1)S(1)}, bf16[256,512]{1,0:T(8,128)(2,1)}, u32[]{:S(2)}) copy-start(bf16[256,512]{1,0:T(8,128)(2,1)} %param.11) | copy-start | bytes 786436
  2.4 18.5 %all-to-all-start = ((bf16[8,64,512]{2,1,0:T(8,128)(2,1)}), bf16[8,64,512]{2,1,0:T(8,128)(2,1)S(1)}, u32[]{:S(2)}, u32[]{:S(2)}) async-start(bf16[8,64,512]{2,1,0:T(8,128)(2,1)} %shard_map.95), calls=%async_computation | async-start | bytes 1048576 | tf_op jit(solution)/shard_map/all_to_all | solution.py:378
  15.9 42.6 %copy-start.12 = (s32[1,4]{1,0:T(1,128)S(1)}, s32[1,4]{1,0:T(1,128)}, u32[]{:S(2)}) copy-start(s32[1,4]{1,0:T(1,128)} %param.12) | copy-start | bytes 52
  15.9 42.7 %copy-start.9 = (s32[1,8]{1,0:T(1,128)S(1)}, s32[1,8]{1,0:T(1,128)}, u32[]{:S(2)}) copy-start(s32[1,8]{1,0:T(1,128)} %param.13) | copy-start | bytes 100
  15.9 43.3 %copy-start.7 = (bf16[128,512]{1,0:T(8,128)(2,1)S(1)}, bf16[128,512]{1,0:T(8,128)(2,1)}, u32[]{:S(2)}) copy-start(bf16[128,512]{1,0:T(8,128)(2,1)} %ks_ref.3) | copy-start | bytes 393220
  20.9 38.3 %copy-start.2 = (bf16[8,64,512]{2,1,0:T(8,128)(2,1)}, bf16[8,64,512]{2,1,0:T(8,128)(2,1)S(1)}, u32[]{:S(2)}) copy-start(bf16[8,64,512]{2,1,0:T(8,128)(2,1)S(1)} %all-to-all-done.k_ref) | copy-start | bytes 1572868
  20.9 49.9 %all-to-all-start.1 = ((bf16[8,128,1024]{2,1,0:T(8,128)(2,1)}), bf16[8,128,1024]{2,1,0:T(8,128)(2,1)S(1)}, u32[]{:S(2)}, u32[]{:S(2)}) async-start(bf16[8,128,1024]{2,1,0:T(8,128)(2,1)} %shard_map.94), calls=%async_computation.1 | async-start | bytes 4194304 | tf_op jit(solution)/shard_map/all_to_all | solution.py:378
  24.5 18.9 %collective-permute-start = (bf16[32,512]{1,0:T(8,128)(2,1)S(1)}, bf16[32,512]{1,0:T(8,128)(2,1)S(1)}, u32[]{:S(2)}, u32[]{:S(2)}) collective-permute-start(bf16[32,512]{1,0:T(8,128)(2,1)S(1)} %constant_dynamic-slice_fusion), channel_id=1, source_target_pairs={{0,128},{128,0},{1,129},{129,1},{2,130},{130,2},{3,131},{131,3},{4... | collective-permute-start | bytes 98312 | tf_op jit(solution)/shard_map/ppermute | solution.py:383
  44.1 9.2 %collective-permute-start.1 = (bf16[64,512]{1,0:T(8,128)(2,1)S(1)}, bf16[64,512]{1,0:T(8,128)(2,1)S(1)}, u32[]{:S(2)}, u32[]{:S(2)}) collective-permute-start(bf16[64,512]{1,0:T(8,128)(2,1)S(1)} %get-tuple-element.41), channel_id=1, source_target_pairs={{0,64},{16,80},{32,96},{48,112},{64,0},{80,16},{96,32},{112,48},{1... | collective-permute-start | bytes 196616 | tf_op jit(solution)/shard_map/ppermute | solution.py:383
  50.4 7.1 %collective-permute-start.3 = (bf16[64,512]{1,0:T(8,128)(2,1)S(1)}, bf16[64,512]{1,0:T(8,128)(2,1)S(1)}, u32[]{:S(2)}, u32[]{:S(2)}) collective-permute-start(bf16[64,512]{1,0:T(8,128)(2,1)S(1)} %get-tuple-element.41), channel_id=1, source_target_pairs={{0,96},{16,112},{32,64},{48,80},{64,32},{80,48},{96,0},{112,16},{1... | collective-permute-start | bytes 196616 | tf_op jit(solution)/shard_map/ppermute | solution.py:383
  50.9 5.2 %collective-permute-start.2 = (bf16[64,512]{1,0:T(8,128)(2,1)S(1)}, bf16[64,512]{1,0:T(8,128)(2,1)S(1)}, u32[]{:S(2)}, u32[]{:S(2)}) collective-permute-start(bf16[64,512]{1,0:T(8,128)(2,1)S(1)} %get-tuple-element.41), channel_id=1, source_target_pairs={{0,32},{16,48},{32,0},{48,16},{64,96},{80,112},{96,64},{112,80},{1... | collective-permute-start | bytes 196616 | tf_op jit(solution)/shard_map/ppermute | solution.py:383
  58.1 9.6 %collective-permute-start.4 = (bf16[256,512]{1,0:T(8,128)(2,1)}, bf16[256,512]{1,0:T(8,128)(2,1)}, u32[]{:S(2)}, u32[]{:S(2)}) collective-permute-start(bf16[256,512]{1,0:T(8,128)(2,1)} %get-tuple-element.33), channel_id=1, source_target_pairs={{0,16},{16,0},{32,48},{48,32},{64,80},{80,64},{96,112},{112,96},{1... | collective-permute-start | bytes 786440 | tf_op jit(solution)/shard_map/ppermute | solution.py:383
  58.7 14.4 %copy-start.10 = (s32[4,1]{0,1:T(1,128)}, s32[4,1]{0,1:T(1,128)S(1)}, u32[]{:S(2)}) copy-start(s32[4,1]{0,1:T(1,128)S(1)} %reduce-window.9) | copy-start | bytes 52
  59.2 1.2 copy-start.3
  60.4 1.2 copy-start.4
  67.0 0.6 copy-start.8
  67.6 1.2 copy-start.5
  68.8 2.0 %collective-permute-start.5 = (bf16[512,512]{1,0:T(8,128)(2,1)S(1)}, bf16[512,512]{1,0:T(8,128)(2,1)S(1)}, u32[]{:S(2)}, u32[]{:S(2)}) collective-permute-start(bf16[512,512]{1,0:T(8,128)(2,1)S(1)} %constant_dynamic-update-slice_fusion.7.mine_ref), channel_id=1, source_target_pairs={{0,8},{8,0},{1,9},{9,1},{2,10},{10,2},{3,11},{11,3},{4,12},{12,4},... | collective-permute-start | bytes 1572872 | tf_op jit(solution)/shard_map/ppermute | solution.py:383
  70.8 1.0 copy-start.6
  139.0 2.7 %copy-start.1 = (bf16[8,192,512]{2,1,0:T(8,128)(2,1)}, bf16[8,192,512]{2,1,0:T(8,128)(2,1)S(1)}, u32[]{:S(2)}) copy-start(bf16[8,192,512]{2,1,0:T(8,128)(2,1)S(1)} %all_to_all.31.d_value_ref.v_hbm) | copy-start | bytes 4718596
  139.8 2.0 %collective-permute-start.6 = (bf16[16,32,512]{2,1,0:T(8,128)(2,1)S(1)}, bf16[16,32,512]{2,1,0:T(8,128)(2,1)S(1)}, u32[]{:S(2)}, u32[]{:S(2)}) collective-permute-start(bf16[16,32,512]{2,1,0:T(8,128)(2,1)S(1)} %shard_map.99), channel_id=1, source_target_pairs={{0,8},{8,0},{1,9},{9,1},{2,10},{10,2},{3,11},{11,3},{4,12},{12,4},... | collective-permute-start | bytes 1572872 | tf_op jit(solution)/shard_map/ppermute | solution.py:383
  143.3 22.8 %all-to-all-start.4 = ((bf16[16,32,512]{2,1,0:T(8,128)(2,1)}), bf16[16,32,512]{2,1,0:T(8,128)(2,1)S(1)}, u32[]{:S(2)}, u32[]{:S(2)}) async-start(bf16[16,32,512]{2,1,0:T(8,128)(2,1)} %shard_map.100), calls=%async_computation.4 | async-start | bytes 1048576 | tf_op jit(solution)/shard_map/all_to_all | solution.py:378
  166.1 0.8 copy-start.11

commit v5 on v4

--- a/solution.py
+++ b/solution.py
@@ -395,15 +395,15 @@
     scalars = (order, lax.dynamic_slice(order, (member,), (1,)), jnp.cumsum(doc_lengths[0]))
 
     all_keys = exchange(key_copies(rotated_key_rows), CTX)
-    grouped = regroup(plane * CORES + lax.axis_index("core"), tokens)
+    weight = lax.dynamic_slice_in_dim(value_projection_weight, member * PIECE, PIECE, 0)
+    weight = jnp.concatenate([weight, swap_along(weight, "ylo", 1)], axis=0)
+    grouped = regroup(after(plane * CORES + lax.axis_index("core"), weight), tokens)
     grouped, all_keys = lax.optimization_barrier((grouped, all_keys))
     tok = exchange(grouped, CTX).reshape(N_CTX * TOK, -1)
 
-    weight = lax.dynamic_slice_in_dim(value_projection_weight, member * PIECE, PIECE, 0)
     weight = after(weight, grouped)
     depth = lax.axis_size("z")
     far = [turned(slot, depth) for slot in range(depth // 2)]
-    weight = jnp.concatenate([weight, swap_along(weight, "ylo", 1)], axis=0)
     weight = jnp.concatenate([weight] + [swap_along(weight, "z", step) for step in far[1:]], axis=0)
     dv_all, dv_short = dvalues(scalars, queries, upstream, rotated_key_rows, after(all_keys, weight))
     if depth > 1:

time: 190 us -> 172 us (0.905)
  waiting for transfers between devices: 33.9 us -> 16.9 us
  blocking collectives: 80.6 us -> 73.7 us
  starting transfers between devices: 26.8 us -> 32 us
    ppermute x7, waiting for transfers between devices: 25.6 us -> 13.2 us  [swap_along(): return lax.ppermute(array, axis, [(i, i ^ step) for i in range(count)])]
    all_to_all x3, blocking collectives: 80.6 us -> 73.7 us  [exchange(): return lax.all_to_all(pieces, axes, 0, 0, tiled=True)]
    all_to_all x3, waiting for transfers between devices: 8.28 us -> 3.71 us  [exchange(): return lax.all_to_all(pieces, axes, 0, 0, tiled=True)]
    all_to_all x3, starting transfers between devices: 17.7 us -> 21.9 us  [exchange(): return lax.all_to_all(pieces, axes, 0, 0, tiled=True)]
    unnamed x30 -> x29, local copies, waits for them, and re-layouts: 7.47 us -> 7.72 us
  transfers between devices with their start and end apart: 10 -> 10, of which waited for: 8 -> 5; matrix products, arithmetic and copies ran while one was open for 3% -> 3% of each run, Pallas kernels for 13% -> 14%
where the time goes in v5:
time: 172 us; the launch traced here: 170 us
  blocking collectives  73.7 us (43%)
  Pallas kernels  36.2 us (21%)
  starting transfers between devices  32 us (19%)
  waiting for transfers between devices  16.9 us (10%)
  local copies, waits for them, and re-layouts  10.1 us (6%)
    all_to_all x3, blocking collectives, exchange(): return lax.all_to_all(pieces, axes, 0, 0, tiled=True)  73.7 us
    all_to_all x3, starting transfers between devices, exchange(): return lax.all_to_all(pieces, axes, 0, 0, tiled=True)  21.9 us
    ppermute x7, waiting for transfers between devices, swap_along(): return lax.ppermute(array, axis, [(i, i ^ step) for i in range(count)])  13.2 us
    pallas_call x1, Pallas kernels, dscores(): pl.pallas_call(dscore_kernel, grid_spec=pltpu.PrefetchScalarGridSpec(num_...  12.2 us
    ppermute x7, starting transfers between devices, swap_along(): return lax.ppermute(array, axis, [(i, i ^ step) for i in range(count)])  10.1 us
    unnamed x29, local copies, waits for them, and re-layouts  7.72 us
    pallas_call x1, Pallas kernels, regroup(): pl.pallas_call(regroup_kernel, grid_spec=pltpu.PrefetchScalarGridSpec(num...  6.55 us
    pallas_call x1, Pallas kernels, dvalues(): pl.pallas_call(dvalue_kernel, grid_spec=pltpu.PrefetchScalarGridSpec(num_...  5.34 us
  transfers between devices with their start and end apart: 10, of which 5 were waited for; matrix products, arithmetic and copies ran while one was open for 3% of the time, Pallas kernels for 14%

profile of v5, /device:TPU:32, one launch (start us, length us, event | category | flops | bytes accessed | tf_op | source)
XLA Modules:
  0.0 170.4 jit_solution(7946657365446502125)
XLA Ops:
  0.6 0.0 copy-start
  0.6 1.7 %shard_map.95 = bf16[8,64,512]{2,1,0:T(8,128)(2,1)} custom-call(bf16[128,512]{1,0:T(8,128)(2,1)} %ks_ref.3), custom_call_target="tpu_custom_call" | custom-call | bytes 524288 | tf_op jit(solution)/shard_map/pallas_call | solution.py:259
  2.4 6.9 %all-to-all-start = ((bf16[8,64,512]{2,1,0:T(8,128)(2,1)}), bf16[8,64,512]{2,1,0:T(8,128)(2,1)S(1)}, u32[]{:S(2)}, u32[]{:S(2)}) async-start(bf16[8,64,512]{2,1,0:T(8,128)(2,1)} %shard_map.95), calls=%async_computation | async-start | bytes 1048576 | tf_op jit(solution)/shard_map/all_to_all | solution.py:378
  9.3 0.0 copy-done
  9.3 0.8 collective-permute-start
  10.1 3.6 %collective-permute-done = bf16[32,512]{1,0:T(8,128)(2,1)S(1)} collective-permute-done((bf16[32,512]{1,0:T(8,128)(2,1)S(1)}, bf16[32,512]{1,0:T(8,128)(2,1)S(1)}, u32[]{:S(2)}, u32[]{:S(2)}) %collective-permute-start) | collective-permute-done | bytes 32800 | tf_op jit(solution)/shard_map/ppermute | solution.py:383
  13.7 0.6 pad_maximum_fusion
  14.3 6.5 %shard_map.94 = bf16[8,128,1024]{2,1,0:T(8,128)(2,1)} custom-call(s32[1]{0:T(128)} %bitcast.4.me_ref, bf16[128,8192]{1,0:T(8,128)(2,1)} %refs_3_.1, bf16[128,8192]{1,0:T(8,128)(2,1)} %refs_3_.1, bf16[128,8192]{1,0:T(8,128)(2,1)} %refs_3_.1, bf16[128,8192]{1,0:T(8,128)(2,1)} %refs_3_.1), custom_call_target="tpu_custom_call" | custom-call | bytes 4194304 | tf_op jit(solution)/shard_map/pallas_call | solution.py:230
  20.8 0.0 copy-start.12
  20.8 0.0 copy-start.9
  20.8 0.0 copy-start.7
  20.8 0.0 all-to-all-done.k_ref
  20.9 0.0 copy-start.2
  20.9 10.9 %all-to-all-start.1 = ((bf16[8,128,1024]{2,1,0:T(8,128)(2,1)}), bf16[8,128,1024]{2,1,0:T(8,128)(2,1)S(1)}, u32[]{:S(2)}, u32[]{:S(2)}) async-start(bf16[8,128,1024]{2,1,0:T(8,128)(2,1)} %shard_map.94), calls=%async_computation.1 | async-start | bytes 4194304 | tf_op jit(solution)/shard_map/all_to_all | solution.py:378
  31.8 5.4 %collective-permute-start.3 = (bf16[64,512]{1,0:T(8,128)(2,1)}, bf16[64,512]{1,0:T(8,128)(2,1)S(1)}, u32[]{:S(2)}, u32[]{:S(2)}) collective-permute-start(bf16[64,512]{1,0:T(8,128)(2,1)} %pad_maximum_fusion), channel_id=1, source_target_pairs={{0,96},{16,112},{32,64},{48,80},{64,32},{80,48},{96,0},{112,16},{1... | collective-permute-start | bytes 196616 | tf_op jit(solution)/shard_map/ppermute | solution.py:383
  37.2 1.5 collective-permute-start.2
  38.6 1.0 collective-permute-start.1
  39.6 1.5 constant_dynamic-update-slice_fusion.3
  41.1 5.9 %collective-permute-done.1 = bf16[64,512]{1,0:T(8,128)(2,1)S(1)} collective-permute-done((bf16[64,512]{1,0:T(8,128)(2,1)}, bf16[64,512]{1,0:T(8,128)(2,1)S(1)}, u32[]{:S(2)}, u32[]{:S(2)}) %collective-permute-start.1) | collective-permute-done | bytes 65568 | tf_op jit(solution)/shard_map/ppermute | solution.py:383
  47.0 0.6 constant_dynamic-update-slice_fusion.2
  47.7 0.0 collective-permute-done.2
  47.7 0.6 constant_dynamic-update-slice_fusion.1
  48.3 0.0 collective-permute-done.3
  48.3 0.6 constant_dynamic-update-slice_fusion
  48.9 1.2 collective-permute-start.4
  50.2 0.0 copy-done.12
  50.2 0.2 reduce-window.9
  50.4 0.0 copy-start.10
  50.4 0.0 copy-done.9
  50.4 0.6 constant_dynamic-slice_fusion.1
  50.9 0.0 copy-done.2
  50.9 0.0 copy-done.7
  50.9 0.0 copy-start.3
  51.0 1.2 copy-done.3
  52.2 0.0 copy-start.4
  52.2 1.2 copy-done.4
  53.4 5.3 %shard_map.96 = (bf16[8,64,512]{2,1,0:T(8,128)(2,1)S(1)}, bf16[64,512]{1,0:T(8,128)(2,1)S(1)}) custom-call(s32[8]{0:T(128)S(1)} %bitcast.11, s32[1]{0:T(128)} %bitcast.1.place_ref, s32[4]{0:T(128)S(1)} %bitcast.12, bf16[128,4096]{1,0:T(8,128)(2,1)S(1)} %copy-done.3, bf16[128,4096]{1,0:T(8,128)(2,1)S(1)} %copy-done.4, bf16[128,512]{1,0:T(8,128)(2,1)S(1)} %copy-done.7, ...), custom_call_target="tpu_custom_call" | custom-call | flops 700000000 | bytes 4194304 | tf_op jit(solution)/shard_map/pallas_call | solution.py:159
  58.7 0.0 copy-start.8
  58.8 0.6 copy-done.8
  59.4 0.0 collective-permute-done.4
  59.4 1.1 constant_dynamic-update-slice_fusion.4.mine_ref
  60.5 0.1 collective-permute-start.5
  60.6 0.0 copy-done.5
  60.6 1.9 %collective-permute-done.5.theirs_ref = bf16[512,512]{1,0:T(8,128)(2,1)S(1)} collective-permute-done((bf16[512,512]{1,0:T(8,128)(2,1)S(1)}, bf16[512,512]{1,0:T(8,128)(2,1)S(1)}, u32[]{:S(2)}, u32[]{:S(2)}) %collective-permute-start.5) | collective-permute-done | bytes 524320 | tf_op jit(solution)/shard_map/ppermute | solution.py:383
  62.5 0.0 all-to-all-done.1
  62.5 0.0 copy-start.6
  62.5 1.0 copy-done.6
  63.6 1.2 shard_map.97
  64.8 0.0 copy-done.10
  64.8 30.3 %all_to_all.30.parts_ref = bf16[8,192,512]{2,1,0:T(8,128)(2,1)} all-to-all(bf16[8,192,512]{2,1,0:T(8,128)(2,1)S(1)} %shard_map.97), channel_id=1, replica_groups=mesh['ylo'=2,'z'=8,'core'=2,'yhi'=2,'x'=4] {'yhi','x'}, dimensions={0} | all-to-all | bytes 3145728 | tf_op jit(solution)/shard_map/all_to_all | solution.py:378
  95.1 2.9 %shard_map.98 = (bf16[8,192,512]{2,1,0:T(8,128)(2,1)}, bf16[128,512]{1,0:T(8,128)(2,1)}) custom-call(bf16[8,192,512]{2,1,0:T(8,128)(2,1)} %all_to_all.30.parts_ref, bf16[64,512]{1,0:T(8,128)(2,1)} %copy-done.8), custom_call_target="tpu_custom_call" | custom-call | flops 786432 | bytes 3145728 | tf_op jit(solution)/shard_map/pallas_call | solution.py:298
  98.0 25.7 %all_to_all.31.d_value_ref.v_hbm = bf16[8,192,512]{2,1,0:T(8,128)(2,1)S(1)} all-to-all(bf16[8,192,512]{2,1,0:T(8,128)(2,1)} %get-tuple-element.28), channel_id=1, replica_groups=mesh['ylo'=2,'z'=8,'core'=2,'yhi'=2,'x'=4] {'yhi','x'}, dimensions={0} | all-to-all | bytes 3145728 | tf_op jit(solution)/shard_map/all_to_all | solution.py:378
  123.7 0.7 shard_map.99
  124.5 0.1 collective-permute-start.6
  124.6 1.9 %collective-permute-done.6.refs_0_ = bf16[16,32,512]{2,1,0:T(8,128)(2,1)S(1)} collective-permute-done((bf16[16,32,512]{2,1,0:T(8,128)(2,1)S(1)}, bf16[16,32,512]{2,1,0:T(8,128)(2,1)S(1)}, u32[]{:S(2)}, u32[]{:S(2)}) %collective-permute-start.6) | collective-permute-done | bytes 524320 | tf_op jit(solution)/shard_map/ppermute | solution.py:383
  126.5 0.0 copy-done.1
  126.5 1.5 shard_map.100
  128.0 4.1 %all-to-all-start.4 = ((bf16[16,32,512]{2,1,0:T(8,128)(2,1)}), bf16[16,32,512]{2,1,0:T(8,128)(2,1)S(1)}, u32[]{:S(2)}, u32[]{:S(2)}) async-start(bf16[16,32,512]{2,1,0:T(8,128)(2,1)} %shard_map.100), calls=%async_computation.4 | async-start | bytes 1048576 | tf_op jit(solution)/shard_map/all_to_all | solution.py:378
  132.1 12.2 %shard_map.101 = (f32[128,4096]{1,0:T(8,128)}, bf16[8,96,512]{2,1,0:T(8,128)(2,1)}, f32[64,512]{1,0:T(8,128)}) custom-call(s32[8]{0:T(128)} %bitcast.10, s32[1]{0:T(128)} %bitcast.1.place_ref, s32[4]{0:T(128)} %bitcast.13, bf16[128,4096]{1,0:T(8,128)(2,1)} %q_hbm.3, bf16[128,4096]{1,0:T(8,128)(2,1)} %u_hbm.3, bf16[128,512]{1,0:T(8,128)(2,1)} %ks_ref.3, ...), custom_call_target="tpu_custom_call" | custom-call | flops 1400000000 | bytes 6291456 | tf_op jit(solution)/shard_map/pallas_call | solution.py:175
  144.4 3.7 %all-to-all-done.4.pieces_ref = bf16[16,32,512]{2,1,0:T(8,128)(2,1)S(1)} async-done(((bf16[16,32,512]{2,1,0:T(8,128)(2,1)}), bf16[16,32,512]{2,1,0:T(8,128)(2,1)S(1)}, u32[]{:S(2)}, u32[]{:S(2)}) %all-to-all-start.4) | async-done | bytes 524320 | tf_op jit(solution)/shard_map/all_to_all | solution.py:378
  148.0 0.8 copy-done.11
  148.8 1.8 %shard_map.102 = bf16[8,96,512]{2,1,0:T(8,128)(2,1)} custom-call(bf16[16,32,512]{2,1,0:T(8,128)(2,1)} %copy-done.11, bf16[8,96,512]{2,1,0:T(8,128)(2,1)} %get-tuple-element.31._), custom_call_target="tpu_custom_call", output_to_operand_aliasing={{}: (1, {})} | custom-call | flops 262144 | bytes 524288 | tf_op jit(solution)/shard_map/pallas_call | solution.py:315
  150.6 17.7 %all_to_all.32.parts_ref = bf16[8,96,512]{2,1,0:T(8,128)(2,1)} all-to-all(bf16[8,96,512]{2,1,0:T(8,128)(2,1)} %shard_map.102), channel_id=1, replica_groups=mesh['ylo'=2,'z'=8,'core'=2,'yhi'=2,'x'=4] {'yhi','x'}, dimensions={0} | all-to-all | bytes 1572864 | tf_op jit(solution)/shard_map/all_to_all | solution.py:378
  168.3 2.1 %shard_map.103 = (f32[128,512]{1,0:T(8,128)}, f32[256,512]{1,0:T(8,128)}) custom-call(bf16[8,96,512]{2,1,0:T(8,128)(2,1)} %all_to_all.32.parts_ref, f32[64,512]{1,0:T(8,128)} %get-tuple-element.32.dk_short_ref), custom_call_target="tpu_custom_call" | custom-call | flops 393216 | bytes 1572864 | tf_op jit(solution)/shard_map/pallas_call | solution.py:334
  (4 shorter events, 0.0 us)
Async XLA Ops:
  0.6 8.7 %copy-start = (bf16[256,512]{1,0:T(8,128)(2,1)S(1)}, bf16[256,512]{1,0:T(8,128)(2,1)}, u32[]{:S(2)}) copy-start(bf16[256,512]{1,0:T(8,128)(2,1)} %param.11) | copy-start | bytes 786436
  2.4 18.5 %all-to-all-start = ((bf16[8,64,512]{2,1,0:T(8,128)(2,1)}), bf16[8,64,512]{2,1,0:T(8,128)(2,1)S(1)}, u32[]{:S(2)}, u32[]{:S(2)}) async-start(bf16[8,64,512]{2,1,0:T(8,128)(2,1)} %shard_map.95), calls=%async_computation | async-start | bytes 1048576 | tf_op jit(solution)/shard_map/all_to_all | solution.py:378
  9.3 4.3 %collective-permute-start = (bf16[32,512]{1,0:T(8,128)(2,1)S(1)}, bf16[32,512]{1,0:T(8,128)(2,1)S(1)}, u32[]{:S(2)}, u32[]{:S(2)}) collective-permute-start(bf16[32,512]{1,0:T(8,128)(2,1)S(1)} %constant_dynamic-slice_fusion), channel_id=1, source_target_pairs={{0,128},{128,0},{1,129},{129,1},{2,130},{130,2},{3,131},{131,3},{4... | collective-permute-start | bytes 98312 | tf_op jit(solution)/shard_map/ppermute | solution.py:383
  20.8 29.4 %copy-start.12 = (s32[1,4]{1,0:T(1,128)S(1)}, s32[1,4]{1,0:T(1,128)}, u32[]{:S(2)}) copy-start(s32[1,4]{1,0:T(1,128)} %param.12) | copy-start | bytes 52
  20.8 29.5 %copy-start.9 = (s32[1,8]{1,0:T(1,128)S(1)}, s32[1,8]{1,0:T(1,128)}, u32[]{:S(2)}) copy-start(s32[1,8]{1,0:T(1,128)} %param.13) | copy-start | bytes 100
  20.8 30.1 %copy-start.7 = (bf16[128,512]{1,0:T(8,128)(2,1)S(1)}, bf16[128,512]{1,0:T(8,128)(2,1)}, u32[]{:S(2)}) copy-start(bf16[128,512]{1,0:T(8,128)(2,1)} %ks_ref.3) | copy-start | bytes 393220
  20.9 30.1 %copy-start.2 = (bf16[8,64,512]{2,1,0:T(8,128)(2,1)}, bf16[8,64,512]{2,1,0:T(8,128)(2,1)S(1)}, u32[]{:S(2)}) copy-start(bf16[8,64,512]{2,1,0:T(8,128)(2,1)S(1)} %all-to-all-done.k_ref) | copy-start | bytes 1572868
  20.9 41.6 %all-to-all-start.1 = ((bf16[8,128,1024]{2,1,0:T(8,128)(2,1)}), bf16[8,128,1024]{2,1,0:T(8,128)(2,1)S(1)}, u32[]{:S(2)}, u32[]{:S(2)}) async-start(bf16[8,128,1024]{2,1,0:T(8,128)(2,1)} %shard_map.94), calls=%async_computation.1 | async-start | bytes 4194304 | tf_op jit(solution)/shard_map/all_to_all | solution.py:378
  31.8 16.5 %collective-permute-start.3 = (bf16[64,512]{1,0:T(8,128)(2,1)}, bf16[64,512]{1,0:T(8,128)(2,1)S(1)}, u32[]{:S(2)}, u32[]{:S(2)}) collective-permute-start(bf16[64,512]{1,0:T(8,128)(2,1)} %pad_maximum_fusion), channel_id=1, source_target_pairs={{0,96},{16,112},{32,64},{48,80},{64,32},{80,48},{96,0},{112,16},{1... | collective-permute-start | bytes 196616 | tf_op jit(solution)/shard_map/ppermute | solution.py:383
  37.2 10.5 %collective-permute-start.2 = (bf16[64,512]{1,0:T(8,128)(2,1)}, bf16[64,512]{1,0:T(8,128)(2,1)S(1)}, u32[]{:S(2)}, u32[]{:S(2)}) collective-permute-start(bf16[64,512]{1,0:T(8,128)(2,1)} %pad_maximum_fusion), channel_id=1, source_target_pairs={{0,32},{16,48},{32,0},{48,16},{64,96},{80,112},{96,64},{112,80},{1... | collective-permute-start | bytes 196616 | tf_op jit(solution)/shard_map/ppermute | solution.py:383
  38.6 8.4 %collective-permute-start.1 = (bf16[64,512]{1,0:T(8,128)(2,1)}, bf16[64,512]{1,0:T(8,128)(2,1)S(1)}, u32[]{:S(2)}, u32[]{:S(2)}) collective-permute-start(bf16[64,512]{1,0:T(8,128)(2,1)} %pad_maximum_fusion), channel_id=1, source_target_pairs={{0,64},{16,80},{32,96},{48,112},{64,0},{80,16},{96,32},{112,48},{1... | collective-permute-start | bytes 196616 | tf_op jit(solution)/shard_map/ppermute | solution.py:383
  48.9 10.4 %collective-permute-start.4 = (bf16[256,512]{1,0:T(8,128)(2,1)}, bf16[256,512]{1,0:T(8,128)(2,1)}, u32[]{:S(2)}, u32[]{:S(2)}) collective-permute-start(bf16[256,512]{1,0:T(8,128)(2,1)} %get-tuple-element.35), channel_id=1, source_target_pairs={{0,16},{16,0},{32,48},{48,32},{64,80},{80,64},{96,112},{112,96},{1... | collective-permute-start | bytes 786440 | tf_op jit(solution)/shard_map/ppermute | solution.py:383
  50.4 14.4 %copy-start.10 = (s32[4,1]{0,1:T(1,128)}, s32[4,1]{0,1:T(1,128)S(1)}, u32[]{:S(2)}) copy-start(s32[4,1]{0,1:T(1,128)S(1)} %reduce-window.9) | copy-start | bytes 52
  50.9 1.2 copy-start.3
  52.2 1.2 copy-start.4
  58.7 0.6 copy-start.8
  59.4 1.2 copy-start.5
  60.5 2.0 %collective-permute-start.5 = (bf16[512,512]{1,0:T(8,128)(2,1)S(1)}, bf16[512,512]{1,0:T(8,128)(2,1)S(1)}, u32[]{:S(2)}, u32[]{:S(2)}) collective-permute-start(bf16[512,512]{1,0:T(8,128)(2,1)S(1)} %constant_dynamic-update-slice_fusion.4.mine_ref), channel_id=1, source_target_pairs={{0,8},{8,0},{1,9},{9,1},{2,10},{10,2},{3,11},{11,3},{4,12},{12,4},... | collective-permute-start | bytes 1572872 | tf_op jit(solution)/shard_map/ppermute | solution.py:383
  62.5 1.0 copy-start.6
  123.7 2.7 %copy-start.1 = (bf16[8,192,512]{2,1,0:T(8,128)(2,1)}, bf16[8,192,512]{2,1,0:T(8,128)(2,1)S(1)}, u32[]{:S(2)}) copy-start(bf16[8,192,512]{2,1,0:T(8,128)(2,1)S(1)} %all_to_all.31.d_value_ref.v_hbm) | copy-start | bytes 4718596
  124.5 2.0 %collective-permute-start.6 = (bf16[16,32,512]{2,1,0:T(8,128)(2,1)S(1)}, bf16[16,32,512]{2,1,0:T(8,128)(2,1)S(1)}, u32[]{:S(2)}, u32[]{:S(2)}) collective-permute-start(bf16[16,32,512]{2,1,0:T(8,128)(2,1)S(1)} %shard_map.99), channel_id=1, source_target_pairs={{0,8},{8,0},{1,9},{9,1},{2,10},{10,2},{3,11},{11,3},{4,12},{12,4},... | collective-permute-start | bytes 1572872 | tf_op jit(solution)/shard_map/ppermute | solution.py:383
  128.0 20.0 %all-to-all-start.4 = ((bf16[16,32,512]{2,1,0:T(8,128)(2,1)}), bf16[16,32,512]{2,1,0:T(8,128)(2,1)S(1)}, u32[]{:S(2)}, u32[]{:S(2)}) async-start(bf16[16,32,512]{2,1,0:T(8,128)(2,1)} %shard_map.100), calls=%async_computation.4 | async-start | bytes 1048576 | tf_op jit(solution)/shard_map/all_to_all | solution.py:378
  148.0 0.8 copy-start.11
